TPU v7x, 256 devices: a whole 4x4x8 slice. The times are simulated.
256 devices in a mesh: role: 2 (over y_lo), grp: 32 (over z, x), tp: 4 (over y_hi, core).
Axes of the slice: x: 4, y: 4 (y_hi: 2, y_lo: 2; y = y_hi * 2 + y_lo), z: 8, core: 2. Of those that a mesh axis runs over, the one named last changes fastest.
Arguments:
- hidden_in: bfloat16 [8192, 4096], P(('role', 'grp')), may hold values from -20 to 20
- moe_gain: bfloat16 [4096], replicated, may hold values from 0.25 to 1.75
- router: bfloat16 [4096, 16], replicated, may hold values from -0.09375 to 0.09375
- routes: int32 [8192, 2], P(('role', 'grp')), may hold values from 0 to 15, all different within a row; in each aligned block of 128 rows (0 to 127, 128 to 255, ...) at most 24 rows name the same one
- gate_weight: bfloat16 [32, 4096, 768], P('grp', None, 'tp'), may hold values from -0.09375 to 0.09375
- up_weight: bfloat16 [32, 4096, 768], P('grp', None, 'tp'), may hold values from -0.09375 to 0.09375
- down_weight: bfloat16 [32, 768, 4096], P('grp', 'tp'), may hold values from -0.15625 to 0.15625
- attn_gain: bfloat16 [4096], replicated, may hold values from 0.25 to 1.75
- kv_weight: bfloat16 [4096, 2, 512], P(None, None, 'tp'), may hold values from -0.09375 to 0.09375
- queries: bfloat16 [8192, 8192], P(('role', 'grp'), 'tp'), may hold values from -8 to 8
- decode_cache: bfloat16 [1024, 4, 2, 128, 128], P(('role', 'grp'), 'tp'), may hold values from -8 to 8
- prompt_cache: bfloat16 [2048, 4, 2, 128, 128], P(('role', 'grp'), 'tp'), may hold values from -8 to 8
- handoff: int32 [64, 32], P(('role', 'grp')), may hold values from 0 to 31, each once within a row
- block_table: int32 [2048, 4], P(('role', 'grp')), may hold values from 0 to 47, as said below
- lengths: int32 [2048], P(('role', 'grp')), may hold values from 1 to 512
Outputs:
- residual_out: float32 [8192, 4096], P(('role', 'grp'), 'tp')
- new_kv: bfloat16 [8192, 2, 512], P(('role', 'grp'), None, 'tp')
- attn_out: bfloat16 [8192, 8192], P(('role', 'grp'), 'tp')
Inputs may be any that keep to these rules, and one draw needn't show every extreme that they name: `routes`: a token's 2 experts differ; in the 128 tokens of one group at most 24 choose the same expert. `handoff`: each row names every prompt block of its prefill group once. `block_table`: the 4 entries of a row differ.
All inputs are finite; a program needn't handle non-finite values.
Results may differ from a plain program's by a relative error of at most 0.014.
Values may be sent and summed in bfloat16 or wider, within the bound.
No kernel may reach another device: no remote copies, remote signals or barrier semaphores. Data moves between devices by JAX's collectives and lax.ppermute only.
A program may use at most 128 MiB of HBM per device.

v0:
```python
import functools

import jax
import jax.numpy as jnp
from jax import lax
from jax.experimental import pallas as pl
from jax.experimental.pallas import tpu as pltpu
from jax.sharding import PartitionSpec as P

epsilon = 1e-06
LANES = 128


def swapped(x, axis, bit):
    return lax.ppermute(x, axis, [(i, i ^ 1 << bit) for i in range(lax.axis_size(axis))])


def turned(x, step):
    roles, parts = lax.axis_size("role"), lax.axis_size("tp")
    chips = roles * parts // 2
    pairs = []
    for role in range(roles):
        for part in range(parts):
            place = ((part // 2) * roles + role + step) % chips
            pairs.append((role * parts + part, (place % roles) * parts + place // roles * 2 + part % 2))
    return lax.ppermute(x, ("role", "tp"), pairs)


def across(x):
    half = x.shape[0] // 2
    up, down = turned(x[:half], 1), turned(x[half:], -1)
    return turned(up, 1), turned(down, -1)


def inverse_rms(square_sum, width):
    return lax.rsqrt(square_sum / width + epsilon)


def prepare(part_ref, routes_ref, hidden_ref, gain_ref, ordered_ref, packed_ref, slots_ref, *, capacity):
    token_rows, model_width = hidden_ref.shape
    peers, _, eighth = packed_ref.shape
    experts = peers // 2
    quarter = 2 * eighth
    f32, bf16 = jnp.float32, jnp.bfloat16
    hidden = hidden_ref[...].astype(f32)
    squares = jnp.sum(hidden * hidden, axis=1, keepdims=True)
    columns = pl.ds(pl.multiple_of(part_ref[0] * quarter, quarter), quarter)
    own = hidden_ref[:, columns].astype(f32) * inverse_rms(squares, model_width) * gain_ref[:, columns].astype(f32)
    one_routes, two_routes = routes_ref[0:1, :], routes_ref[1:2, :]
    expert = lax.broadcasted_iota(jnp.int32, (max(experts, 8), token_rows), 0)
    one_hot, two_hot = (expert == one_routes).astype(f32), (expert == two_routes).astype(f32)
    before = lax.broadcasted_iota(jnp.int32, (token_rows, token_rows), 0) < lax.broadcasted_iota(
        jnp.int32, (token_rows, token_rows), 1
    )
    taken = jnp.dot((one_hot + two_hot).astype(bf16), before.astype(f32).astype(bf16), preferred_element_type=f32)
    one_slot = one_routes * capacity + jnp.sum(taken * one_hot, axis=0, keepdims=True).astype(jnp.int32)
    two_slot = two_routes * capacity + jnp.sum(taken * two_hot, axis=0, keepdims=True).astype(jnp.int32)
    slots_ref[0:1, :] = one_slot
    slots_ref[1:2, :] = two_slot
    target = lax.broadcasted_iota(jnp.int32, (experts * capacity, token_rows), 0)
    placing = ((target == one_slot) | (target == two_slot)).astype(f32).astype(bf16)
    packed = jnp.dot(placing, own.astype(bf16), preferred_element_type=f32)
    for e in range(experts):
        for half in range(2):
            block = packed[e * capacity : (e + 1) * capacity, half * eighth : (half + 1) * eighth]
            packed_ref[2 * e + half] = block.astype(bf16)


def expert_units(blocks_ref, *refs):
    f32, bf16 = jnp.float32, jnp.bfloat16
    inputs, (gate_ref, up_ref, down_ref), outputs = refs[:12], refs[12:15], refs[15:]
    rows, eighth = outputs[0].shape
    half = rows // 2

    def window(i):
        return pl.ds(pl.multiple_of(blocks_ref[i] * eighth, eighth), eighth)

    for part in range(2):
        span = slice(part * half, (part + 1) * half)
        gate = up = None
        for core in range(2):
            own, side, y_low, y_high, d_low, d_high = inputs[6 * core : 6 * core + 6]
            pieces = (own[span], side[span], (y_low, y_high)[part][...], (d_low, d_high)[part][...])
            for i, piece in enumerate(pieces):
                more_gate = jnp.dot(piece, gate_ref[window(4 * core + i), :], preferred_element_type=f32)
                more_up = jnp.dot(piece, up_ref[window(4 * core + i), :], preferred_element_type=f32)
                gate = more_gate if gate is None else gate + more_gate
                up = more_up if up is None else up + more_up
        act = (gate / (1.0 + jnp.exp(-gate)) * up).astype(bf16)
        for i in range(8):
            outputs[i][span] = jnp.dot(act, down_ref[:, window(i)], preferred_element_type=f32).astype(bf16)


def join(near_ref, x_ref, y_low_ref, y_high_ref, *refs):
    out_ref = refs[-1]
    half = y_low_ref.shape[0]
    for part, y_ref in enumerate((y_low_ref, y_high_ref)):
        span = slice(part * half, (part + 1) * half)
        total = near_ref[span].astype(jnp.float32) + x_ref[span].astype(jnp.float32) + y_ref[...].astype(jnp.float32)
        out_ref[span] = total.astype(out_ref.dtype)


def finish(part_ref, combine_ref, returned_ref, hidden_ref, gain_ref, residual_ref, scaled_ref):
    f32, bf16 = jnp.float32, jnp.bfloat16
    token_rows = hidden_ref.shape[0]
    eighth = returned_ref.shape[1]
    quarter = 2 * eighth
    squares = jnp.zeros((token_rows, 1), f32)
    for half in range(2):
        start = pl.multiple_of(part_ref[0] * quarter + half * eighth, eighth)
        terms = jnp.dot(combine_ref[half], returned_ref[...], preferred_element_type=f32)
        moe = terms[:token_rows] + terms[token_rows:]
        value = hidden_ref[:, pl.ds(start, eighth)].astype(f32) + moe
        residual_ref[:, half * eighth : (half + 1) * eighth] = value
        scaled_ref[:, half * eighth : (half + 1) * eighth] = (value * gain_ref[:, pl.ds(start, eighth)].astype(f32)).astype(bf16)
        squares = squares + jnp.sum(value * value, axis=1, keepdims=True)
    high = squares.astype(bf16).astype(f32)
    lane = lax.broadcasted_iota(jnp.int32, (token_rows, LANES), 1)
    extra = jnp.where(lane == 0, high, jnp.where(lane == 1, squares - high, 0.0))
    scaled_ref[:, quarter:] = extra.astype(bf16)


def last_step(part_ref, own_ref, core_ref, y_ref, diagonal_ref, weight_ref, query_ref, top_ref, total_ref, mixed_ref, kv_ref, out_ref, *, draft):
    f32, bf16 = jnp.float32, jnp.bfloat16
    token_rows = query_ref.shape[0]
    head_dim = kv_ref.shape[1] // 2
    quarter = own_ref.shape[1] - LANES
    parts = (own_ref, core_ref, y_ref, diagonal_ref)
    squares = jnp.zeros((token_rows, LANES), f32)
    fresh = jnp.zeros((token_rows, 2 * head_dim), f32)
    for i, ref in enumerate(parts):
        rows = pl.ds(pl.multiple_of((part_ref[0] ^ i) * quarter, quarter), quarter)
        fresh = fresh + jnp.dot(ref[:, :quarter], weight_ref[rows, :], preferred_element_type=f32)
        squares = squares + ref[:, quarter:].astype(f32)
    square_sum = jnp.sum(squares, axis=1, keepdims=True)
    fresh = (fresh * inverse_rms(square_sum, len(parts) * quarter)).astype(bf16)
    kv_ref[...] = fresh
    keys, values = fresh[:, :head_dim], fresh[:, head_dim:]
    row = lax.broadcasted_iota(jnp.int32, (token_rows, token_rows), 0)
    col = lax.broadcasted_iota(jnp.int32, (token_rows, token_rows), 1)
    seen = (row // draft == col // draft) & (col <= row)
    for h in range(query_ref.shape[1] // head_dim):
        lanes = slice(h * head_dim, (h + 1) * head_dim)
        scores = lax.dot_general(
            query_ref[:, lanes], keys, (((1,), (1,)), ((), ())), preferred_element_type=f32
        )
        scores = jnp.where(seen, scores * head_dim ** (-0.5), -jnp.inf)
        top = top_ref[:, lanes][:, :1]
        new_top = jnp.maximum(top, jnp.max(scores, axis=1, keepdims=True))
        exps = jnp.exp(scores - new_top)
        shrink = jnp.exp(top - new_top)
        denom = shrink * total_ref[:, lanes][:, :1] + jnp.sum(exps, axis=1, keepdims=True)
        mixed = mixed_ref[:, lanes] * (shrink / denom)
        mixed = mixed + jnp.dot((exps / denom).astype(bf16), values, preferred_element_type=f32)
        out_ref[:, lanes] = mixed.astype(bf16)


def call(kernel, out_shape, args, smem=0, name=None, away=0, flops=0):
    spaces = [pltpu.SMEM] * smem + [pltpu.VMEM] * (len(args) - smem - away) + [pl.ANY] * away
    out_specs = jax.tree.map(lambda _: pl.BlockSpec(memory_space=pltpu.VMEM), out_shape)
    moved = sum(x.size * x.dtype.itemsize for x in list(args) + jax.tree.leaves(out_shape))
    return pl.pallas_call(
        kernel,
        out_shape=out_shape,
        in_specs=[pl.BlockSpec(memory_space=space) for space in spaces],
        out_specs=out_specs,
        compiler_params=pltpu.CompilerParams(vmem_limit_bytes=48 << 20),
        cost_estimate=pl.CostEstimate(flops=flops, transcendentals=0, bytes_accessed=moved),
        name=name,
    )(*args)


def cached_attention(table_ref, length_ref, query_ref, pool_ref, top_ref, total_ref, mixed_ref, *, max_blocks):
    requests, rows, head_dim = query_ref.shape
    block_len = pool_ref.shape[2]
    span = max_blocks * block_len
    scale = head_dim ** (-0.5)
    places = lax.broadcasted_iota(jnp.int32, (rows, span), 1)

    def one(r, carry):
        ids = [table_ref[r * max_blocks + b] for b in range(max_blocks)]
        keys = jnp.concatenate([pool_ref[i, 0] for i in ids], axis=0)
        values = jnp.concatenate([pool_ref[i, 1] for i in ids], axis=0)
        scores = lax.dot_general(
            query_ref[r], keys, (((1,), (1,)), ((), ())), preferred_element_type=jnp.float32
        )
        scores = jnp.where(places < length_ref[r], scores * scale, -jnp.inf)
        top = jnp.max(scores, axis=1, keepdims=True)
        exps = jnp.exp(scores - top)
        total = jnp.sum(exps, axis=1, keepdims=True)
        mixed = jnp.dot(exps.astype(jnp.bfloat16), values, preferred_element_type=jnp.float32)
        top_ref[r] = jnp.broadcast_to(top, (rows, head_dim))
        total_ref[r] = jnp.broadcast_to(total, (rows, head_dim))
        mixed_ref[r] = mixed
        return carry

    lax.fori_loop(0, requests, one, 0, unroll=2)


def local(
    hidden_in,
    moe_gain,
    router,
    routes,
    gate_weight,
    up_weight,
    down_weight,
    attn_gain,
    kv_weight,
    queries,
    decode_cache,
    prompt_cache,
    handoff,
    block_table,
    lengths,
):
    peer_count = lax.axis_size("grp")
    expert_count = peer_count // 2
    tp_count = lax.axis_size("tp")
    tp_rank = lax.axis_index("tp")
    token_rows, model_width = hidden_in.shape
    picks_per = routes.shape[1]
    quarter = model_width // tp_count
    capacity = min(token_rows, 3 * token_rows * picks_per // (2 * expert_count))
    total_slots = 2 * expert_count * capacity
    eighth = quarter // 2
    f32, bf16 = jnp.float32, jnp.bfloat16
    shape = jax.ShapeDtypeStruct
    side = lax.axis_index("grp") & 1
    part = tp_rank.astype(jnp.int32).reshape(1)

    ordered = jnp.take(prompt_cache[:, 0], handoff[0], axis=0)
    crossed = swapped(ordered, "role", 0)

    packed, slots = call(
        functools.partial(prepare, capacity=capacity),
        (shape((peer_count, capacity, eighth), bf16), shape((picks_per, token_rows), jnp.int32)),
        (part, routes.T, hidden_in, moe_gain.reshape(1, model_width), ordered),
        smem=1,
        away=1,
        name="prepare",
    )
    landed = lax.all_to_all(packed, "grp", split_axis=0, concat_axis=0, tiled=True)
    landed = landed.reshape(total_slots, eighth)

    arrived = lax.all_to_all(crossed, "grp", split_axis=0, concat_axis=0, tiled=True)

    hidden = hidden_in.astype(f32)
    scale_in = inverse_rms(jnp.sum(hidden * hidden, axis=1, keepdims=True), model_width)
    moe_in = (hidden * scale_in * moe_gain.astype(f32)).astype(bf16)
    logits = jnp.dot(moe_in, router, preferred_element_type=f32)
    gate_probs = jax.nn.softmax(jnp.take_along_axis(logits, routes, axis=1), axis=1)
    targets = jnp.arange(total_slots, dtype=jnp.int32)
    target_slot = targets // (2 * capacity) * capacity + targets % capacity
    hits = (slots.T[:, :, None] == target_slot).astype(f32)
    combine = jnp.sum(hits * gate_probs[:, :, None], axis=1)
    combine_high = combine.astype(bf16)
    combine_low = (combine - combine_high.astype(f32)).astype(bf16)
    both_terms = jnp.concatenate([combine_high, combine_low], axis=0)
    target_half = targets // capacity % 2
    halves = jnp.stack([jnp.where(target_half == i, both_terms, jnp.zeros((), bf16)) for i in range(2)])

    from_x = swapped(landed, "grp", 0)
    y_low, y_high = across(landed)
    d_low, d_high = swapped(y_low, "grp", 0), swapped(y_high, "grp", 0)
    mine = (landed, from_x, y_low, y_high, d_low, d_high)
    theirs = tuple(swapped(x, "tp", 0) for x in mine)
    blocks = jnp.stack(
        [
            (tp_rank ^ (core + 2 * y)) * 2 + (side ^ x)
            for core in range(2)
            for y, x in ((0, 0), (0, 1), (1, 0), (1, 1))
        ]
    ).astype(jnp.int32)
    sums = call(
        expert_units,
        (shape((total_slots, eighth), bf16),) * 8,
        (blocks, *mine, *theirs, gate_weight[0], up_weight[0], down_weight[0]),
        smem=1,
        name="expert_units",
        flops=6 * total_slots * model_width * gate_weight.shape[2],
    )

    def both_cores(i):
        return sums[i].astype(f32) + swapped(sums[4 + i], "tp", 0).astype(f32)

    far = swapped(both_cores(3).astype(bf16), "grp", 0)
    far = (both_cores(2) + far.astype(f32)).astype(bf16)
    sum_x = swapped(both_cores(1).astype(bf16), "grp", 0)
    sum_low, sum_high = across(far)
    near = both_cores(0).astype(bf16)

    requests, max_blocks = block_table.shape
    head_dim = kv_weight.shape[2]
    draft_count = token_rows // requests
    per_kv = queries.shape[1] // head_dim
    query_rows = queries.reshape(requests, draft_count * per_kv, head_dim)
    pool = jnp.concatenate([decode_cache[:, 0], arrived], axis=0)
    stats = call(
        functools.partial(cached_attention, max_blocks=max_blocks),
        (shape((requests, draft_count * per_kv, head_dim), f32),) * 3,
        (block_table.reshape(-1), lengths, query_rows, pool),
        smem=2,
        name="cached_attention",
        flops=4 * requests * draft_count * per_kv * head_dim * max_blocks * decode_cache.shape[3],
    )
    stats = tuple(x.reshape(token_rows, per_kv * head_dim) for x in stats)
    summed = call(
        join,
        shape((total_slots, eighth), bf16),
        (near, sum_x, sum_low, sum_high, *stats),
        away=3,
        name="join",
    )
    returned = lax.all_to_all(
        summed.reshape(peer_count, capacity, eighth), "grp", split_axis=0, concat_axis=0, tiled=True
    ).reshape(total_slots, eighth)
    residual_out, scaled = call(
        finish,
        (shape((token_rows, quarter), f32), shape((token_rows, quarter + LANES), bf16)),
        (part, halves, returned, hidden_in, attn_gain.reshape(1, model_width)),
        smem=1,
        name="finish",
    )

    scaled_core = swapped(scaled, "tp", 0)
    scaled_y = swapped(scaled, "tp", 1)
    scaled_diagonal = swapped(scaled_y, "tp", 0)
    fresh_kv, attn_out = call(
        functools.partial(last_step, draft=draft_count),
        (shape((token_rows, 2 * head_dim), bf16), shape((token_rows, per_kv * head_dim), bf16)),
        (part, scaled, scaled_core, scaled_y, scaled_diagonal, kv_weight.reshape(model_width, 2 * head_dim), queries, *stats),
        smem=1,
        name="last_step",
    )
    return (residual_out, fresh_kv.reshape(token_rows, 2, head_dim), attn_out)


def solution(mesh):
    in_specs = (
        P(("role", "grp"), None),
        P(),
        P(),
        P(("role", "grp"), None),
        P("grp", None, "tp"),
        P("grp", None, "tp"),
        P("grp", "tp", None),
        P(),
        P(None, None, "tp"),
        P(("role", "grp"), "tp"),
        P(("role", "grp"), "tp", None, None, None),
        P(("role", "grp"), "tp", None, None, None),
        P(("role", "grp"), None),
        P(("role", "grp"), None),
        P(("role", "grp")),
    )
    out_specs = (P(("role", "grp"), "tp"), P(("role", "grp"), None, "tp"), P(("role", "grp"), "tp"))
    return jax.shard_map(local, mesh=mesh, in_specs=in_specs, out_specs=out_specs, check_vma=False)
```

profile of v0, /device:TPU:1, one launch (start us, length us, event | category | flops | bytes accessed | tf_op | source)
XLA Modules:
  0.0 265.1 jit_solution(12121106225934844739)
XLA Ops:
  2.9 2.2 gather_fusion
  5.0 1.9 broadcast_select_fusion.ordered_ref
  9.1 12.0 %all-to-all-start = ((bf16[32,24,512]{2,1,0:T(8,128)(2,1)}), bf16[32,24,512]{2,1,0:T(8,128)(2,1)}, u32[]{:S(2)}, u32[]{:S(2)}) async-start(bf16[32,24,512]{2,1,0:T(8,128)(2,1)} %copy-done.14), calls=%async_computation | async-start | bytes 1572864 | tf_op jit(solution)/shard_map/all_to_all | solution.py:243
  22.5 19.7 %all-to-all-done = bf16[32,24,512]{2,1,0:T(8,128)(2,1)} async-done(((bf16[32,24,512]{2,1,0:T(8,128)(2,1)}), bf16[32,24,512]{2,1,0:T(8,128)(2,1)}, u32[]{:S(2)}, u32[]{:S(2)}) %all-to-all-start) | async-done | bytes 786464 | tf_op jit(solution)/shard_map/all_to_all | solution.py:243
  47.7 3.0 %collective-permute-start.7 = (bf16[768,512]{1,0:T(8,128)(2,1)}, bf16[768,512]{1,0:T(8,128)(2,1)}, u32[]{:S(2)}, u32[]{:S(2)}) collective-permute-start(bf16[768,512]{1,0:T(8,128)(2,1)} %bitcast.18.refs_0_), channel_id=1, source_target_pairs={{0,1},{1,0},{2,3},{3,2},{4,5},{5,4},{6,7},{7,6},{8,9},{9,8},{10,11... | collective-permute-start | bytes 2359304 | tf_op jit(solution)/shard_map/ppermute | solution.py:15
  50.8 24.1 %collective-permute-done.1 = bf16[384,512]{1,0:T(8,128)(2,1)S(1)} collective-permute-done((bf16[384,512]{1,0:T(8,128)(2,1)S(1)}, bf16[384,512]{1,0:T(8,128)(2,1)S(1)}, u32[]{:S(2)}, u32[]{:S(2)}) %collective-permute-start.1) | collective-permute-done | bytes 393248 | tf_op jit(solution)/shard_map/ppermute | solution.py:26
  74.9 2.2 collective-permute-start.2
  78.5 7.7 %collective-permute-done.2.refs_2_ = bf16[384,512]{1,0:T(8,128)(2,1)} collective-permute-done((bf16[384,512]{1,0:T(8,128)(2,1)S(1)}, bf16[384,512]{1,0:T(8,128)(2,1)}, u32[]{:S(2)}, u32[]{:S(2)}) %collective-permute-start.2) | collective-permute-done | bytes 393248 | tf_op jit(solution)/shard_map/ppermute | solution.py:26
  87.7 3.1 %collective-permute-start.8 = (bf16[768,512]{1,0:T(8,128)(2,1)}, bf16[768,512]{1,0:T(8,128)(2,1)}, u32[]{:S(2)}, u32[]{:S(2)}) collective-permute-start(bf16[768,512]{1,0:T(8,128)(2,1)} %collective-permute-done.refs_1_), channel_id=1, source_target_pairs={{0,1},{1,0},{2,3},{3,2},{4,5},{5,4},{6,7},{7,6},{8,9},{9,8},{10,11... | collective-permute-start | bytes 2359304 | tf_op jit(solution)/shard_map/ppermute | solution.py:15
  90.7 9.0 %all-to-all-start.1 = ((bf16[32,2,128,128]{3,2,1,0:T(8,128)(2,1)}), bf16[32,2,128,128]{3,2,1,0:T(8,128)(2,1)}, u32[]{:S(2)}, u32[]{:S(2)}) async-start(bf16[32,2,128,128]{3,2,1,0:T(8,128)(2,1)} %collective-permute-done.23), calls=%async_computation.1 | async-start | bytes 4194304 | tf_op jit(solution)/shard_map/all_to_all | solution.py:246
  101.1 2.0 collective-permute-done.6.refs_5_
  103.0 12.5 %collective-permute-start.12 = (bf16[384,512]{1,0:T(8,128)(2,1)}, bf16[384,512]{1,0:T(8,128)(2,1)S(1)}, u32[]{:S(2)}, u32[]{:S(2)}) collective-permute-start(bf16[384,512]{1,0:T(8,128)(2,1)} %collective-permute-done.6.refs_5_), channel_id=1, source_target_pairs={{0,1},{1,0},{2,3},{3,2},{4,5},{5,4},{6,7},{7,6},{8,9},{9,8},{10,11... | collective-permute-start | bytes 1179656 | tf_op jit(solution)/shard_map/ppermute | solution.py:15
  115.5 3.8 %copy.43 = bf16[1,4096,192]{2,1,0:T(8,128)(2,1)} copy(bf16[1,4096,192]{1,2,0:T(8,128)(2,1)} %param.19) | data formatting | bytes 3145728 | tf_op args[4]
  119.3 3.8 %copy.44 = bf16[1,4096,192]{2,1,0:T(8,128)(2,1)} copy(bf16[1,4096,192]{1,2,0:T(8,128)(2,1)} %param.20) | data formatting | bytes 3145728 | tf_op args[5]
  130.2 10.7 %expert_units.1 = (bf16[768,512]{1,0:T(8,128)(2,1)S(1)}, bf16[768,512]{1,0:T(8,128)(2,1)S(1)}, bf16[768,512]{1,0:T(8,128)(2,1)S(1)}, bf16[768,512]{1,0:T(8,128)(...) custom-call(s32[8]{0:T(128)S(1)} %stack.41.blocks_ref, ...), custom_call_target="tpu_custom_call" | custom-call | flops 3623878656 | bytes 17301536 | tf_op jit(solution)/shard_map/expert_units/pallas_call | solution.py:162
  141.6 1.9 collective-permute-done.17
  146.6 1.8 collective-permute-start.15
  148.3 15.6 %collective-permute-done.18 = bf16[768,512]{1,0:T(8,128)(2,1)S(1)} collective-permute-done((bf16[768,512]{1,0:T(8,128)(2,1)S(1)}, bf16[768,512]{1,0:T(8,128)(2,1)S(1)}, u32[]{:S(2)}, u32[]{:S(2)}) %collective-permute-start.18) | collective-permute-done | bytes 786464 | tf_op jit(solution)/shard_map/ppermute | solution.py:15
  165.1 2.7 %collective-permute-start.21 = (bf16[384,512]{1,0:T(8,128)(2,1)}, bf16[384,512]{1,0:T(8,128)(2,1)}, u32[]{:S(2)}, u32[]{:S(2)}) collective-permute-start(bf16[384,512]{1,0:T(8,128)(2,1)} %get-tuple-element.39), channel_id=1, source_target_pairs={{0,130},{1,131},{2,128},{3,129},{128,0},{129,1},{130,2},{131,3},{4... | collective-permute-start | bytes 1179656 | tf_op jit(solution)/shard_map/ppermute | solution.py:26
  168.9 2.0 gather_fusion.1
  171.7 3.8 %collective-permute-done.19 = bf16[384,512]{1,0:T(8,128)(2,1)} collective-permute-done((bf16[384,512]{1,0:T(8,128)(2,1)S(1)}, bf16[384,512]{1,0:T(8,128)(2,1)}, u32[]{:S(2)}, u32[]{:S(2)}) %collective-permute-start.19) | collective-permute-done | bytes 393248 | tf_op jit(solution)/shard_map/ppermute | solution.py:26
  175.5 2.7 %collective-permute-start.22 = (bf16[384,512]{1,0:T(8,128)(2,1)}, bf16[384,512]{1,0:T(8,128)(2,1)}, u32[]{:S(2)}, u32[]{:S(2)}) collective-permute-start(bf16[384,512]{1,0:T(8,128)(2,1)} %collective-permute-done.21), channel_id=1, source_target_pairs={{0,130},{1,131},{2,128},{3,129},{128,0},{129,1},{130,2},{131,3},{4... | collective-permute-start | bytes 1179656 | tf_op jit(solution)/shard_map/ppermute | solution.py:26
  178.2 2.3 add_convert_fusion.3.near_ref
  180.5 3.8 %pad_maximum_fusion.pool_ref = bf16[48,2,128,128]{3,2,1,0:T(8,128)(2,1)} fusion(bf16[32,2,128,128]{3,2,1,0:T(8,128)(2,1)} %all-to-all-done.1, bf16[16,2,128,128]{3,2,1,0:T(8,128)(2,1)} %bitcast.49), kind=kLoop, calls=%fused_computation.2 | loop fusion | flops 1572864 | bytes 6291456 | tf_op jit(solution)/shard_map/concatenate | solution.py:298
  184.3 12.1 %cached_attention.1 = (f32[32,64,128]{2,1,0:T(8,128)S(1)}, f32[32,64,128]{2,1,0:T(8,128)S(1)}, f32[32,64,128]{2,1,0:T(8,128)S(1)}) custom-call(s32[128]{0:T(128)S(1)} %reshape.226.table_ref, s32[32]{0:T(128)S(1)} %copy-done.17, bf16[32,64,128]{2,1,0:T(8,128)(2,1)S(1)} %reshape.227.query_ref, bf16[48,2,128,128]{3,2,1,0:T(8,128)(2,1)} %pad_maximum_fusion.pool_ref), custom_call_target="tpu_custom_call" | custom-call | flops 536870912 | bytes 6816384 | tf_op jit(solution)/shard_map/cached_attention/pallas_call | solution.py:162
  202.2 2.8 %reshape.230.refs_2_.mixed_ref = f32[128,2048]{1,0:T(8,128)} reshape(f32[32,64,128]{2,1,0:T(8,128)} %copy-done.11) | data formatting | bytes 2097152 | tf_op jit(solution)/shard_map/reshape | solution.py:307
  208.6 8.8 %all-to-all-start.2 = ((bf16[32,24,512]{2,1,0:T(8,128)(2,1)}), bf16[32,24,512]{2,1,0:T(8,128)(2,1)S(1)}, u32[]{:S(2)}, u32[]{:S(2)}) async-start(bf16[32,24,512]{2,1,0:T(8,128)(2,1)} %bitcast.41), calls=%async_computation.2 | async-start | bytes 1572864 | tf_op jit(solution)/shard_map/all_to_all | solution.py:315
  220.1 15.6 %all-to-all-done.2 = bf16[32,24,512]{2,1,0:T(8,128)(2,1)S(1)} async-done(((bf16[32,24,512]{2,1,0:T(8,128)(2,1)}), bf16[32,24,512]{2,1,0:T(8,128)(2,1)S(1)}, u32[]{:S(2)}, u32[]{:S(2)}) %all-to-all-start.2) | async-done | bytes 786464 | tf_op jit(solution)/shard_map/all_to_all | solution.py:315
  238.4 5.5 %collective-permute-start.24 = (bf16[128,1152]{1,0:T(8,128)(2,1)S(1)}, bf16[128,1152]{1,0:T(8,128)(2,1)S(1)}, u32[]{:S(2)}, u32[]{:S(2)}) collective-permute-start(bf16[128,1152]{1,0:T(8,128)(2,1)S(1)} %get-tuple-element.34.own_ref), channel_id=1, source_target_pairs={{0,1},{1,0},{2,3},{3,2},{4,5},{5,4},{6,7},{7,6},{8,9},{9,8},{10,11... | collective-permute-start | bytes 884744 | tf_op jit(solution)/shard_map/ppermute | solution.py:15
  245.4 6.8 %collective-permute-start.26 = (bf16[128,1152]{1,0:T(8,128)(2,1)S(1)}, bf16[128,1152]{1,0:T(8,128)(2,1)S(1)}, u32[]{:S(2)}, u32[]{:S(2)}) collective-permute-start(bf16[128,1152]{1,0:T(8,128)(2,1)S(1)} %collective-permute-done.25.y_ref), channel_id=1, source_target_pairs={{0,1},{1,0},{2,3},{3,2},{4,5},{5,4},{6,7},{7,6},{8,9},{9,8},{10,11... | collective-permute-start | bytes 884744 | tf_op jit(solution)/shard_map/ppermute | solution.py:15
  252.2 1.6 copy.48
  254.6 9.9 %last_step.1 = (bf16[128,256]{1,0:T(8,128)(2,1)S(1)}, bf16[128,2048]{1,0:T(8,128)(2,1)}) custom-call(s32[1]{0:T(128)} %bitcast.part_ref, bf16[128,1152]{1,0:T(8,128)(2,1)S(1)} %get-tuple-element.34.own_ref, bf16[128,1152]{1,0:T(8,128)(2,1)S(1)} %collective-permute-done.24.core_ref, bf16[128,1152]{1,0:T(8,128)(2,1)S(1)} %collective-permute-done.25.y_ref, ...), custom_call_target="tpu_custom_call" | custom-call | bytes 7536644 | tf_op jit(solution)/shard_map/last_step/pallas_call | solution.py:162
  (140 shorter events, 46.9 us)
Async XLA Ops:
  9.1 33.0 %all-to-all-start = ((bf16[32,24,512]{2,1,0:T(8,128)(2,1)}), bf16[32,24,512]{2,1,0:T(8,128)(2,1)}, u32[]{:S(2)}, u32[]{:S(2)}) async-start(bf16[32,24,512]{2,1,0:T(8,128)(2,1)} %copy-done.14), calls=%async_computation | async-start | bytes 1572864 | tf_op jit(solution)/shard_map/all_to_all | solution.py:243
  21.1 69.6 %collective-permute-start.23 = (bf16[32,2,128,128]{3,2,1,0:T(8,128)(2,1)S(1)}, bf16[32,2,128,128]{3,2,1,0:T(8,128)(2,1)}, u32[]{:S(2)}, u32[]{:S(2)}) collective-permute-start(bf16[32,2,128,128]{3,2,1,0:T(8,128)(2,1)S(1)} %broadcast_select_fusion.ordered_ref), channel_id=1, source_target_pairs={{0,128},{128,0},{1,129},{129,1},{2,130},{130,2},{3,131},{131,3},{4... | collective-permute-start | bytes 6291464 | tf_op jit(solution)/shard_map/ppermute | solution.py:15
  43.3 31.6 %collective-permute-start.1 = (bf16[384,512]{1,0:T(8,128)(2,1)S(1)}, bf16[384,512]{1,0:T(8,128)(2,1)S(1)}, u32[]{:S(2)}, u32[]{:S(2)}) collective-permute-start(bf16[384,512]{1,0:T(8,128)(2,1)S(1)} %bitcast.51), channel_id=1, source_target_pairs={{0,128},{1,129},{2,130},{3,131},{128,2},{129,3},{130,0},{131,1},{4... | collective-permute-start | bytes 1179656 | tf_op jit(solution)/shard_map/ppermute | solution.py:26
  44.7 32.4 %collective-permute-start.3 = (bf16[384,512]{1,0:T(8,128)(2,1)S(1)}, bf16[384,512]{1,0:T(8,128)(2,1)S(1)}, u32[]{:S(2)}, u32[]{:S(2)}) collective-permute-start(bf16[384,512]{1,0:T(8,128)(2,1)S(1)} %bitcast.50), channel_id=1, source_target_pairs={{0,130},{1,131},{2,128},{3,129},{128,0},{129,1},{130,2},{131,3},{4... | collective-permute-start | bytes 1179656 | tf_op jit(solution)/shard_map/ppermute | solution.py:26
  46.2 41.4 %collective-permute-start = (bf16[768,512]{1,0:T(8,128)(2,1)}, bf16[768,512]{1,0:T(8,128)(2,1)}, u32[]{:S(2)}, u32[]{:S(2)}) collective-permute-start(bf16[768,512]{1,0:T(8,128)(2,1)} %bitcast.18.refs_0_), channel_id=1, source_target_pairs={{0,4},{4,0},{8,12},{12,8},{16,20},{20,16},{24,28},{28,24},{32,36},... | collective-permute-start | bytes 2359304 | tf_op jit(solution)/shard_map/ppermute | solution.py:15
  47.7 52.4 %collective-permute-start.7 = (bf16[768,512]{1,0:T(8,128)(2,1)}, bf16[768,512]{1,0:T(8,128)(2,1)}, u32[]{:S(2)}, u32[]{:S(2)}) collective-permute-start(bf16[768,512]{1,0:T(8,128)(2,1)} %bitcast.18.refs_0_), channel_id=1, source_target_pairs={{0,1},{1,0},{2,3},{3,2},{4,5},{5,4},{6,7},{7,6},{8,9},{9,8},{10,11... | collective-permute-start | bytes 2359304 | tf_op jit(solution)/shard_map/ppermute | solution.py:15
  74.9 11.3 %collective-permute-start.2 = (bf16[384,512]{1,0:T(8,128)(2,1)S(1)}, bf16[384,512]{1,0:T(8,128)(2,1)}, u32[]{:S(2)}, u32[]{:S(2)}) collective-permute-start(bf16[384,512]{1,0:T(8,128)(2,1)S(1)} %collective-permute-done.1), channel_id=1, source_target_pairs={{0,128},{1,129},{2,130},{3,131},{128,2},{129,3},{130,0},{131,1},{4... | collective-permute-start | bytes 1179656 | tf_op jit(solution)/shard_map/ppermute | solution.py:26
  77.1 9.7 %collective-permute-start.4 = (bf16[384,512]{1,0:T(8,128)(2,1)S(1)}, bf16[384,512]{1,0:T(8,128)(2,1)}, u32[]{:S(2)}, u32[]{:S(2)}) collective-permute-start(bf16[384,512]{1,0:T(8,128)(2,1)S(1)} %collective-permute-done.3), channel_id=1, source_target_pairs={{0,130},{1,131},{2,128},{3,129},{128,0},{129,1},{130,2},{131,3},{4... | collective-permute-start | bytes 1179656 | tf_op jit(solution)/shard_map/ppermute | solution.py:26
  86.2 14.1 %collective-permute-start.5 = (bf16[384,512]{1,0:T(8,128)(2,1)}, bf16[384,512]{1,0:T(8,128)(2,1)}, u32[]{:S(2)}, u32[]{:S(2)}) collective-permute-start(bf16[384,512]{1,0:T(8,128)(2,1)} %collective-permute-done.2.refs_2_), channel_id=1, source_target_pairs={{0,4},{4,0},{8,12},{12,8},{16,20},{20,16},{24,28},{28,24},{32,36},... | collective-permute-start | bytes 1179656 | tf_op jit(solution)/shard_map/ppermute | solution.py:15
  86.8 16.3 %collective-permute-start.6 = (bf16[384,512]{1,0:T(8,128)(2,1)}, bf16[384,512]{1,0:T(8,128)(2,1)}, u32[]{:S(2)}, u32[]{:S(2)}) collective-permute-start(bf16[384,512]{1,0:T(8,128)(2,1)} %collective-permute-done.4.refs_3_), channel_id=1, source_target_pairs={{0,4},{4,0},{8,12},{12,8},{16,20},{20,16},{24,28},{28,24},{32,36},... | collective-permute-start | bytes 1179656 | tf_op jit(solution)/shard_map/ppermute | solution.py:15
  87.7 38.6 %collective-permute-start.8 = (bf16[768,512]{1,0:T(8,128)(2,1)}, bf16[768,512]{1,0:T(8,128)(2,1)}, u32[]{:S(2)}, u32[]{:S(2)}) collective-permute-start(bf16[768,512]{1,0:T(8,128)(2,1)} %collective-permute-done.refs_1_), channel_id=1, source_target_pairs={{0,1},{1,0},{2,3},{3,2},{4,5},{5,4},{6,7},{7,6},{8,9},{9,8},{10,11... | collective-permute-start | bytes 2359304 | tf_op jit(solution)/shard_map/ppermute | solution.py:15
  90.7 89.8 %all-to-all-start.1 = ((bf16[32,2,128,128]{3,2,1,0:T(8,128)(2,1)}), bf16[32,2,128,128]{3,2,1,0:T(8,128)(2,1)}, u32[]{:S(2)}, u32[]{:S(2)}) async-start(bf16[32,2,128,128]{3,2,1,0:T(8,128)(2,1)} %collective-permute-done.23), calls=%async_computation.1 | async-start | bytes 4194304 | tf_op jit(solution)/shard_map/all_to_all | solution.py:246
  99.7 23.5 %collective-permute-start.10 = (bf16[384,512]{1,0:T(8,128)(2,1)}, bf16[384,512]{1,0:T(8,128)(2,1)S(1)}, u32[]{:S(2)}, u32[]{:S(2)}) collective-permute-start(bf16[384,512]{1,0:T(8,128)(2,1)} %collective-permute-done.4.refs_3_), channel_id=1, source_target_pairs={{0,1},{1,0},{2,3},{3,2},{4,5},{5,4},{6,7},{7,6},{8,9},{9,8},{10,11... | collective-permute-start | bytes 1179656 | tf_op jit(solution)/shard_map/ppermute | solution.py:15
  100.1 23.9 %collective-permute-start.9 = (bf16[384,512]{1,0:T(8,128)(2,1)}, bf16[384,512]{1,0:T(8,128)(2,1)S(1)}, u32[]{:S(2)}, u32[]{:S(2)}) collective-permute-start(bf16[384,512]{1,0:T(8,128)(2,1)} %collective-permute-done.2.refs_2_), channel_id=1, source_target_pairs={{0,1},{1,0},{2,3},{3,2},{4,5},{5,4},{6,7},{7,6},{8,9},{9,8},{10,11... | collective-permute-start | bytes 1179656 | tf_op jit(solution)/shard_map/ppermute | solution.py:15
  100.3 24.4 %collective-permute-start.11 = (bf16[384,512]{1,0:T(8,128)(2,1)}, bf16[384,512]{1,0:T(8,128)(2,1)S(1)}, u32[]{:S(2)}, u32[]{:S(2)}) collective-permute-start(bf16[384,512]{1,0:T(8,128)(2,1)} %collective-permute-done.5.refs_4_), channel_id=1, source_target_pairs={{0,1},{1,0},{2,3},{3,2},{4,5},{5,4},{6,7},{7,6},{8,9},{9,8},{10,11... | collective-permute-start | bytes 1179656 | tf_op jit(solution)/shard_map/ppermute | solution.py:15
  103.0 22.4 %collective-permute-start.12 = (bf16[384,512]{1,0:T(8,128)(2,1)}, bf16[384,512]{1,0:T(8,128)(2,1)S(1)}, u32[]{:S(2)}, u32[]{:S(2)}) collective-permute-start(bf16[384,512]{1,0:T(8,128)(2,1)} %collective-permute-done.6.refs_5_), channel_id=1, source_target_pairs={{0,1},{1,0},{2,3},{3,2},{4,5},{5,4},{6,7},{7,6},{8,9},{9,8},{10,11... | collective-permute-start | bytes 1179656 | tf_op jit(solution)/shard_map/ppermute | solution.py:15
  141.0 2.5 collective-permute-start.17
  141.0 4.5 %collective-permute-start.14 = (bf16[768,512]{1,0:T(8,128)(2,1)}, bf16[768,512]{1,0:T(8,128)(2,1)S(1)}, u32[]{:S(2)}, u32[]{:S(2)}) collective-permute-start(bf16[768,512]{1,0:T(8,128)(2,1)} %get-tuple-element.25), channel_id=1, source_target_pairs={{0,1},{1,0},{2,3},{3,2},{4,5},{5,4},{6,7},{7,6},{8,9},{9,8},{10,11... | collective-permute-start | bytes 2359304 | tf_op jit(solution)/shard_map/ppermute | solution.py:15
  141.5 6.9 %collective-permute-start.16 = (bf16[768,512]{1,0:T(8,128)(2,1)}, bf16[768,512]{1,0:T(8,128)(2,1)S(1)}, u32[]{:S(2)}, u32[]{:S(2)}) collective-permute-start(bf16[768,512]{1,0:T(8,128)(2,1)} %get-tuple-element.27), channel_id=1, source_target_pairs={{0,1},{1,0},{2,3},{3,2},{4,5},{5,4},{6,7},{7,6},{8,9},{9,8},{10,11... | collective-permute-start | bytes 2359304 | tf_op jit(solution)/shard_map/ppermute | solution.py:15
  144.8 19.1 %collective-permute-start.18 = (bf16[768,512]{1,0:T(8,128)(2,1)S(1)}, bf16[768,512]{1,0:T(8,128)(2,1)S(1)}, u32[]{:S(2)}, u32[]{:S(2)}) collective-permute-start(bf16[768,512]{1,0:T(8,128)(2,1)S(1)} %add_convert_fusion.1), channel_id=1, source_target_pairs={{0,4},{4,0},{8,12},{12,8},{16,20},{20,16},{24,28},{28,24},{32,36},... | collective-permute-start | bytes 2359304 | tf_op jit(solution)/shard_map/ppermute | solution.py:15
  145.2 33.0 %collective-permute-start.13 = (bf16[768,512]{1,0:T(8,128)(2,1)}, bf16[768,512]{1,0:T(8,128)(2,1)}, u32[]{:S(2)}, u32[]{:S(2)}) collective-permute-start(bf16[768,512]{1,0:T(8,128)(2,1)} %get-tuple-element.23), channel_id=1, source_target_pairs={{0,1},{1,0},{2,3},{3,2},{4,5},{5,4},{6,7},{7,6},{8,9},{9,8},{10,11... | collective-permute-start | bytes 2359304 | tf_op jit(solution)/shard_map/ppermute | solution.py:15
  146.6 58.5 %collective-permute-start.15 = (bf16[768,512]{1,0:T(8,128)(2,1)}, bf16[768,512]{1,0:T(8,128)(2,1)}, u32[]{:S(2)}, u32[]{:S(2)}) collective-permute-start(bf16[768,512]{1,0:T(8,128)(2,1)} %add_convert_fusion.2), channel_id=1, source_target_pairs={{0,4},{4,0},{8,12},{12,8},{16,20},{20,16},{24,28},{28,24},{32,36},... | collective-permute-start | bytes 2359304 | tf_op jit(solution)/shard_map/ppermute | solution.py:15
  165.1 10.4 %collective-permute-start.19 = (bf16[384,512]{1,0:T(8,128)(2,1)S(1)}, bf16[384,512]{1,0:T(8,128)(2,1)}, u32[]{:S(2)}, u32[]{:S(2)}) collective-permute-start(bf16[384,512]{1,0:T(8,128)(2,1)S(1)} %get-tuple-element.40), channel_id=1, source_target_pairs={{0,128},{1,129},{2,130},{3,131},{128,2},{129,3},{130,0},{131,1},{4... | collective-permute-start | bytes 1179656 | tf_op jit(solution)/shard_map/ppermute | solution.py:26
  165.1 10.4 %collective-permute-start.21 = (bf16[384,512]{1,0:T(8,128)(2,1)}, bf16[384,512]{1,0:T(8,128)(2,1)}, u32[]{:S(2)}, u32[]{:S(2)}) collective-permute-start(bf16[384,512]{1,0:T(8,128)(2,1)} %get-tuple-element.39), channel_id=1, source_target_pairs={{0,130},{1,131},{2,128},{3,129},{128,0},{129,1},{130,2},{131,3},{4... | collective-permute-start | bytes 1179656 | tf_op jit(solution)/shard_map/ppermute | solution.py:26
  175.5 29.5 %collective-permute-start.20 = (bf16[384,512]{1,0:T(8,128)(2,1)}, bf16[384,512]{1,0:T(8,128)(2,1)S(1)}, u32[]{:S(2)}, u32[]{:S(2)}) collective-permute-start(bf16[384,512]{1,0:T(8,128)(2,1)} %collective-permute-done.19), channel_id=1, source_target_pairs={{0,128},{1,129},{2,130},{3,131},{128,2},{129,3},{130,0},{131,1},{4... | collective-permute-start | bytes 1179656 | tf_op jit(solution)/shard_map/ppermute | solution.py:26
  175.5 29.5 %collective-permute-start.22 = (bf16[384,512]{1,0:T(8,128)(2,1)}, bf16[384,512]{1,0:T(8,128)(2,1)}, u32[]{:S(2)}, u32[]{:S(2)}) collective-permute-start(bf16[384,512]{1,0:T(8,128)(2,1)} %collective-permute-done.21), channel_id=1, source_target_pairs={{0,130},{1,131},{2,128},{3,129},{128,0},{129,1},{130,2},{131,3},{4... | collective-permute-start | bytes 1179656 | tf_op jit(solution)/shard_map/ppermute | solution.py:26
  208.6 27.2 %all-to-all-start.2 = ((bf16[32,24,512]{2,1,0:T(8,128)(2,1)}), bf16[32,24,512]{2,1,0:T(8,128)(2,1)S(1)}, u32[]{:S(2)}, u32[]{:S(2)}) async-start(bf16[32,24,512]{2,1,0:T(8,128)(2,1)} %bitcast.41), calls=%async_computation.2 | async-start | bytes 1572864 | tf_op jit(solution)/shard_map/all_to_all | solution.py:315
  236.9 15.3 %copy-start.26 = (bf16[4096,2,128]{2,1,0:T(2,128)(2,1)S(1)}, bf16[4096,2,128]{2,1,0:T(2,128)(2,1)}, u32[]{:S(2)}) copy-start(bf16[4096,2,128]{2,1,0:T(2,128)(2,1)} %param.23) | copy-start | bytes 6291460
  238.3 7.1 %collective-permute-start.25 = (bf16[128,1152]{1,0:T(8,128)(2,1)S(1)}, bf16[128,1152]{1,0:T(8,128)(2,1)S(1)}, u32[]{:S(2)}, u32[]{:S(2)}) collective-permute-start(bf16[128,1152]{1,0:T(8,128)(2,1)S(1)} %get-tuple-element.34.own_ref), channel_id=1, source_target_pairs={{0,2},{1,3},{2,0},{3,1},{4,6},{5,7},{6,4},{7,5},{8,10},{9,11},{10,... | collective-permute-start | bytes 884744 | tf_op jit(solution)/shard_map/ppermute | solution.py:15
  238.4 15.4 %collective-permute-start.24 = (bf16[128,1152]{1,0:T(8,128)(2,1)S(1)}, bf16[128,1152]{1,0:T(8,128)(2,1)S(1)}, u32[]{:S(2)}, u32[]{:S(2)}) collective-permute-start(bf16[128,1152]{1,0:T(8,128)(2,1)S(1)} %get-tuple-element.34.own_ref), channel_id=1, source_target_pairs={{0,1},{1,0},{2,3},{3,2},{4,5},{5,4},{6,7},{7,6},{8,9},{9,8},{10,11... | collective-permute-start | bytes 884744 | tf_op jit(solution)/shard_map/ppermute | solution.py:15
  245.4 8.5 %collective-permute-start.26 = (bf16[128,1152]{1,0:T(8,128)(2,1)S(1)}, bf16[128,1152]{1,0:T(8,128)(2,1)S(1)}, u32[]{:S(2)}, u32[]{:S(2)}) collective-permute-start(bf16[128,1152]{1,0:T(8,128)(2,1)S(1)} %collective-permute-done.25.y_ref), channel_id=1, source_target_pairs={{0,1},{1,0},{2,3},{3,2},{4,5},{5,4},{6,7},{7,6},{8,9},{9,8},{10,11... | collective-permute-start | bytes 884744 | tf_op jit(solution)/shard_map/ppermute | solution.py:15
  253.8 11.3 %copy-start.1 = (bf16[32,1,2,128,128]{4,3,2,1,0:T(8,128)(2,1)S(1)}, bf16[32,1,2,128,128]{4,3,2,1,0:T(8,128)(2,1)}, u32[]{:S(2)}) copy-start(bf16[32,1,2,128,128]{4,3,2,1,0:T(8,128)(2,1)} %param.26) | copy-start | bytes 6291460
  (29 other events, 54.8 us)
where the time goes:
time: 266 us; the launch traced here: 265 us
  waiting for transfers between devices  91.8 us (35%)
  starting transfers between devices  81 us (30%)
  local copies, waits for them, and re-layouts  39.2 us (15%)
  Pallas kernels  36.3 us (14%)
  other arithmetic  15.4 us (6%)
    ppermute x19, starting transfers between devices, swapped(): lax.ppermute(x, axis, [(i, i ^ 1 << bit) for i in range(lax.axis_size(axi...  39.4 us
    pallas_call x6, Pallas kernels, call(): pl.pallas_call(kernel, out_shape=out_shape, in_specs=[pl.BlockSpec(memory...  36.3 us
    ppermute x8, waiting for transfers between devices, turned(): return lax.ppermute(x, ('role', 'tp'), pairs)  35.5 us
    unnamed x66, local copies, waits for them, and re-layouts  24.7 us
    ppermute x19, waiting for transfers between devices, swapped(): lax.ppermute(x, axis, [(i, i ^ 1 << bit) for i in range(lax.axis_size(axi...  20.9 us
    all_to_all x1, waiting for transfers between devices, local(): lax.all_to_all(packed, 'grp', split_axis=0, concat_axis=0, tiled=True)  19.7 us
    all_to_all x1, waiting for transfers between devices, local(): lax.all_to_all(summed.reshape(peer_count, capacity, eighth), 'grp', split...  15.6 us
    all_to_all x1, starting transfers between devices, local(): lax.all_to_all(packed, 'grp', split_axis=0, concat_axis=0, tiled=True)  12 us
  transfers between devices with their start and end apart: 30, of which 9 were waited for; matrix products, arithmetic and copies ran while one was open for 12% of the time, Pallas kernels for 9%

commit v1 on v0

--- a/solution.py
+++ b/solution.py
@@ -15,28 +15,11 @@
     return lax.ppermute(x, axis, [(i, i ^ 1 << bit) for i in range(lax.axis_size(axis))])
 
 
-def turned(x, step):
-    roles, parts = lax.axis_size("role"), lax.axis_size("tp")
-    chips = roles * parts // 2
-    pairs = []
-    for role in range(roles):
-        for part in range(parts):
-            place = ((part // 2) * roles + role + step) % chips
-            pairs.append((role * parts + part, (place % roles) * parts + place // roles * 2 + part % 2))
-    return lax.ppermute(x, ("role", "tp"), pairs)
-
-
-def across(x):
-    half = x.shape[0] // 2
-    up, down = turned(x[:half], 1), turned(x[half:], -1)
-    return turned(up, 1), turned(down, -1)
-
-
 def inverse_rms(square_sum, width):
     return lax.rsqrt(square_sum / width + epsilon)
 
 
-def prepare(part_ref, routes_ref, hidden_ref, gain_ref, ordered_ref, packed_ref, slots_ref, *, capacity):
+def prepare(part_ref, routes_ref, hidden_ref, gain_ref, packed_ref, slots_ref, *, capacity):
     token_rows, model_width = hidden_ref.shape
     peers, _, eighth = packed_ref.shape
     experts = peers // 2
@@ -66,42 +49,62 @@
             packed_ref[2 * e + half] = block.astype(bf16)
 
 
-def expert_units(blocks_ref, *refs):
+def wide(a, b):
+    return lax.dot_general(a, b, (((1,), (1,)), ((), ())), preferred_element_type=jnp.float32)
+
+
+def window(blocks_ref, i, size):
+    return pl.ds(pl.multiple_of(blocks_ref[i] * size, size), size)
+
+
+def early_units(blocks_ref, *refs):
+    pieces, (gate_ref, up_ref, gate_out, up_out) = refs[:6], refs[6:]
+    eighth = pieces[0].shape[1]
+    for weight, out in ((gate_ref, gate_out), (up_ref, up_out)):
+        total = None
+        for i, piece in enumerate(pieces):
+            more = wide(piece[...], weight[:, window(blocks_ref, 4 * (i // 3) + i % 3, eighth)])
+            total = more if total is None else total + more
+        out[...] = total
+
+
+def late_units(blocks_ref, mine_ref, theirs_ref, gate_sum, up_sum, gate_ref, up_ref, down_ref, *refs):
+    outputs = refs[-8:]
+    eighth = mine_ref.shape[1]
+    gate, up = gate_sum[...], up_sum[...]
+    for i, piece in ((3, mine_ref), (7, theirs_ref)):
+        gate = gate + wide(piece[...], gate_ref[:, window(blocks_ref, i, eighth)])
+        up = up + wide(piece[...], up_ref[:, window(blocks_ref, i, eighth)])
+    act = (gate / (1.0 + jnp.exp(-gate)) * up).astype(jnp.bfloat16)
+    for i in (3, 7, 2, 6, 1, 5, 0, 4):
+        columns = down_ref[:, window(blocks_ref, i, eighth)]
+        outputs[i][...] = jnp.dot(act, columns, preferred_element_type=jnp.float32).astype(jnp.bfloat16)
+
+
+def join(mine_ref, theirs_ref, x_ref, y_ref, *refs):
+    total = mine_ref[...].astype(jnp.float32) + theirs_ref[...].astype(jnp.float32)
+    total = total + x_ref[...].astype(jnp.float32) + y_ref[...].astype(jnp.float32)
+    refs[-1][...] = total.astype(jnp.bfloat16)
+
+
+def held_until(x, other):
+    def kernel(x_ref, other_ref, out_ref):
+        pass
+
+    any_space = pl.BlockSpec(memory_space=pl.ANY)
+    return pl.pallas_call(
+        kernel,
+        out_shape=jax.ShapeDtypeStruct(x.shape, x.dtype),
+        in_specs=[any_space, any_space],
+        out_specs=any_space,
+        input_output_aliases={0: 0},
+        name="held_until",
+    )(x, other)
+
+
+def finish(part_ref, combine_ref, returned_ref, hidden_ref, gain_ref, *refs):
     f32, bf16 = jnp.float32, jnp.bfloat16
-    inputs, (gate_ref, up_ref, down_ref), outputs = refs[:12], refs[12:15], refs[15:]
-    rows, eighth = outputs[0].shape
-    half = rows // 2
-
-    def window(i):
-        return pl.ds(pl.multiple_of(blocks_ref[i] * eighth, eighth), eighth)
-
-    for part in range(2):
-        span = slice(part * half, (part + 1) * half)
-        gate = up = None
-        for core in range(2):
-            own, side, y_low, y_high, d_low, d_high = inputs[6 * core : 6 * core + 6]
-            pieces = (own[span], side[span], (y_low, y_high)[part][...], (d_low, d_high)[part][...])
-            for i, piece in enumerate(pieces):
-                more_gate = jnp.dot(piece, gate_ref[window(4 * core + i), :], preferred_element_type=f32)
-                more_up = jnp.dot(piece, up_ref[window(4 * core + i), :], preferred_element_type=f32)
-                gate = more_gate if gate is None else gate + more_gate
-                up = more_up if up is None else up + more_up
-        act = (gate / (1.0 + jnp.exp(-gate)) * up).astype(bf16)
-        for i in range(8):
-            outputs[i][span] = jnp.dot(act, down_ref[:, window(i)], preferred_element_type=f32).astype(bf16)
-
-
-def join(near_ref, x_ref, y_low_ref, y_high_ref, *refs):
-    out_ref = refs[-1]
-    half = y_low_ref.shape[0]
-    for part, y_ref in enumerate((y_low_ref, y_high_ref)):
-        span = slice(part * half, (part + 1) * half)
-        total = near_ref[span].astype(jnp.float32) + x_ref[span].astype(jnp.float32) + y_ref[...].astype(jnp.float32)
-        out_ref[span] = total.astype(out_ref.dtype)
-
-
-def finish(part_ref, combine_ref, returned_ref, hidden_ref, gain_ref, residual_ref, scaled_ref):
-    f32, bf16 = jnp.float32, jnp.bfloat16
+    residual_ref, scaled_ref = refs[-2:]
     token_rows = hidden_ref.shape[0]
     eighth = returned_ref.shape[1]
     quarter = 2 * eighth
@@ -135,24 +138,20 @@
     square_sum = jnp.sum(squares, axis=1, keepdims=True)
     fresh = (fresh * inverse_rms(square_sum, len(parts) * quarter)).astype(bf16)
     kv_ref[...] = fresh
-    keys, values = fresh[:, :head_dim], fresh[:, head_dim:]
+    keys = fresh[:, :head_dim]
+    values = jnp.concatenate([fresh[:, head_dim:], jnp.ones((token_rows, head_dim), bf16)], axis=1)
     row = lax.broadcasted_iota(jnp.int32, (token_rows, token_rows), 0)
     col = lax.broadcasted_iota(jnp.int32, (token_rows, token_rows), 1)
     seen = (row // draft == col // draft) & (col <= row)
     for h in range(query_ref.shape[1] // head_dim):
         lanes = slice(h * head_dim, (h + 1) * head_dim)
-        scores = lax.dot_general(
-            query_ref[:, lanes], keys, (((1,), (1,)), ((), ())), preferred_element_type=f32
-        )
-        scores = jnp.where(seen, scores * head_dim ** (-0.5), -jnp.inf)
-        top = top_ref[:, lanes][:, :1]
+        scores = jnp.where(seen, wide(query_ref[:, lanes], keys) * head_dim ** (-0.5), -jnp.inf)
+        top = top_ref[:, lanes]
         new_top = jnp.maximum(top, jnp.max(scores, axis=1, keepdims=True))
-        exps = jnp.exp(scores - new_top)
         shrink = jnp.exp(top - new_top)
-        denom = shrink * total_ref[:, lanes][:, :1] + jnp.sum(exps, axis=1, keepdims=True)
-        mixed = mixed_ref[:, lanes] * (shrink / denom)
-        mixed = mixed + jnp.dot((exps / denom).astype(bf16), values, preferred_element_type=f32)
-        out_ref[:, lanes] = mixed.astype(bf16)
+        recent = jnp.dot(jnp.exp(scores - new_top).astype(bf16), values, preferred_element_type=f32)
+        denom = shrink * total_ref[:, lanes] + recent[:, head_dim:]
+        out_ref[:, lanes] = ((mixed_ref[:, lanes] * shrink + recent[:, :head_dim]) / denom).astype(bf16)
 
 
 def call(kernel, out_shape, args, smem=0, name=None, away=0, flops=0):
@@ -176,22 +175,23 @@
     span = max_blocks * block_len
     scale = head_dim ** (-0.5)
     places = lax.broadcasted_iota(jnp.int32, (rows, span), 1)
+    ones = jnp.ones((span, head_dim), jnp.bfloat16)
 
     def one(r, carry):
         ids = [table_ref[r * max_blocks + b] for b in range(max_blocks)]
         keys = jnp.concatenate([pool_ref[i, 0] for i in ids], axis=0)
         values = jnp.concatenate([pool_ref[i, 1] for i in ids], axis=0)
+        values = jnp.concatenate([values, ones], axis=1)
         scores = lax.dot_general(
             query_ref[r], keys, (((1,), (1,)), ((), ())), preferred_element_type=jnp.float32
         )
         scores = jnp.where(places < length_ref[r], scores * scale, -jnp.inf)
         top = jnp.max(scores, axis=1, keepdims=True)
         exps = jnp.exp(scores - top)
-        total = jnp.sum(exps, axis=1, keepdims=True)
         mixed = jnp.dot(exps.astype(jnp.bfloat16), values, preferred_element_type=jnp.float32)
         top_ref[r] = jnp.broadcast_to(top, (rows, head_dim))
-        total_ref[r] = jnp.broadcast_to(total, (rows, head_dim))
-        mixed_ref[r] = mixed
+        total_ref[r] = mixed[:, head_dim:]
+        mixed_ref[r] = mixed[:, :head_dim]
         return carry
 
     lax.fori_loop(0, requests, one, 0, unroll=2)
@@ -229,21 +229,20 @@
     side = lax.axis_index("grp") & 1
     part = tp_rank.astype(jnp.int32).reshape(1)
 
-    ordered = jnp.take(prompt_cache[:, 0], handoff[0], axis=0)
-    crossed = swapped(ordered, "role", 0)
-
     packed, slots = call(
         functools.partial(prepare, capacity=capacity),
         (shape((peer_count, capacity, eighth), bf16), shape((picks_per, token_rows), jnp.int32)),
-        (part, routes.T, hidden_in, moe_gain.reshape(1, model_width), ordered),
-        smem=1,
-        away=1,
+        (part, routes.T, hidden_in, moe_gain.reshape(1, model_width)),
+        smem=1,
         name="prepare",
     )
     landed = lax.all_to_all(packed, "grp", split_axis=0, concat_axis=0, tiled=True)
     landed = landed.reshape(total_slots, eighth)
 
-    arrived = lax.all_to_all(crossed, "grp", split_axis=0, concat_axis=0, tiled=True)
+    ordered = prompt_cache[:, 0].at[handoff[0]].get(mode="promise_in_bounds")
+    middle = peer_count // 2
+    crossed = swapped(ordered[:middle], "role", 0)
+    landed = held_until(landed, crossed)
 
     hidden = hidden_in.astype(f32)
     scale_in = inverse_rms(jnp.sum(hidden * hidden, axis=1, keepdims=True), model_width)
@@ -261,10 +260,15 @@
     halves = jnp.stack([jnp.where(target_half == i, both_terms, jnp.zeros((), bf16)) for i in range(2)])
 
     from_x = swapped(landed, "grp", 0)
-    y_low, y_high = across(landed)
-    d_low, d_high = swapped(y_low, "grp", 0), swapped(y_high, "grp", 0)
-    mine = (landed, from_x, y_low, y_high, d_low, d_high)
+    from_y = swapped(landed, "tp", 1)
+    mine = (landed, from_x, from_y)
     theirs = tuple(swapped(x, "tp", 0) for x in mine)
+    last_mine = swapped(from_y, "grp", 0)
+    last_theirs = swapped(last_mine, "tp", 0)
+
+    crossed = jnp.concatenate([crossed, swapped(held_until(ordered[middle:], from_y), "role", 0)], axis=0)
+    arrived = lax.all_to_all(crossed, "grp", split_axis=0, concat_axis=0, tiled=True)
+
     blocks = jnp.stack(
         [
             (tp_rank ^ (core + 2 * y)) * 2 + (side ^ x)
@@ -272,23 +276,42 @@
             for y, x in ((0, 0), (0, 1), (1, 0), (1, 1))
         ]
     ).astype(jnp.int32)
+    gate_own, up_own = gate_weight[0].T, up_weight[0].T
+    unit_count = gate_own.shape[0]
     sums = call(
-        expert_units,
+        early_units,
+        (shape((total_slots, unit_count), f32),) * 2,
+        (blocks, *mine, *theirs, gate_own, up_own),
+        smem=1,
+        name="early_units",
+        flops=3 * total_slots * model_width * unit_count,
+    )
+    sums = call(
+        late_units,
         (shape((total_slots, eighth), bf16),) * 8,
-        (blocks, *mine, *theirs, gate_weight[0], up_weight[0], down_weight[0]),
-        smem=1,
-        name="expert_units",
-        flops=6 * total_slots * model_width * gate_weight.shape[2],
+        (blocks, last_mine, last_theirs, *sums, gate_own, up_own, down_weight[0], crossed),
+        smem=1,
+        away=1,
+        name="late_units",
+        flops=3 * total_slots * model_width * unit_count,
     )
 
     def both_cores(i):
         return sums[i].astype(f32) + swapped(sums[4 + i], "tp", 0).astype(f32)
 
     far = swapped(both_cores(3).astype(bf16), "grp", 0)
-    far = (both_cores(2) + far.astype(f32)).astype(bf16)
+    sum_y = swapped((both_cores(2) + far.astype(f32)).astype(bf16), "tp", 1)
     sum_x = swapped(both_cores(1).astype(bf16), "grp", 0)
-    sum_low, sum_high = across(far)
-    near = both_cores(0).astype(bf16)
+    summed = call(
+        join,
+        shape((total_slots, eighth), bf16),
+        (sums[0], swapped(sums[4], "tp", 0), sum_x, sum_y, arrived),
+        away=1,
+        name="join",
+    )
+    returned = lax.all_to_all(
+        summed.reshape(peer_count, capacity, eighth), "grp", split_axis=0, concat_axis=0, tiled=True
+    ).reshape(total_slots, eighth)
 
     requests, max_blocks = block_table.shape
     head_dim = kv_weight.shape[2]
@@ -305,21 +328,13 @@
         flops=4 * requests * draft_count * per_kv * head_dim * max_blocks * decode_cache.shape[3],
     )
     stats = tuple(x.reshape(token_rows, per_kv * head_dim) for x in stats)
-    summed = call(
-        join,
-        shape((total_slots, eighth), bf16),
-        (near, sum_x, sum_low, sum_high, *stats),
-        away=3,
-        name="join",
-    )
-    returned = lax.all_to_all(
-        summed.reshape(peer_count, capacity, eighth), "grp", split_axis=0, concat_axis=0, tiled=True
-    ).reshape(total_slots, eighth)
+    flat_weight = kv_weight.reshape(model_width, 2 * head_dim)
     residual_out, scaled = call(
         finish,
         (shape((token_rows, quarter), f32), shape((token_rows, quarter + LANES), bf16)),
-        (part, halves, returned, hidden_in, attn_gain.reshape(1, model_width)),
-        smem=1,
+        (part, halves, returned, hidden_in, attn_gain.reshape(1, model_width), flat_weight, *stats),
+        smem=1,
+        away=4,
         name="finish",
     )
 
@@ -329,7 +344,7 @@
     fresh_kv, attn_out = call(
         functools.partial(last_step, draft=draft_count),
         (shape((token_rows, 2 * head_dim), bf16), shape((token_rows, per_kv * head_dim), bf16)),
-        (part, scaled, scaled_core, scaled_y, scaled_diagonal, kv_weight.reshape(model_width, 2 * head_dim), queries, *stats),
+        (part, scaled, scaled_core, scaled_y, scaled_diagonal, flat_weight, queries, *stats),
         smem=1,
         name="last_step",
     )

time: 266 us -> 239 us (0.90)
  starting transfers between devices: 81 us -> 65.5 us
  other arithmetic: 15.4 us -> 7.74 us
  waiting for transfers between devices: 91.8 us -> 88.1 us
    ppermute x19, waiting for transfers between devices: 20.9 us -> 88.1 us  [swapped(): lax.ppermute(x, axis, [(i, i ^ 1 << bit) for i in range(lax.axis_size(axi...]
    ppermute x8 -> x0, waiting for transfers between devices: 35.5 us -> none  [turned(): return lax.ppermute(x, ('role', 'tp'), pairs)]
    all_to_all x1, waiting for transfers between devices: 19.7 us -> 0.01 us  [local(): lax.all_to_all(packed, 'grp', split_axis=0, concat_axis=0, tiled=True)]
    all_to_all x1, waiting for transfers between devices: 15.6 us -> 0.01 us  [local(): lax.all_to_all(summed.reshape(peer_count, capacity, eighth), 'grp', split...]
    ppermute x8 -> x0, starting transfers between devices: 11.9 us -> none  [turned(): return lax.ppermute(x, ('role', 'tp'), pairs)]
    unnamed x66 -> x65, local copies, waits for them, and re-layouts: 24.7 us -> 20.9 us
    ppermute x19, starting transfers between devices: 39.4 us -> 35.7 us  [swapped(): lax.ppermute(x, axis, [(i, i ^ 1 << bit) for i in range(lax.axis_size(axi...]
    select_n x2 -> x1, other arithmetic: 2.74 us -> 0.01 us  [local(): ordered = prompt_cache[:, 0].at[handoff[0]].get(mode='promise_in_bounds')]
  transfers between devices with their start and end apart: 30 -> 22, of which waited for: 9 -> 9; matrix products, arithmetic and copies ran while one was open for 12% -> 13% of each run, Pallas kernels for 9% -> 10%
where the time goes in v1:
time: 239 us; the launch traced here: 238 us
  waiting for transfers between devices  88.1 us (37%)
  starting transfers between devices  65.5 us (27%)
  local copies, waits for them, and re-layouts  40.2 us (17%)
  Pallas kernels  34.7 us (15%)
  other arithmetic  7.74 us (3%)
    ppermute x19, waiting for transfers between devices, swapped(): lax.ppermute(x, axis, [(i, i ^ 1 << bit) for i in range(lax.axis_size(axi...  88.1 us
    ppermute x19, starting transfers between devices, swapped(): lax.ppermute(x, axis, [(i, i ^ 1 << bit) for i in range(lax.axis_size(axi...  35.7 us
    pallas_call x7, Pallas kernels, call(): pl.pallas_call(kernel, out_shape=out_shape, in_specs=[pl.BlockSpec(memory...  34.7 us
    unnamed x65, local copies, waits for them, and re-layouts  20.9 us
    all_to_all x1, starting transfers between devices, local(): lax.all_to_all(packed, 'grp', split_axis=0, concat_axis=0, tiled=True)  11.9 us
    all_to_all x1, starting transfers between devices, local(): lax.all_to_all(crossed, 'grp', split_axis=0, concat_axis=0, tiled=True)  9.05 us
    all_to_all x1, starting transfers between devices, local(): lax.all_to_all(summed.reshape(peer_count, capacity, eighth), 'grp', split...  8.84 us
    reshape x3, local copies, waits for them, and re-layouts, local(): stats = tuple((x.reshape(token_rows, per_kv * head_dim) for x in stats))  7.11 us
  transfers between devices with their start and end apart: 22, of which 9 were waited for; matrix products, arithmetic and copies ran while one was open for 13% of the time, Pallas kernels for 10%

profile of v1, /device:TPU:1, one launch (start us, length us, event | category | flops | bytes accessed | tf_op | source)
XLA Modules:
  0.0 237.6 jit_solution(704100006953160929)
XLA Ops:
  5.0 11.9 %all-to-all-start = ((bf16[32,24,512]{2,1,0:T(8,128)(2,1)}), bf16[32,24,512]{2,1,0:T(8,128)(2,1)S(1)}, u32[]{:S(2)}, u32[]{:S(2)}) async-start(bf16[32,24,512]{2,1,0:T(8,128)(2,1)} %copy-done.19), calls=%async_computation | async-start | bytes 1572864 | tf_op jit(solution)/shard_map/all_to_all | solution.py:239
  16.9 2.2 gather_fusion
  19.1 2.7 %fusion.24 = (bf16[16,2,128,128]{3,2,1,0:T(8,128)(2,1)}, bf16[16,2,128,128]{3,2,1,0:T(8,128)(2,1)S(1)}) fusion(bf16[32,2,128,128]{3,2,1,0:T(8,128)(2,1)} %gather_fusion), kind=kLoop, calls=%fused_computation.60 | loop fusion | bytes 4194304 | tf_op jit(solution)/shard_map/slice | solution.py:269
  23.1 22.5 %collective-permute-done.other_ref = bf16[16,2,128,128]{3,2,1,0:T(8,128)(2,1)} collective-permute-done((bf16[16,2,128,128]{3,2,1,0:T(8,128)(2,1)S(1)}, bf16[16,2,128,128]{3,2,1,0:T(8,128)(2,1)}, u32[]{:S(2)}, u32[]{:S(2)}) %collective-permute-start) | collective-permute-done | bytes 1048608 | tf_op jit(solution)/shard_map/ppermute | solution.py:15
  46.5 2.9 %collective-permute-start.1 = (bf16[768,512]{1,0:T(8,128)(2,1)}, bf16[768,512]{1,0:T(8,128)(2,1)}, u32[]{:S(2)}, u32[]{:S(2)}) collective-permute-start(bf16[768,512]{1,0:T(8,128)(2,1)} %held_until.2.refs_0_), channel_id=1, source_target_pairs={{0,2},{1,3},{2,0},{3,1},{4,6},{5,7},{6,4},{7,5},{8,10},{9,11},{10,... | collective-permute-start | bytes 2359304 | tf_op jit(solution)/shard_map/ppermute | solution.py:15
  49.4 16.1 %collective-permute-done.1.refs_2_.other_ref = bf16[768,512]{1,0:T(8,128)(2,1)} collective-permute-done((bf16[768,512]{1,0:T(8,128)(2,1)}, bf16[768,512]{1,0:T(8,128)(2,1)}, u32[]{:S(2)}, u32[]{:S(2)}) %collective-permute-start.1) | collective-permute-done | bytes 786464 | tf_op jit(solution)/shard_map/ppermute | solution.py:15
  68.2 2.3 constant_dynamic-update-slice_fusion.1
  70.6 3.6 %collective-permute-start.5 = (bf16[768,512]{1,0:T(8,128)(2,1)S(1)}, bf16[768,512]{1,0:T(8,128)(2,1)}, u32[]{:S(2)}, u32[]{:S(2)}) collective-permute-start(bf16[768,512]{1,0:T(8,128)(2,1)S(1)} %copy-done.9), channel_id=1, source_target_pairs={{0,1},{1,0},{2,3},{3,2},{4,5},{5,4},{6,7},{7,6},{8,9},{9,8},{10,11... | collective-permute-start | bytes 2359304 | tf_op jit(solution)/shard_map/ppermute | solution.py:15
  74.2 8.6 %collective-permute-done.4.refs_1_ = bf16[768,512]{1,0:T(8,128)(2,1)} collective-permute-done((bf16[768,512]{1,0:T(8,128)(2,1)S(1)}, bf16[768,512]{1,0:T(8,128)(2,1)}, u32[]{:S(2)}, u32[]{:S(2)}) %collective-permute-start.4) | collective-permute-done | bytes 786464 | tf_op jit(solution)/shard_map/ppermute | solution.py:15
  82.8 7.6 %collective-permute-start.6 = (bf16[768,512]{1,0:T(8,128)(2,1)}, bf16[768,512]{1,0:T(8,128)(2,1)}, u32[]{:S(2)}, u32[]{:S(2)}) collective-permute-start(bf16[768,512]{1,0:T(8,128)(2,1)} %collective-permute-done.4.refs_1_), channel_id=1, source_target_pairs={{0,1},{1,0},{2,3},{3,2},{4,5},{5,4},{6,7},{7,6},{8,9},{9,8},{10,11... | collective-permute-start | bytes 2359304 | tf_op jit(solution)/shard_map/ppermute | solution.py:15
  91.4 9.1 %all-to-all-start.1 = ((bf16[32,2,128,128]{3,2,1,0:T(8,128)(2,1)}), bf16[32,2,128,128]{3,2,1,0:T(8,128)(2,1)}, u32[]{:S(2)}, u32[]{:S(2)}) async-start(bf16[32,2,128,128]{3,2,1,0:T(8,128)(2,1)} %constant_dynamic-update-slice_fusion.refs_0_), calls=%async_computation.1 | async-start | bytes 4194304 | tf_op jit(solution)/shard_map/all_to_all | solution.py:270
  100.5 3.3 %collective-permute-start.3 = (bf16[768,512]{1,0:T(8,128)(2,1)}, bf16[768,512]{1,0:T(8,128)(2,1)}, u32[]{:S(2)}, u32[]{:S(2)}) collective-permute-start(bf16[768,512]{1,0:T(8,128)(2,1)} %collective-permute-done.2.mine_ref), channel_id=1, source_target_pairs={{0,1},{1,0},{2,3},{3,2},{4,5},{5,4},{6,7},{7,6},{8,9},{9,8},{10,11... | collective-permute-start | bytes 2359304 | tf_op jit(solution)/shard_map/ppermute | solution.py:15
  103.9 5.7 %early_units.1 = (f32[768,192]{1,0:T(8,128)S(1)}, f32[768,192]{1,0:T(8,128)S(1)}) custom-call(s32[8]{0:T(128)S(1)} %stack.41.blocks_ref, bf16[768,512]{1,0:T(8,128)(2,1)S(1)} %copy-done.9, bf16[768,512]{1,0:T(8,128)(2,1)} %collective-permute-done.4.refs_1_, bf16[768,512]{1,0:T(8,128)(2,1)} %collective-permute-done.1.refs_2_.other_ref, ...), custom_call_target="tpu_custom_call" | custom-call | flops 1811939328 | bytes 9044000 | tf_op jit(solution)/shard_map/early_units/pallas_call | solution.py:161
  111.4 7.0 %late_units.1 = (bf16[768,512]{1,0:T(8,128)(2,1)S(1)}, bf16[768,512]{1,0:T(8,128)(2,1)S(1)}, bf16[768,512]{1,0:T(8,128)(2,1)S(1)}, bf16[768,512]{1,0:T(8,128)(2,...) custom-call(s32[8]{0:T(128)S(1)} %stack.41.blocks_ref, ...), custom_call_target="tpu_custom_call" | custom-call | flops 1811939328 | bytes 15859744 | tf_op jit(solution)/shard_map/late_units/pallas_call | solution.py:161
  124.8 26.3 %collective-permute-done.14 = bf16[768,512]{1,0:T(8,128)(2,1)S(1)} collective-permute-done((bf16[768,512]{1,0:T(8,128)(2,1)S(1)}, bf16[768,512]{1,0:T(8,128)(2,1)S(1)}, u32[]{:S(2)}, u32[]{:S(2)}) %collective-permute-start.14) | collective-permute-done | bytes 786464 | tf_op jit(solution)/shard_map/ppermute | solution.py:15
  152.3 2.7 %collective-permute-start.15 = (bf16[768,512]{1,0:T(8,128)(2,1)}, bf16[768,512]{1,0:T(8,128)(2,1)}, u32[]{:S(2)}, u32[]{:S(2)}) collective-permute-start(bf16[768,512]{1,0:T(8,128)(2,1)} %add_convert_fusion), channel_id=1, source_target_pairs={{0,2},{1,3},{2,0},{3,1},{4,6},{5,7},{6,4},{7,5},{8,10},{9,11},{10,... | collective-permute-start | bytes 2359304 | tf_op jit(solution)/shard_map/ppermute | solution.py:15
  158.3 2.1 reshape.223.query_ref
  160.6 3.2 %copy.42 = bf16[512,8,2,128]{3,1,2,0:T(8,128)(2,1)} copy(bf16[512,8,2,128]{3,2,1,0:T(2,128)(2,1)} %bitcast.51) | data formatting | bytes 4194304
  163.9 4.1 %collective-permute-done.11.x_ref = bf16[768,512]{1,0:T(8,128)(2,1)} collective-permute-done((bf16[768,512]{1,0:T(8,128)(2,1)}, bf16[768,512]{1,0:T(8,128)(2,1)}, u32[]{:S(2)}, u32[]{:S(2)}) %collective-permute-start.11) | collective-permute-done | bytes 786464 | tf_op jit(solution)/shard_map/ppermute | solution.py:15
  168.0 4.7 %collective-permute-done.15.y_ref = bf16[768,512]{1,0:T(8,128)(2,1)} collective-permute-done((bf16[768,512]{1,0:T(8,128)(2,1)}, bf16[768,512]{1,0:T(8,128)(2,1)}, u32[]{:S(2)}, u32[]{:S(2)}) %collective-permute-start.15) | collective-permute-done | bytes 786464 | tf_op jit(solution)/shard_map/ppermute | solution.py:15
  176.7 8.8 %all-to-all-start.2 = ((bf16[32,24,512]{2,1,0:T(8,128)(2,1)}), bf16[32,24,512]{2,1,0:T(8,128)(2,1)}, u32[]{:S(2)}, u32[]{:S(2)}) async-start(bf16[32,24,512]{2,1,0:T(8,128)(2,1)} %bitcast.42), calls=%async_computation.2 | async-start | bytes 1572864 | tf_op jit(solution)/shard_map/all_to_all | solution.py:312
  187.0 3.6 %pad_maximum_fusion.pool_ref = bf16[48,2,128,128]{3,2,1,0:T(8,128)(2,1)} fusion(bf16[32,2,128,128]{3,2,1,0:T(8,128)(2,1)} %all-to-all-done.1.refs_0_, bf16[16,2,128,128]{3,2,1,0:T(8,128)(2,1)S(1)} %bitcast.53), kind=kLoop, calls=%fused_computation.2 | loop fusion | flops 1572864 | bytes 6291456 | tf_op jit(solution)/shard_map/concatenate | solution.py:321
  190.5 10.2 %cached_attention.1 = (f32[32,64,128]{2,1,0:T(8,128)S(1)}, f32[32,64,128]{2,1,0:T(8,128)S(1)}, f32[32,64,128]{2,1,0:T(8,128)S(1)}) custom-call(s32[128]{0:T(128)S(1)} %reshape.222.table_ref, s32[32]{0:T(128)S(1)} %copy-done.24, bf16[32,64,128]{2,1,0:T(8,128)(2,1)S(1)} %copy-done.12, bf16[48,2,128,128]{3,2,1,0:T(8,128)(2,1)} %pad_maximum_fusion.pool_ref), custom_call_target="tpu_custom_call" | custom-call | flops 536870912 | bytes 6816384 | tf_op jit(solution)/shard_map/cached_attention/pallas_call | solution.py:161
  203.7 2.4 reshape.224.refs_1_.top_ref
  206.0 2.4 %reshape.225.refs_2_.total_ref = f32[128,2048]{1,0:T(8,128)} reshape(f32[32,64,128]{2,1,0:T(8,128)} %copy-done.15) | data formatting | bytes 2097152 | tf_op jit(solution)/shard_map/reshape | solution.py:330
  208.4 2.4 reshape.226.refs_3_.mixed_ref
  215.6 2.7 %finish.1 = (f32[128,1024]{1,0:T(8,128)}, bf16[128,1152]{1,0:T(8,128)(2,1)S(1)}) custom-call(s32[1]{0:T(128)} %bitcast.part_ref, bf16[2,256,768]{2,1,0:T(8,128)(2,1)S(1)} %copy-done.11, bf16[768,512]{1,0:T(8,128)(2,1)} %bitcast.24.returned_ref, bf16[128,4096]{1,0:T(8,128)(2,1)S(1)} %copy-done.2, bf16[1,4096]{1,0:T(2,128)(2,1)S(1)} %reshape.220.gain_ref, ...), custom_call_target="tpu_custom_call" | custom-call | bytes 8691716 | tf_op jit(solution)/shard_map/finish/pallas_call | solution.py:161
  218.3 2.8 %collective-permute-start.17 = (bf16[128,1152]{1,0:T(8,128)(2,1)S(1)}, bf16[128,1152]{1,0:T(8,128)(2,1)S(1)}, u32[]{:S(2)}, u32[]{:S(2)}) collective-permute-start(bf16[128,1152]{1,0:T(8,128)(2,1)S(1)} %get-tuple-element.38.own_ref), channel_id=1, source_target_pairs={{0,2},{1,3},{2,0},{3,1},{4,6},{5,7},{6,4},{7,5},{8,10},{9,11},{10,... | collective-permute-start | bytes 884744 | tf_op jit(solution)/shard_map/ppermute | solution.py:15
  221.1 2.2 collective-permute-start.16
  223.3 2.8 %collective-permute-done.17.y_ref = bf16[128,1152]{1,0:T(8,128)(2,1)S(1)} collective-permute-done((bf16[128,1152]{1,0:T(8,128)(2,1)S(1)}, bf16[128,1152]{1,0:T(8,128)(2,1)S(1)}, u32[]{:S(2)}, u32[]{:S(2)}) %collective-permute-start.17) | collective-permute-done | bytes 294944 | tf_op jit(solution)/shard_map/ppermute | solution.py:15
  226.1 3.1 %collective-permute-start.18 = (bf16[128,1152]{1,0:T(8,128)(2,1)S(1)}, bf16[128,1152]{1,0:T(8,128)(2,1)S(1)}, u32[]{:S(2)}, u32[]{:S(2)}) collective-permute-start(bf16[128,1152]{1,0:T(8,128)(2,1)S(1)} %collective-permute-done.17.y_ref), channel_id=1, source_target_pairs={{0,1},{1,0},{2,3},{3,2},{4,5},{5,4},{6,7},{7,6},{8,9},{9,8},{10,11... | collective-permute-start | bytes 884744 | tf_op jit(solution)/shard_map/ppermute | solution.py:15
  230.4 6.6 %last_step.1 = (bf16[128,256]{1,0:T(8,128)(2,1)S(1)}, bf16[128,2048]{1,0:T(8,128)(2,1)}) custom-call(s32[1]{0:T(128)} %bitcast.part_ref, bf16[128,1152]{1,0:T(8,128)(2,1)S(1)} %get-tuple-element.38.own_ref, bf16[128,1152]{1,0:T(8,128)(2,1)S(1)} %collective-permute-done.16.core_ref, bf16[128,1152]{1,0:T(8,128)(2,1)S(1)} %collective-permute-done.17.y_ref, ...), custom_call_target="tpu_custom_call" | custom-call | bytes 7536644 | tf_op jit(solution)/shard_map/last_step/pallas_call | solution.py:161
  (123 shorter events, 38.2 us)
Async XLA Ops:
  0.6 16.3 %copy-start = (bf16[32,1,2,128,128]{4,3,2,1,0:T(8,128)(2,1)S(1)}, bf16[32,1,2,128,128]{4,3,2,1,0:T(8,128)(2,1)}, u32[]{:S(2)}) copy-start(bf16[32,1,2,128,128]{4,3,2,1,0:T(8,128)(2,1)} %param.26) | copy-start | bytes 6291460
  0.6 16.2 %copy-start.30 = (s32[1,32]{1,0:T(1,128)S(1)}, s32[1,32]{1,0:T(1,128)}, u32[]{:S(2)}) copy-start(s32[1,32]{1,0:T(1,128)} %param.27) | copy-start | bytes 388
  5.0 40.6 %all-to-all-start = ((bf16[32,24,512]{2,1,0:T(8,128)(2,1)}), bf16[32,24,512]{2,1,0:T(8,128)(2,1)S(1)}, u32[]{:S(2)}, u32[]{:S(2)}) async-start(bf16[32,24,512]{2,1,0:T(8,128)(2,1)} %copy-done.19), calls=%async_computation | async-start | bytes 1572864 | tf_op jit(solution)/shard_map/all_to_all | solution.py:239
  21.8 23.8 %collective-permute-start = (bf16[16,2,128,128]{3,2,1,0:T(8,128)(2,1)S(1)}, bf16[16,2,128,128]{3,2,1,0:T(8,128)(2,1)}, u32[]{:S(2)}, u32[]{:S(2)}) collective-permute-start(bf16[16,2,128,128]{3,2,1,0:T(8,128)(2,1)S(1)} %get-tuple-element.44), channel_id=1, source_target_pairs={{0,128},{128,0},{1,129},{129,1},{2,130},{130,2},{3,131},{131,3},{4... | collective-permute-start | bytes 3145736 | tf_op jit(solution)/shard_map/ppermute | solution.py:15
  46.5 20.3 %copy-start.9 = (bf16[768,512]{1,0:T(8,128)(2,1)S(1)}, bf16[768,512]{1,0:T(8,128)(2,1)}, u32[]{:S(2)}) copy-start(bf16[768,512]{1,0:T(8,128)(2,1)} %held_until.2.refs_0_) | copy-start | bytes 2359300
  46.5 19.0 %collective-permute-start.1 = (bf16[768,512]{1,0:T(8,128)(2,1)}, bf16[768,512]{1,0:T(8,128)(2,1)}, u32[]{:S(2)}, u32[]{:S(2)}) collective-permute-start(bf16[768,512]{1,0:T(8,128)(2,1)} %held_until.2.refs_0_), channel_id=1, source_target_pairs={{0,2},{1,3},{2,0},{3,1},{4,6},{5,7},{6,4},{7,5},{8,10},{9,11},{10,... | collective-permute-start | bytes 2359304 | tf_op jit(solution)/shard_map/ppermute | solution.py:15
  65.5 24.9 %collective-permute-start.8 = (bf16[16,2,128,128]{3,2,1,0:T(8,128)(2,1)}, bf16[16,2,128,128]{3,2,1,0:T(8,128)(2,1)S(1)}, u32[]{:S(2)}, u32[]{:S(2)}) collective-permute-start(bf16[16,2,128,128]{3,2,1,0:T(8,128)(2,1)} %held_until.3), channel_id=1, source_target_pairs={{0,128},{128,0},{1,129},{129,1},{2,130},{130,2},{3,131},{131,3},{4... | collective-permute-start | bytes 3145736 | tf_op jit(solution)/shard_map/ppermute | solution.py:15
  66.7 16.1 %collective-permute-start.4 = (bf16[768,512]{1,0:T(8,128)(2,1)S(1)}, bf16[768,512]{1,0:T(8,128)(2,1)}, u32[]{:S(2)}, u32[]{:S(2)}) collective-permute-start(bf16[768,512]{1,0:T(8,128)(2,1)S(1)} %copy-done.9), channel_id=1, source_target_pairs={{0,4},{4,0},{8,12},{12,8},{16,20},{20,16},{24,28},{28,24},{32,36},... | collective-permute-start | bytes 2359304 | tf_op jit(solution)/shard_map/ppermute | solution.py:15
  67.4 33.1 %collective-permute-start.2 = (bf16[768,512]{1,0:T(8,128)(2,1)}, bf16[768,512]{1,0:T(8,128)(2,1)}, u32[]{:S(2)}, u32[]{:S(2)}) collective-permute-start(bf16[768,512]{1,0:T(8,128)(2,1)} %collective-permute-done.1.refs_2_.other_ref), channel_id=1, source_target_pairs={{0,4},{4,0},{8,12},{12,8},{16,20},{20,16},{24,28},{28,24},{32,36},... | collective-permute-start | bytes 2359304 | tf_op jit(solution)/shard_map/ppermute | solution.py:15
  70.6 33.3 %collective-permute-start.5 = (bf16[768,512]{1,0:T(8,128)(2,1)S(1)}, bf16[768,512]{1,0:T(8,128)(2,1)}, u32[]{:S(2)}, u32[]{:S(2)}) collective-permute-start(bf16[768,512]{1,0:T(8,128)(2,1)S(1)} %copy-done.9), channel_id=1, source_target_pairs={{0,1},{1,0},{2,3},{3,2},{4,5},{5,4},{6,7},{7,6},{8,9},{9,8},{10,11... | collective-permute-start | bytes 2359304 | tf_op jit(solution)/shard_map/ppermute | solution.py:15
  74.2 29.7 %collective-permute-start.7 = (bf16[768,512]{1,0:T(8,128)(2,1)}, bf16[768,512]{1,0:T(8,128)(2,1)}, u32[]{:S(2)}, u32[]{:S(2)}) collective-permute-start(bf16[768,512]{1,0:T(8,128)(2,1)} %collective-permute-done.1.refs_2_.other_ref), channel_id=1, source_target_pairs={{0,1},{1,0},{2,3},{3,2},{4,5},{5,4},{6,7},{7,6},{8,9},{9,8},{10,11... | collective-permute-start | bytes 2359304 | tf_op jit(solution)/shard_map/ppermute | solution.py:15
  82.8 21.1 %collective-permute-start.6 = (bf16[768,512]{1,0:T(8,128)(2,1)}, bf16[768,512]{1,0:T(8,128)(2,1)}, u32[]{:S(2)}, u32[]{:S(2)}) collective-permute-start(bf16[768,512]{1,0:T(8,128)(2,1)} %collective-permute-done.4.refs_1_), channel_id=1, source_target_pairs={{0,1},{1,0},{2,3},{3,2},{4,5},{5,4},{6,7},{7,6},{8,9},{9,8},{10,11... | collective-permute-start | bytes 2359304 | tf_op jit(solution)/shard_map/ppermute | solution.py:15
  91.4 81.3 %all-to-all-start.1 = ((bf16[32,2,128,128]{3,2,1,0:T(8,128)(2,1)}), bf16[32,2,128,128]{3,2,1,0:T(8,128)(2,1)}, u32[]{:S(2)}, u32[]{:S(2)}) async-start(bf16[32,2,128,128]{3,2,1,0:T(8,128)(2,1)} %constant_dynamic-update-slice_fusion.refs_0_), calls=%async_computation.1 | async-start | bytes 4194304 | tf_op jit(solution)/shard_map/all_to_all | solution.py:270
  100.5 10.9 %collective-permute-start.3 = (bf16[768,512]{1,0:T(8,128)(2,1)}, bf16[768,512]{1,0:T(8,128)(2,1)}, u32[]{:S(2)}, u32[]{:S(2)}) collective-permute-start(bf16[768,512]{1,0:T(8,128)(2,1)} %collective-permute-done.2.mine_ref), channel_id=1, source_target_pairs={{0,1},{1,0},{2,3},{3,2},{4,5},{5,4},{6,7},{7,6},{8,9},{9,8},{10,11... | collective-permute-start | bytes 2359304 | tf_op jit(solution)/shard_map/ppermute | solution.py:15
  118.4 6.3 %copy-start.20 = (bf16[768,512]{1,0:T(8,128)(2,1)}, bf16[768,512]{1,0:T(8,128)(2,1)S(1)}, u32[]{:S(2)}) copy-start(bf16[768,512]{1,0:T(8,128)(2,1)S(1)} %get-tuple-element.26.mine_ref) | copy-start | bytes 2359300
  118.4 4.7 %copy-start.23 = (s32[128,2]{0,1:T(2,128)S(1)}, s32[128,2]{0,1:T(2,128)}, u32[]{:S(2)}) copy-start(s32[128,2]{0,1:T(2,128)} %param.18) | copy-start | bytes 3076
  118.4 2.6 %collective-permute-start.13 = (bf16[768,512]{1,0:T(8,128)(2,1)}, bf16[768,512]{1,0:T(8,128)(2,1)S(1)}, u32[]{:S(2)}, u32[]{:S(2)}) collective-permute-start(bf16[768,512]{1,0:T(8,128)(2,1)} %get-tuple-element.33), channel_id=1, source_target_pairs={{0,1},{1,0},{2,3},{3,2},{4,5},{5,4},{6,7},{7,6},{8,9},{9,8},{10,11... | collective-permute-start | bytes 2359304 | tf_op jit(solution)/shard_map/ppermute | solution.py:15
  118.5 5.2 %collective-permute-start.10 = (bf16[768,512]{1,0:T(8,128)(2,1)S(1)}, bf16[768,512]{1,0:T(8,128)(2,1)S(1)}, u32[]{:S(2)}, u32[]{:S(2)}) collective-permute-start(bf16[768,512]{1,0:T(8,128)(2,1)S(1)} %get-tuple-element.29), channel_id=1, source_target_pairs={{0,1},{1,0},{2,3},{3,2},{4,5},{5,4},{6,7},{7,6},{8,9},{9,8},{10,11... | collective-permute-start | bytes 2359304 | tf_op jit(solution)/shard_map/ppermute | solution.py:15
  119.0 5.8 %collective-permute-start.12 = (bf16[768,512]{1,0:T(8,128)(2,1)S(1)}, bf16[768,512]{1,0:T(8,128)(2,1)S(1)}, u32[]{:S(2)}, u32[]{:S(2)}) collective-permute-start(bf16[768,512]{1,0:T(8,128)(2,1)S(1)} %get-tuple-element.31), channel_id=1, source_target_pairs={{0,1},{1,0},{2,3},{3,2},{4,5},{5,4},{6,7},{7,6},{8,9},{9,8},{10,11... | collective-permute-start | bytes 2359304 | tf_op jit(solution)/shard_map/ppermute | solution.py:15
  121.2 29.9 %collective-permute-start.14 = (bf16[768,512]{1,0:T(8,128)(2,1)S(1)}, bf16[768,512]{1,0:T(8,128)(2,1)S(1)}, u32[]{:S(2)}, u32[]{:S(2)}) collective-permute-start(bf16[768,512]{1,0:T(8,128)(2,1)S(1)} %add_convert_fusion.1), channel_id=1, source_target_pairs={{0,4},{4,0},{8,12},{12,8},{16,20},{20,16},{24,28},{28,24},{32,36},... | collective-permute-start | bytes 2359304 | tf_op jit(solution)/shard_map/ppermute | solution.py:15
  123.1 40.7 %collective-permute-start.9 = (bf16[768,512]{1,0:T(8,128)(2,1)}, bf16[768,512]{1,0:T(8,128)(2,1)}, u32[]{:S(2)}, u32[]{:S(2)}) collective-permute-start(bf16[768,512]{1,0:T(8,128)(2,1)} %get-tuple-element.27), channel_id=1, source_target_pairs={{0,1},{1,0},{2,3},{3,2},{4,5},{5,4},{6,7},{7,6},{8,9},{9,8},{10,11... | collective-permute-start | bytes 2359304 | tf_op jit(solution)/shard_map/ppermute | solution.py:15
  124.7 30.3 %copy-start.2 = (bf16[128,4096]{1,0:T(8,128)(2,1)S(1)}, bf16[128,4096]{1,0:T(8,128)(2,1)}, u32[]{:S(2)}) copy-start(bf16[128,4096]{1,0:T(8,128)(2,1)} %hidden_ref.3) | copy-start | bytes 3145732
  124.7 43.2 %collective-permute-start.11 = (bf16[768,512]{1,0:T(8,128)(2,1)}, bf16[768,512]{1,0:T(8,128)(2,1)}, u32[]{:S(2)}, u32[]{:S(2)}) collective-permute-start(bf16[768,512]{1,0:T(8,128)(2,1)} %add_convert_fusion.2), channel_id=1, source_target_pairs={{0,4},{4,0},{8,12},{12,8},{16,20},{20,16},{24,28},{28,24},{32,36},... | collective-permute-start | bytes 2359304 | tf_op jit(solution)/shard_map/ppermute | solution.py:15
  151.1 4.5 %copy-start.29 = (bf16[4096,16]{0,1:T(8,128)(2,1)S(1)}, bf16[4096,16]{0,1:T(8,128)(2,1)}, u32[]{:S(2)}) copy-start(bf16[4096,16]{0,1:T(8,128)(2,1)} %param.17) | copy-start | bytes 393220
  152.3 20.4 %collective-permute-start.15 = (bf16[768,512]{1,0:T(8,128)(2,1)}, bf16[768,512]{1,0:T(8,128)(2,1)}, u32[]{:S(2)}, u32[]{:S(2)}) collective-permute-start(bf16[768,512]{1,0:T(8,128)(2,1)} %add_convert_fusion), channel_id=1, source_target_pairs={{0,2},{1,3},{2,0},{3,1},{4,6},{5,7},{6,4},{7,5},{8,10},{9,11},{10,... | collective-permute-start | bytes 2359304 | tf_op jit(solution)/shard_map/ppermute | solution.py:15
  176.7 34.1 %all-to-all-start.2 = ((bf16[32,24,512]{2,1,0:T(8,128)(2,1)}), bf16[32,24,512]{2,1,0:T(8,128)(2,1)}, u32[]{:S(2)}, u32[]{:S(2)}) async-start(bf16[32,24,512]{2,1,0:T(8,128)(2,1)} %bitcast.42), calls=%async_computation.2 | async-start | bytes 1572864 | tf_op jit(solution)/shard_map/all_to_all | solution.py:312
  215.6 14.8 %copy-start.5 = (f32[128,2048]{1,0:T(8,128)S(1)}, f32[128,2048]{1,0:T(8,128)}, u32[]{:S(2)}) copy-start(f32[128,2048]{1,0:T(8,128)} %reshape.225.refs_2_.total_ref) | copy-start | bytes 3145732
  215.6 14.8 %copy-start.7 = (f32[128,2048]{1,0:T(8,128)S(1)}, f32[128,2048]{1,0:T(8,128)}, u32[]{:S(2)}) copy-start(f32[128,2048]{1,0:T(8,128)} %reshape.226.refs_3_.mixed_ref) | copy-start | bytes 3145732
  215.6 14.8 %copy-start.13 = (bf16[128,2048]{1,0:T(8,128)(2,1)S(1)}, bf16[128,2048]{1,0:T(8,128)(2,1)}, u32[]{:S(2)}) copy-start(bf16[128,2048]{1,0:T(8,128)(2,1)} %query_ref.1) | copy-start | bytes 1572868
  218.3 7.8 %collective-permute-start.17 = (bf16[128,1152]{1,0:T(8,128)(2,1)S(1)}, bf16[128,1152]{1,0:T(8,128)(2,1)S(1)}, u32[]{:S(2)}, u32[]{:S(2)}) collective-permute-start(bf16[128,1152]{1,0:T(8,128)(2,1)S(1)} %get-tuple-element.38.own_ref), channel_id=1, source_target_pairs={{0,2},{1,3},{2,0},{3,1},{4,6},{5,7},{6,4},{7,5},{8,10},{9,11},{10,... | collective-permute-start | bytes 884744 | tf_op jit(solution)/shard_map/ppermute | solution.py:15
  221.1 8.1 %collective-permute-start.16 = (bf16[128,1152]{1,0:T(8,128)(2,1)S(1)}, bf16[128,1152]{1,0:T(8,128)(2,1)S(1)}, u32[]{:S(2)}, u32[]{:S(2)}) collective-permute-start(bf16[128,1152]{1,0:T(8,128)(2,1)S(1)} %get-tuple-element.38.own_ref), channel_id=1, source_target_pairs={{0,1},{1,0},{2,3},{3,2},{4,5},{5,4},{6,7},{7,6},{8,9},{9,8},{10,11... | collective-permute-start | bytes 884744 | tf_op jit(solution)/shard_map/ppermute | solution.py:15
  226.1 4.3 %collective-permute-start.18 = (bf16[128,1152]{1,0:T(8,128)(2,1)S(1)}, bf16[128,1152]{1,0:T(8,128)(2,1)S(1)}, u32[]{:S(2)}, u32[]{:S(2)}) collective-permute-start(bf16[128,1152]{1,0:T(8,128)(2,1)S(1)} %collective-permute-done.17.y_ref), channel_id=1, source_target_pairs={{0,1},{1,0},{2,3},{3,2},{4,5},{5,4},{6,7},{7,6},{8,9},{9,8},{10,11... | collective-permute-start | bytes 884744 | tf_op jit(solution)/shard_map/ppermute | solution.py:15
  (21 other events, 35.5 us)

commit v2 on v1

--- a/solution.py
+++ b/solution.py
@@ -87,19 +87,19 @@
     refs[-1][...] = total.astype(jnp.bfloat16)
 
 
-def held_until(x, other):
-    def kernel(x_ref, other_ref, out_ref):
+def held_until(x, *others):
+    def kernel(*refs):
         pass
 
     any_space = pl.BlockSpec(memory_space=pl.ANY)
     return pl.pallas_call(
         kernel,
         out_shape=jax.ShapeDtypeStruct(x.shape, x.dtype),
-        in_specs=[any_space, any_space],
+        in_specs=[any_space] * (1 + len(others)),
         out_specs=any_space,
         input_output_aliases={0: 0},
         name="held_until",
-    )(x, other)
+    )(x, *others)
 
 
 def finish(part_ref, combine_ref, returned_ref, hidden_ref, gain_ref, *refs):
@@ -239,10 +239,9 @@
     landed = lax.all_to_all(packed, "grp", split_axis=0, concat_axis=0, tiled=True)
     landed = landed.reshape(total_slots, eighth)
 
-    ordered = prompt_cache[:, 0].at[handoff[0]].get(mode="promise_in_bounds")
-    middle = peer_count // 2
-    crossed = swapped(ordered[:middle], "role", 0)
-    landed = held_until(landed, crossed)
+    crossed = swapped(prompt_cache[:, 0], "role", 0)
+    order = swapped(handoff, "role", 0)
+    landed = held_until(landed, crossed, order)
 
     hidden = hidden_in.astype(f32)
     scale_in = inverse_rms(jnp.sum(hidden * hidden, axis=1, keepdims=True), model_width)
@@ -259,15 +258,15 @@
     target_half = targets // capacity % 2
     halves = jnp.stack([jnp.where(target_half == i, both_terms, jnp.zeros((), bf16)) for i in range(2)])
 
-    from_x = swapped(landed, "grp", 0)
     from_y = swapped(landed, "tp", 1)
+    from_x = held_until(swapped(landed, "grp", 0), from_y)
     mine = (landed, from_x, from_y)
     theirs = tuple(swapped(x, "tp", 0) for x in mine)
-    last_mine = swapped(from_y, "grp", 0)
+    last_mine = swapped(from_x, "tp", 1)
     last_theirs = swapped(last_mine, "tp", 0)
 
-    crossed = jnp.concatenate([crossed, swapped(held_until(ordered[middle:], from_y), "role", 0)], axis=0)
-    arrived = lax.all_to_all(crossed, "grp", split_axis=0, concat_axis=0, tiled=True)
+    ordered = held_until(crossed.at[order[0]].get(mode="promise_in_bounds"), from_x)
+    arrived = lax.all_to_all(ordered, "grp", split_axis=0, concat_axis=0, tiled=True)
 
     blocks = jnp.stack(
         [
@@ -289,29 +288,12 @@
     sums = call(
         late_units,
         (shape((total_slots, eighth), bf16),) * 8,
-        (blocks, last_mine, last_theirs, *sums, gate_own, up_own, down_weight[0], crossed),
+        (blocks, last_mine, last_theirs, *sums, gate_own, up_own, down_weight[0], ordered),
         smem=1,
         away=1,
         name="late_units",
         flops=3 * total_slots * model_width * unit_count,
     )
-
-    def both_cores(i):
-        return sums[i].astype(f32) + swapped(sums[4 + i], "tp", 0).astype(f32)
-
-    far = swapped(both_cores(3).astype(bf16), "grp", 0)
-    sum_y = swapped((both_cores(2) + far.astype(f32)).astype(bf16), "tp", 1)
-    sum_x = swapped(both_cores(1).astype(bf16), "grp", 0)
-    summed = call(
-        join,
-        shape((total_slots, eighth), bf16),
-        (sums[0], swapped(sums[4], "tp", 0), sum_x, sum_y, arrived),
-        away=1,
-        name="join",
-    )
-    returned = lax.all_to_all(
-        summed.reshape(peer_count, capacity, eighth), "grp", split_axis=0, concat_axis=0, tiled=True
-    ).reshape(total_slots, eighth)
 
     requests, max_blocks = block_table.shape
     head_dim = kv_weight.shape[2]
@@ -327,6 +309,23 @@
         name="cached_attention",
         flops=4 * requests * draft_count * per_kv * head_dim * max_blocks * decode_cache.shape[3],
     )
+
+    def both_cores(i):
+        return sums[i].astype(f32) + swapped(sums[4 + i], "tp", 0).astype(f32)
+
+    far = swapped(both_cores(3).astype(bf16), "tp", 1)
+    sum_x = swapped((both_cores(1) + far.astype(f32)).astype(bf16), "grp", 0)
+    sum_y = swapped(held_until(both_cores(2).astype(bf16), far), "tp", 1)
+    summed = call(
+        join,
+        shape((total_slots, eighth), bf16),
+        (sums[0], swapped(sums[4], "tp", 0), sum_x, sum_y, *stats),
+        away=3,
+        name="join",
+    )
+    returned = lax.all_to_all(
+        summed.reshape(peer_count, capacity, eighth), "grp", split_axis=0, concat_axis=0, tiled=True
+    ).reshape(total_slots, eighth)
     stats = tuple(x.reshape(token_rows, per_kv * head_dim) for x in stats)
     flat_weight = kv_weight.reshape(model_width, 2 * head_dim)
     residual_out, scaled = call(

time: 239 us -> 220 us (0.921)
  local copies, waits for them, and re-layouts: 40.2 us -> 25.8 us
  starting transfers between devices: 65.5 us -> 58.1 us
    ppermute x19, waiting for transfers between devices: 88.1 us -> 72.9 us  [swapped(): lax.ppermute(x, axis, [(i, i ^ 1 << bit) for i in range(lax.axis_size(axi...]
    all_to_all x1, waiting for transfers between devices: 0.01 us -> 15.2 us  [local(): lax.all_to_all(summed.reshape(peer_count, capacity, eighth), 'grp', split...]
    ppermute x19, starting transfers between devices: 35.7 us -> 27.2 us  [swapped(): lax.ppermute(x, axis, [(i, i ^ 1 << bit) for i in range(lax.axis_size(axi...]
    unnamed x65 -> x64, local copies, waits for them, and re-layouts: 20.9 us -> 13.9 us
    reshape x3, local copies, waits for them, and re-layouts: 7.11 us -> 3.9 us  [local(): stats = tuple((x.reshape(token_rows, per_kv * head_dim) for x in stats))]
    slice x1 -> x0, local copies, waits for them, and re-layouts: 2.71 us -> none  [local(): ordered[middle:]]
  transfers between devices with their start and end apart: 22 -> 22, of which waited for: 9 -> 11; matrix products, arithmetic and copies ran while one was open for 13% -> 11% of each run, Pallas kernels for 10% -> 11%
where the time goes in v2:
time: 220 us; the launch traced here: 219 us
  waiting for transfers between devices  88.1 us (40%)
  starting transfers between devices  58.1 us (26%)
  Pallas kernels  36.1 us (16%)
  local copies, waits for them, and re-layouts  25.8 us (12%)
  other arithmetic  9.14 us (4%)
    ppermute x19, waiting for transfers between devices, swapped(): lax.ppermute(x, axis, [(i, i ^ 1 << bit) for i in range(lax.axis_size(axi...  72.9 us
    pallas_call x7, Pallas kernels, call(): pl.pallas_call(kernel, out_shape=out_shape, in_specs=[pl.BlockSpec(memory...  36.1 us
    ppermute x19, starting transfers between devices, swapped(): lax.ppermute(x, axis, [(i, i ^ 1 << bit) for i in range(lax.axis_size(axi...  27.2 us
    all_to_all x1, waiting for transfers between devices, local(): lax.all_to_all(summed.reshape(peer_count, capacity, eighth), 'grp', split...  15.2 us
    unnamed x64, local copies, waits for them, and re-layouts  13.9 us
    all_to_all x1, starting transfers between devices, local(): lax.all_to_all(ordered, 'grp', split_axis=0, concat_axis=0, tiled=True)  11.3 us
    all_to_all x1, starting transfers between devices, local(): lax.all_to_all(packed, 'grp', split_axis=0, concat_axis=0, tiled=True)  11 us
    all_to_all x1, starting transfers between devices, local(): lax.all_to_all(summed.reshape(peer_count, capacity, eighth), 'grp', split...  8.6 us
  transfers between devices with their start and end apart: 22, of which 11 were waited for; matrix products, arithmetic and copies ran while one was open for 11% of the time, Pallas kernels for 11%

profile of v2, /device:TPU:1, one launch (start us, length us, event | category | flops | bytes accessed | tf_op | source)
XLA Modules:
  0.0 218.7 jit_solution(15187456200444133542)
XLA Ops:
  0.7 2.2 %collective-permute-start = (bf16[32,2,128,128]{3,2,1,0:T(8,128)(2,1)}, bf16[32,2,128,128]{3,2,1,0:T(8,128)(2,1)S(1)}, u32[]{:S(2)}, u32[]{:S(2)}) collective-permute-start(bf16[32,2,128,128]{3,2,1,0:T(8,128)(2,1)} %bitcast.52), channel_id=1, source_target_pairs={{0,128},{128,0},{1,129},{129,1},{2,130},{130,2},{3,131},{131,3},{4... | collective-permute-start | bytes 6291464 | tf_op jit(solution)/shard_map/ppermute | solution.py:15
  5.5 1.5 prepare.1
  7.0 11.0 %all-to-all-start = ((bf16[32,24,512]{2,1,0:T(8,128)(2,1)}), bf16[32,24,512]{2,1,0:T(8,128)(2,1)S(1)}, u32[]{:S(2)}, u32[]{:S(2)}) async-start(bf16[32,24,512]{2,1,0:T(8,128)(2,1)} %get-tuple-element.23), calls=%async_computation | async-start | bytes 1572864 | tf_op jit(solution)/shard_map/all_to_all | solution.py:239
  18.3 29.0 %collective-permute-done.1.refs_2_ = s32[1,32]{1,0:T(1,128)S(1)} collective-permute-done((s32[1,32]{1,0:T(1,128)S(1)}, s32[1,32]{1,0:T(1,128)S(1)}, u32[]{:S(2)}, u32[]{:S(2)}) %collective-permute-start.1) | collective-permute-done | bytes 160 | tf_op jit(solution)/shard_map/ppermute | solution.py:15
  48.9 3.9 %collective-permute-start.3 = (bf16[768,512]{1,0:T(8,128)(2,1)}, bf16[768,512]{1,0:T(8,128)(2,1)S(1)}, u32[]{:S(2)}, u32[]{:S(2)}) collective-permute-start(bf16[768,512]{1,0:T(8,128)(2,1)} %held_until.4.refs_0_), channel_id=1, source_target_pairs={{0,2},{1,3},{2,0},{3,1},{4,6},{5,7},{6,4},{7,5},{8,10},{9,11},{10,... | collective-permute-start | bytes 2359304 | tf_op jit(solution)/shard_map/ppermute | solution.py:15
  54.0 15.1 %collective-permute-done.3.refs_1_.refs_2_ = bf16[768,512]{1,0:T(8,128)(2,1)S(1)} collective-permute-done((bf16[768,512]{1,0:T(8,128)(2,1)}, bf16[768,512]{1,0:T(8,128)(2,1)S(1)}, u32[]{:S(2)}, u32[]{:S(2)}) %collective-permute-start.3) | collective-permute-done | bytes 786464 | tf_op jit(solution)/shard_map/ppermute | solution.py:15
  71.1 2.7 %collective-permute-start.4 = (bf16[768,512]{1,0:T(8,128)(2,1)}, bf16[768,512]{1,0:T(8,128)(2,1)}, u32[]{:S(2)}, u32[]{:S(2)}) collective-permute-start(bf16[768,512]{1,0:T(8,128)(2,1)} %held_until.5.refs_1_), channel_id=1, source_target_pairs={{0,2},{1,3},{2,0},{3,1},{4,6},{5,7},{6,4},{7,5},{8,10},{9,11},{10,... | collective-permute-start | bytes 2359304 | tf_op jit(solution)/shard_map/ppermute | solution.py:15
  73.8 3.8 %gather_fusion = bf16[32,2,128,128]{3,2,1,0:T(8,128)(2,1)} fusion(bf16[32,2,128,128]{3,2,1,0:T(8,128)(2,1)} %copy-done.22, s32[1024]{0:T(1024)S(1)} %pad_clamp_fusion), kind=kCustom, calls=%fused_computation | custom fusion | bytes 4194432 | tf_op jit(solution)/shard_map/gather | solution.py:268
  77.6 11.3 %all-to-all-start.1 = ((bf16[32,2,128,128]{3,2,1,0:T(8,128)(2,1)}), bf16[32,2,128,128]{3,2,1,0:T(8,128)(2,1)}, u32[]{:S(2)}, u32[]{:S(2)}) async-start(bf16[32,2,128,128]{3,2,1,0:T(8,128)(2,1)} %held_until.6.refs_0_), calls=%async_computation.1 | async-start | bytes 4194304 | tf_op jit(solution)/shard_map/all_to_all | solution.py:269
  88.9 3.2 %collective-permute-start.6 = (bf16[768,512]{1,0:T(8,128)(2,1)S(1)}, bf16[768,512]{1,0:T(8,128)(2,1)S(1)}, u32[]{:S(2)}, u32[]{:S(2)}) collective-permute-start(bf16[768,512]{1,0:T(8,128)(2,1)S(1)} %copy-done.7), channel_id=1, source_target_pairs={{0,1},{1,0},{2,3},{3,2},{4,5},{5,4},{6,7},{7,6},{8,9},{9,8},{10,11... | collective-permute-start | bytes 2359304 | tf_op jit(solution)/shard_map/ppermute | solution.py:15
  94.0 2.3 %collective-permute-done.7.refs_4_ = bf16[768,512]{1,0:T(8,128)(2,1)} collective-permute-done((bf16[768,512]{1,0:T(8,128)(2,1)S(1)}, bf16[768,512]{1,0:T(8,128)(2,1)}, u32[]{:S(2)}, u32[]{:S(2)}) %collective-permute-start.7) | collective-permute-done | bytes 786464 | tf_op jit(solution)/shard_map/ppermute | solution.py:15
  97.5 5.0 %early_units.1 = (f32[768,192]{1,0:T(8,128)S(1)}, f32[768,192]{1,0:T(8,128)S(1)}) custom-call(s32[8]{0:T(128)S(1)} %stack.41.blocks_ref, bf16[768,512]{1,0:T(8,128)(2,1)S(1)} %copy-done.7, bf16[768,512]{1,0:T(8,128)(2,1)S(1)} %copy-done.5, bf16[768,512]{1,0:T(8,128)(2,1)S(1)} %copy-done.12, bf16[768,512]{1,0:T(8,128)(2,1)S(1)} %collective-permute-done.6.refs_3_, ...), custom_call_target="tpu_custom_call" | custom-call | flops 1811939328 | bytes 9044000 | tf_op jit(solution)/shard_map/early_units/pallas_call | solution.py:161
  104.3 7.0 %late_units.1 = (bf16[768,512]{1,0:T(8,128)(2,1)S(1)}, bf16[768,512]{1,0:T(8,128)(2,1)S(1)}, bf16[768,512]{1,0:T(8,128)(2,1)S(1)}, bf16[768,512]{1,0:T(8,128)(2,...) custom-call(s32[8]{0:T(128)S(1)} %stack.41.blocks_ref, ...), custom_call_target="tpu_custom_call" | custom-call | flops 1811939328 | bytes 15859744 | tf_op jit(solution)/shard_map/late_units/pallas_call | solution.py:161
  112.0 1.8 collective-permute-done.11
  116.0 18.5 %collective-permute-done.12.refs_1_ = bf16[768,512]{1,0:T(8,128)(2,1)S(1)} collective-permute-done((bf16[768,512]{1,0:T(8,128)(2,1)S(1)}, bf16[768,512]{1,0:T(8,128)(2,1)S(1)}, u32[]{:S(2)}, u32[]{:S(2)}) %collective-permute-start.12) | collective-permute-done | bytes 786464 | tf_op jit(solution)/shard_map/ppermute | solution.py:15
  135.7 2.6 %add_convert_fusion.1 = bf16[768,512]{1,0:T(8,128)(2,1)} fusion(bf16[768,512]{1,0:T(8,128)(2,1)} %copy-done.23, bf16[768,512]{1,0:T(8,128)(2,1)} %collective-permute-done.10, bf16[768,512]{1,0:T(8,128)(2,1)S(1)} %get-tuple-element.28), kind=kLoop, calls=%fused_computation.10 | loop fusion | flops 2359296 | bytes 3145728 | tf_op jit(solution)/shard_map/convert_element_type | solution.py:317
  138.4 1.4 collective-permute-start.13
  141.3 2.0 gather_fusion.1
  143.5 3.3 %copy.44 = bf16[512,8,2,128]{3,1,2,0:T(8,128)(2,1)} copy(bf16[512,8,2,128]{3,2,1,0:T(2,128)(2,1)} %bitcast.49) | data formatting | bytes 4194304
  146.9 3.5 %pad_maximum_fusion.pool_ref = bf16[48,2,128,128]{3,2,1,0:T(8,128)(2,1)} fusion(bf16[32,2,128,128]{3,2,1,0:T(8,128)(2,1)} %all-to-all-done.1, bf16[16,2,128,128]{3,2,1,0:T(8,128)(2,1)S(1)} %bitcast.51), kind=kLoop, calls=%fused_computation.2 | loop fusion | flops 1572864 | bytes 6291456 | tf_op jit(solution)/shard_map/concatenate | solution.py:303
  150.4 10.3 %cached_attention.1 = (f32[32,64,128]{2,1,0:T(8,128)S(1)}, f32[32,64,128]{2,1,0:T(8,128)S(1)}, f32[32,64,128]{2,1,0:T(8,128)S(1)}) custom-call(s32[128]{0:T(128)S(1)} %reshape.218.table_ref, s32[32]{0:T(128)S(1)} %copy-done.21, bf16[32,64,128]{2,1,0:T(8,128)(2,1)S(1)} %reshape.219.query_ref, bf16[48,2,128,128]{3,2,1,0:T(8,128)(2,1)} %pad_maximum_fusion.pool_ref), custom_call_target="tpu_custom_call" | custom-call | flops 536870912 | bytes 6816384 | tf_op jit(solution)/shard_map/cached_attention/pallas_call | solution.py:161
  161.7 3.2 %join.1 = bf16[768,512]{1,0:T(8,128)(2,1)} custom-call(bf16[768,512]{1,0:T(8,128)(2,1)S(1)} %copy-done.16, bf16[768,512]{1,0:T(8,128)(2,1)} %collective-permute-done.9.theirs_ref, bf16[768,512]{1,0:T(8,128)(2,1)} %collective-permute-done.13.x_ref, bf16[768,512]{1,0:T(8,128)(2,1)} %collective-permute-done.15.y_ref, ...), custom_call_target="tpu_custom_call" | custom-call | bytes 7077888 | tf_op jit(solution)/shard_map/join/pallas_call | solution.py:161
  164.9 8.6 %all-to-all-start.2 = ((bf16[32,24,512]{2,1,0:T(8,128)(2,1)}), bf16[32,24,512]{2,1,0:T(8,128)(2,1)}, u32[]{:S(2)}, u32[]{:S(2)}) async-start(bf16[32,24,512]{2,1,0:T(8,128)(2,1)} %bitcast.24), calls=%async_computation.2 | async-start | bytes 1572864 | tf_op jit(solution)/shard_map/all_to_all | solution.py:326
  175.1 1.4 reshape.225.refs_2_.total_ref
  176.5 2.4 %reshape.226.refs_3_.mixed_ref = f32[128,2048]{1,0:T(8,128)} reshape(f32[32,64,128]{2,1,0:T(8,128)} %copy-done.8) | data formatting | bytes 2097152 | tf_op jit(solution)/shard_map/reshape | solution.py:329
  178.8 15.2 %all-to-all-done.2 = bf16[32,24,512]{2,1,0:T(8,128)(2,1)} async-done(((bf16[32,24,512]{2,1,0:T(8,128)(2,1)}), bf16[32,24,512]{2,1,0:T(8,128)(2,1)}, u32[]{:S(2)}, u32[]{:S(2)}) %all-to-all-start.2) | async-done | bytes 786464 | tf_op jit(solution)/shard_map/all_to_all | solution.py:326
  196.4 2.6 %finish.1 = (f32[128,1024]{1,0:T(8,128)}, bf16[128,1152]{1,0:T(8,128)(2,1)S(1)}) custom-call(s32[1]{0:T(128)} %bitcast.part_ref, bf16[2,256,768]{2,1,0:T(8,128)(2,1)S(1)} %copy-done.10, bf16[768,512]{1,0:T(8,128)(2,1)} %bitcast.25.returned_ref, bf16[128,4096]{1,0:T(8,128)(2,1)S(1)} %copy-done.2, bf16[1,4096]{1,0:T(2,128)(2,1)S(1)} %reshape.222.gain_ref, ...), custom_call_target="tpu_custom_call" | custom-call | bytes 8691716 | tf_op jit(solution)/shard_map/finish/pallas_call | solution.py:161
  199.0 1.3 collective-permute-start.17
  200.3 4.1 %collective-permute-start.16 = (bf16[128,1152]{1,0:T(8,128)(2,1)S(1)}, bf16[128,1152]{1,0:T(8,128)(2,1)S(1)}, u32[]{:S(2)}, u32[]{:S(2)}) collective-permute-start(bf16[128,1152]{1,0:T(8,128)(2,1)S(1)} %get-tuple-element.38.own_ref), channel_id=1, source_target_pairs={{0,1},{1,0},{2,3},{3,2},{4,5},{5,4},{6,7},{7,6},{8,9},{9,8},{10,11... | collective-permute-start | bytes 884744 | tf_op jit(solution)/shard_map/ppermute | solution.py:15
  204.4 1.6 collective-permute-done.17.y_ref
  206.0 4.3 %collective-permute-start.18 = (bf16[128,1152]{1,0:T(8,128)(2,1)S(1)}, bf16[128,1152]{1,0:T(8,128)(2,1)S(1)}, u32[]{:S(2)}, u32[]{:S(2)}) collective-permute-start(bf16[128,1152]{1,0:T(8,128)(2,1)S(1)} %collective-permute-done.17.y_ref), channel_id=1, source_target_pairs={{0,1},{1,0},{2,3},{3,2},{4,5},{5,4},{6,7},{7,6},{8,9},{9,8},{10,11... | collective-permute-start | bytes 884744 | tf_op jit(solution)/shard_map/ppermute | solution.py:15
  211.5 6.6 %last_step.1 = (bf16[128,256]{1,0:T(8,128)(2,1)S(1)}, bf16[128,2048]{1,0:T(8,128)(2,1)}) custom-call(s32[1]{0:T(128)} %bitcast.part_ref, bf16[128,1152]{1,0:T(8,128)(2,1)S(1)} %get-tuple-element.38.own_ref, bf16[128,1152]{1,0:T(8,128)(2,1)S(1)} %collective-permute-done.16.core_ref, bf16[128,1152]{1,0:T(8,128)(2,1)S(1)} %collective-permute-done.17.y_ref, ...), custom_call_target="tpu_custom_call" | custom-call | bytes 7536644 | tf_op jit(solution)/shard_map/last_step/pallas_call | solution.py:161
  (122 shorter events, 25.0 us)
Async XLA Ops:
  0.6 140.2 %copy-start = (bf16[4096,16]{0,1:T(8,128)(2,1)S(1)}, bf16[4096,16]{0,1:T(8,128)(2,1)}, u32[]{:S(2)}) copy-start(bf16[4096,16]{0,1:T(8,128)(2,1)} %param.17) | copy-start | bytes 393220
  0.6 17.4 %copy-start.30 = (s32[1,32]{1,0:T(1,128)S(1)}, s32[1,32]{1,0:T(1,128)}, u32[]{:S(2)}) copy-start(s32[1,32]{1,0:T(1,128)} %param.27) | copy-start | bytes 388
  0.7 46.7 %collective-permute-start = (bf16[32,2,128,128]{3,2,1,0:T(8,128)(2,1)}, bf16[32,2,128,128]{3,2,1,0:T(8,128)(2,1)S(1)}, u32[]{:S(2)}, u32[]{:S(2)}) collective-permute-start(bf16[32,2,128,128]{3,2,1,0:T(8,128)(2,1)} %bitcast.52), channel_id=1, source_target_pairs={{0,128},{128,0},{1,129},{129,1},{2,130},{130,2},{3,131},{131,3},{4... | collective-permute-start | bytes 6291464 | tf_op jit(solution)/shard_map/ppermute | solution.py:15
  7.0 40.3 %all-to-all-start = ((bf16[32,24,512]{2,1,0:T(8,128)(2,1)}), bf16[32,24,512]{2,1,0:T(8,128)(2,1)S(1)}, u32[]{:S(2)}, u32[]{:S(2)}) async-start(bf16[32,24,512]{2,1,0:T(8,128)(2,1)} %get-tuple-element.23), calls=%async_computation | async-start | bytes 1572864 | tf_op jit(solution)/shard_map/all_to_all | solution.py:239
  18.1 29.2 %collective-permute-start.1 = (s32[1,32]{1,0:T(1,128)S(1)}, s32[1,32]{1,0:T(1,128)S(1)}, u32[]{:S(2)}, u32[]{:S(2)}) collective-permute-start(s32[1,32]{1,0:T(1,128)S(1)} %copy-done.30), channel_id=1, source_target_pairs={{0,128},{128,0},{1,129},{129,1},{2,130},{130,2},{3,131},{131,3},{4... | collective-permute-start | bytes 392 | tf_op jit(solution)/shard_map/ppermute | solution.py:15
  48.9 24.9 %copy-start.29 = (s32[1,32]{1,0:T(1,128)S(1)}, s32[1,32]{1,0:T(1,128)}, u32[]{:S(2)}) copy-start(s32[1,32]{1,0:T(1,128)} %copy-done.28) | copy-start | bytes 388
  48.9 20.2 %collective-permute-start.3 = (bf16[768,512]{1,0:T(8,128)(2,1)}, bf16[768,512]{1,0:T(8,128)(2,1)S(1)}, u32[]{:S(2)}, u32[]{:S(2)}) collective-permute-start(bf16[768,512]{1,0:T(8,128)(2,1)} %held_until.4.refs_0_), channel_id=1, source_target_pairs={{0,2},{1,3},{2,0},{3,1},{4,6},{5,7},{6,4},{7,5},{8,10},{9,11},{10,... | collective-permute-start | bytes 2359304 | tf_op jit(solution)/shard_map/ppermute | solution.py:15
  52.8 17.4 %collective-permute-start.2 = (bf16[768,512]{1,0:T(8,128)(2,1)}, bf16[768,512]{1,0:T(8,128)(2,1)S(1)}, u32[]{:S(2)}, u32[]{:S(2)}) collective-permute-start(bf16[768,512]{1,0:T(8,128)(2,1)} %held_until.4.refs_0_), channel_id=1, source_target_pairs={{0,4},{4,0},{8,12},{12,8},{16,20},{20,16},{24,28},{28,24},{32,36},... | collective-permute-start | bytes 2359304 | tf_op jit(solution)/shard_map/ppermute | solution.py:15
  71.1 21.5 %collective-permute-start.4 = (bf16[768,512]{1,0:T(8,128)(2,1)}, bf16[768,512]{1,0:T(8,128)(2,1)}, u32[]{:S(2)}, u32[]{:S(2)}) collective-permute-start(bf16[768,512]{1,0:T(8,128)(2,1)} %held_until.5.refs_1_), channel_id=1, source_target_pairs={{0,2},{1,3},{2,0},{3,1},{4,6},{5,7},{6,4},{7,5},{8,10},{9,11},{10,... | collective-permute-start | bytes 2359304 | tf_op jit(solution)/shard_map/ppermute | solution.py:15
  77.6 11.3 %copy-start.7 = (bf16[768,512]{1,0:T(8,128)(2,1)S(1)}, bf16[768,512]{1,0:T(8,128)(2,1)}, u32[]{:S(2)}) copy-start(bf16[768,512]{1,0:T(8,128)(2,1)} %held_until.4.refs_0_) | copy-start | bytes 2359300
  77.6 14.5 %copy-start.5 = (bf16[768,512]{1,0:T(8,128)(2,1)S(1)}, bf16[768,512]{1,0:T(8,128)(2,1)}, u32[]{:S(2)}) copy-start(bf16[768,512]{1,0:T(8,128)(2,1)} %held_until.5.refs_1_) | copy-start | bytes 2359300
  77.6 14.6 %copy-start.12 = (bf16[768,512]{1,0:T(8,128)(2,1)S(1)}, bf16[768,512]{1,0:T(8,128)(2,1)}, u32[]{:S(2)}) copy-start(bf16[768,512]{1,0:T(8,128)(2,1)} %copy-done.11) | copy-start | bytes 2359300
  77.6 69.3 %all-to-all-start.1 = ((bf16[32,2,128,128]{3,2,1,0:T(8,128)(2,1)}), bf16[32,2,128,128]{3,2,1,0:T(8,128)(2,1)}, u32[]{:S(2)}, u32[]{:S(2)}) async-start(bf16[32,2,128,128]{3,2,1,0:T(8,128)(2,1)} %held_until.6.refs_0_), calls=%async_computation.1 | async-start | bytes 4194304 | tf_op jit(solution)/shard_map/all_to_all | solution.py:269
  88.9 5.1 %collective-permute-start.6 = (bf16[768,512]{1,0:T(8,128)(2,1)S(1)}, bf16[768,512]{1,0:T(8,128)(2,1)S(1)}, u32[]{:S(2)}, u32[]{:S(2)}) collective-permute-start(bf16[768,512]{1,0:T(8,128)(2,1)S(1)} %copy-done.7), channel_id=1, source_target_pairs={{0,1},{1,0},{2,3},{3,2},{4,5},{5,4},{6,7},{7,6},{8,9},{9,8},{10,11... | collective-permute-start | bytes 2359304 | tf_op jit(solution)/shard_map/ppermute | solution.py:15
  92.1 4.3 %collective-permute-start.7 = (bf16[768,512]{1,0:T(8,128)(2,1)S(1)}, bf16[768,512]{1,0:T(8,128)(2,1)}, u32[]{:S(2)}, u32[]{:S(2)}) collective-permute-start(bf16[768,512]{1,0:T(8,128)(2,1)S(1)} %copy-done.5), channel_id=1, source_target_pairs={{0,1},{1,0},{2,3},{3,2},{4,5},{5,4},{6,7},{7,6},{8,9},{9,8},{10,11... | collective-permute-start | bytes 2359304 | tf_op jit(solution)/shard_map/ppermute | solution.py:15
  92.2 5.3 %collective-permute-start.8 = (bf16[768,512]{1,0:T(8,128)(2,1)S(1)}, bf16[768,512]{1,0:T(8,128)(2,1)}, u32[]{:S(2)}, u32[]{:S(2)}) collective-permute-start(bf16[768,512]{1,0:T(8,128)(2,1)S(1)} %copy-done.12), channel_id=1, source_target_pairs={{0,1},{1,0},{2,3},{3,2},{4,5},{5,4},{6,7},{7,6},{8,9},{9,8},{10,11... | collective-permute-start | bytes 2359304 | tf_op jit(solution)/shard_map/ppermute | solution.py:15
  92.6 11.7 %collective-permute-start.5 = (bf16[768,512]{1,0:T(8,128)(2,1)}, bf16[768,512]{1,0:T(8,128)(2,1)}, u32[]{:S(2)}, u32[]{:S(2)}) collective-permute-start(bf16[768,512]{1,0:T(8,128)(2,1)} %collective-permute-done.4.mine_ref), channel_id=1, source_target_pairs={{0,1},{1,0},{2,3},{3,2},{4,5},{5,4},{6,7},{7,6},{8,9},{9,8},{10,11... | collective-permute-start | bytes 2359304 | tf_op jit(solution)/shard_map/ppermute | solution.py:15
  111.2 4.7 %copy-start.15 = (bf16[768,512]{1,0:T(8,128)(2,1)}, bf16[768,512]{1,0:T(8,128)(2,1)S(1)}, u32[]{:S(2)}) copy-start(bf16[768,512]{1,0:T(8,128)(2,1)S(1)} %get-tuple-element.26.mine_ref) | copy-start | bytes 2359300
  111.2 2.6 %collective-permute-start.11 = (bf16[768,512]{1,0:T(8,128)(2,1)}, bf16[768,512]{1,0:T(8,128)(2,1)S(1)}, u32[]{:S(2)}, u32[]{:S(2)}) collective-permute-start(bf16[768,512]{1,0:T(8,128)(2,1)} %get-tuple-element.31), channel_id=1, source_target_pairs={{0,1},{1,0},{2,3},{3,2},{4,5},{5,4},{6,7},{7,6},{8,9},{9,8},{10,11... | collective-permute-start | bytes 2359304 | tf_op jit(solution)/shard_map/ppermute | solution.py:15
  111.7 3.1 %collective-permute-start.14 = (bf16[768,512]{1,0:T(8,128)(2,1)S(1)}, bf16[768,512]{1,0:T(8,128)(2,1)S(1)}, u32[]{:S(2)}, u32[]{:S(2)}) collective-permute-start(bf16[768,512]{1,0:T(8,128)(2,1)S(1)} %get-tuple-element.33), channel_id=1, source_target_pairs={{0,1},{1,0},{2,3},{3,2},{4,5},{5,4},{6,7},{7,6},{8,9},{9,8},{10,11... | collective-permute-start | bytes 2359304 | tf_op jit(solution)/shard_map/ppermute | solution.py:15
  114.0 20.5 %collective-permute-start.12 = (bf16[768,512]{1,0:T(8,128)(2,1)S(1)}, bf16[768,512]{1,0:T(8,128)(2,1)S(1)}, u32[]{:S(2)}, u32[]{:S(2)}) collective-permute-start(bf16[768,512]{1,0:T(8,128)(2,1)S(1)} %add_convert_fusion.2), channel_id=1, source_target_pairs={{0,2},{1,3},{2,0},{3,1},{4,6},{5,7},{6,4},{7,5},{8,10},{9,11},{10,... | collective-permute-start | bytes 2359304 | tf_op jit(solution)/shard_map/ppermute | solution.py:15
  114.1 21.6 %collective-permute-start.10 = (bf16[768,512]{1,0:T(8,128)(2,1)S(1)}, bf16[768,512]{1,0:T(8,128)(2,1)}, u32[]{:S(2)}, u32[]{:S(2)}) collective-permute-start(bf16[768,512]{1,0:T(8,128)(2,1)S(1)} %get-tuple-element.29), channel_id=1, source_target_pairs={{0,1},{1,0},{2,3},{3,2},{4,5},{5,4},{6,7},{7,6},{8,9},{9,8},{10,11... | collective-permute-start | bytes 2359304 | tf_op jit(solution)/shard_map/ppermute | solution.py:15
  114.6 47.0 %collective-permute-start.9 = (bf16[768,512]{1,0:T(8,128)(2,1)}, bf16[768,512]{1,0:T(8,128)(2,1)}, u32[]{:S(2)}, u32[]{:S(2)}) collective-permute-start(bf16[768,512]{1,0:T(8,128)(2,1)} %get-tuple-element.27), channel_id=1, source_target_pairs={{0,1},{1,0},{2,3},{3,2},{4,5},{5,4},{6,7},{7,6},{8,9},{9,8},{10,11... | collective-permute-start | bytes 2359304 | tf_op jit(solution)/shard_map/ppermute | solution.py:15
  135.4 26.3 %collective-permute-start.15 = (bf16[768,512]{1,0:T(8,128)(2,1)}, bf16[768,512]{1,0:T(8,128)(2,1)}, u32[]{:S(2)}, u32[]{:S(2)}) collective-permute-start(bf16[768,512]{1,0:T(8,128)(2,1)} %held_until.7), channel_id=1, source_target_pairs={{0,2},{1,3},{2,0},{3,1},{4,6},{5,7},{6,4},{7,5},{8,10},{9,11},{10,... | collective-permute-start | bytes 2359304 | tf_op jit(solution)/shard_map/ppermute | solution.py:15
  135.7 4.7 %copy-start.27 = (s32[32,4]{0,1:T(4,128)S(1)}, s32[32,4]{0,1:T(4,128)}, u32[]{:S(2)}) copy-start(s32[32,4]{0,1:T(4,128)} %param.28) | copy-start | bytes 1540
  138.4 23.3 %collective-permute-start.13 = (bf16[768,512]{1,0:T(8,128)(2,1)}, bf16[768,512]{1,0:T(8,128)(2,1)}, u32[]{:S(2)}, u32[]{:S(2)}) collective-permute-start(bf16[768,512]{1,0:T(8,128)(2,1)} %add_convert_fusion.1), channel_id=1, source_target_pairs={{0,4},{4,0},{8,12},{12,8},{16,20},{20,16},{24,28},{28,24},{32,36},... | collective-permute-start | bytes 2359304 | tf_op jit(solution)/shard_map/ppermute | solution.py:15
  150.4 11.3 %copy-start.16 = (bf16[768,512]{1,0:T(8,128)(2,1)S(1)}, bf16[768,512]{1,0:T(8,128)(2,1)}, u32[]{:S(2)}) copy-start(bf16[768,512]{1,0:T(8,128)(2,1)} %copy-done.15) | copy-start | bytes 2359300
  164.9 29.1 %all-to-all-start.2 = ((bf16[32,24,512]{2,1,0:T(8,128)(2,1)}), bf16[32,24,512]{2,1,0:T(8,128)(2,1)}, u32[]{:S(2)}, u32[]{:S(2)}) async-start(bf16[32,24,512]{2,1,0:T(8,128)(2,1)} %bitcast.24), calls=%async_computation.2 | async-start | bytes 1572864 | tf_op jit(solution)/shard_map/all_to_all | solution.py:326
  196.4 15.1 %copy-start.14 = (bf16[128,2048]{1,0:T(8,128)(2,1)S(1)}, bf16[128,2048]{1,0:T(8,128)(2,1)}, u32[]{:S(2)}) copy-start(bf16[128,2048]{1,0:T(8,128)(2,1)} %query_ref.1) | copy-start | bytes 1572868
  199.0 7.1 %collective-permute-start.17 = (bf16[128,1152]{1,0:T(8,128)(2,1)S(1)}, bf16[128,1152]{1,0:T(8,128)(2,1)S(1)}, u32[]{:S(2)}, u32[]{:S(2)}) collective-permute-start(bf16[128,1152]{1,0:T(8,128)(2,1)S(1)} %get-tuple-element.38.own_ref), channel_id=1, source_target_pairs={{0,2},{1,3},{2,0},{3,1},{4,6},{5,7},{6,4},{7,5},{8,10},{9,11},{10,... | collective-permute-start | bytes 884744 | tf_op jit(solution)/shard_map/ppermute | solution.py:15
  200.3 10.0 %collective-permute-start.16 = (bf16[128,1152]{1,0:T(8,128)(2,1)S(1)}, bf16[128,1152]{1,0:T(8,128)(2,1)S(1)}, u32[]{:S(2)}, u32[]{:S(2)}) collective-permute-start(bf16[128,1152]{1,0:T(8,128)(2,1)S(1)} %get-tuple-element.38.own_ref), channel_id=1, source_target_pairs={{0,1},{1,0},{2,3},{3,2},{4,5},{5,4},{6,7},{7,6},{8,9},{9,8},{10,11... | collective-permute-start | bytes 884744 | tf_op jit(solution)/shard_map/ppermute | solution.py:15
  206.0 5.5 %collective-permute-start.18 = (bf16[128,1152]{1,0:T(8,128)(2,1)S(1)}, bf16[128,1152]{1,0:T(8,128)(2,1)S(1)}, u32[]{:S(2)}, u32[]{:S(2)}) collective-permute-start(bf16[128,1152]{1,0:T(8,128)(2,1)S(1)} %collective-permute-done.17.y_ref), channel_id=1, source_target_pairs={{0,1},{1,0},{2,3},{3,2},{4,5},{5,4},{6,7},{7,6},{8,9},{9,8},{10,11... | collective-permute-start | bytes 884744 | tf_op jit(solution)/shard_map/ppermute | solution.py:15
  (21 other events, 42.9 us)

commit v3 on v2

--- a/solution.py
+++ b/solution.py
@@ -19,7 +19,7 @@
     return lax.rsqrt(square_sum / width + epsilon)
 
 
-def prepare(part_ref, routes_ref, hidden_ref, gain_ref, packed_ref, slots_ref, *, capacity):
+def prepare(part_ref, routes_ref, hidden_ref, gain_ref, packed_ref, slots_ref, scale_ref, *, capacity):
     token_rows, model_width = hidden_ref.shape
     peers, _, eighth = packed_ref.shape
     experts = peers // 2
@@ -28,7 +28,9 @@
     hidden = hidden_ref[...].astype(f32)
     squares = jnp.sum(hidden * hidden, axis=1, keepdims=True)
     columns = pl.ds(pl.multiple_of(part_ref[0] * quarter, quarter), quarter)
-    own = hidden_ref[:, columns].astype(f32) * inverse_rms(squares, model_width) * gain_ref[:, columns].astype(f32)
+    scale = inverse_rms(squares, model_width)
+    scale_ref[...] = jnp.broadcast_to(scale, scale_ref.shape)
+    own = hidden_ref[:, columns].astype(f32) * scale * gain_ref[:, columns].astype(f32)
     one_routes, two_routes = routes_ref[0:1, :], routes_ref[1:2, :]
     expert = lax.broadcasted_iota(jnp.int32, (max(experts, 8), token_rows), 0)
     one_hot, two_hot = (expert == one_routes).astype(f32), (expert == two_routes).astype(f32)
@@ -68,17 +70,29 @@
         out[...] = total
 
 
-def late_units(blocks_ref, mine_ref, theirs_ref, gate_sum, up_sum, gate_ref, up_ref, down_ref, *refs):
+def late_units(blocks_ref, mine_low, mine_high, theirs_low, theirs_high, gate_sum, up_sum, gate_ref, up_ref, down_ref, *refs):
     outputs = refs[-8:]
-    eighth = mine_ref.shape[1]
+    eighth = mine_low.shape[1]
     gate, up = gate_sum[...], up_sum[...]
-    for i, piece in ((3, mine_ref), (7, theirs_ref)):
-        gate = gate + wide(piece[...], gate_ref[:, window(blocks_ref, i, eighth)])
-        up = up + wide(piece[...], up_ref[:, window(blocks_ref, i, eighth)])
+    for i, low, high in ((3, mine_low, mine_high), (7, theirs_low, theirs_high)):
+        piece = jnp.concatenate([low[...], high[...]], axis=0)
+        gate = gate + wide(piece, gate_ref[:, window(blocks_ref, i, eighth)])
+        up = up + wide(piece, up_ref[:, window(blocks_ref, i, eighth)])
     act = (gate / (1.0 + jnp.exp(-gate)) * up).astype(jnp.bfloat16)
     for i in (3, 7, 2, 6, 1, 5, 0, 4):
         columns = down_ref[:, window(blocks_ref, i, eighth)]
         outputs[i][...] = jnp.dot(act, columns, preferred_element_type=jnp.float32).astype(jnp.bfloat16)
+
+
+def turn(mine_x, theirs_x, mine_y, theirs_y, low_ref, high_ref, x_ref, y_ref):
+    half = low_ref.shape[0]
+    for mine, theirs, far, part, out in ((mine_x, theirs_x, low_ref, 0, x_ref), (mine_y, theirs_y, high_ref, 1, y_ref)):
+        for i in range(2):
+            span = slice(i * half, (i + 1) * half)
+            total = mine[span].astype(jnp.float32) + theirs[span].astype(jnp.float32)
+            if i == part:
+                total = total + far[...].astype(jnp.float32)
+            out[span] = total.astype(jnp.bfloat16)
 
 
 def join(mine_ref, theirs_ref, x_ref, y_ref, *refs):
@@ -229,9 +243,9 @@
     side = lax.axis_index("grp") & 1
     part = tp_rank.astype(jnp.int32).reshape(1)
 
-    packed, slots = call(
+    packed, slots, scale_in = call(
         functools.partial(prepare, capacity=capacity),
-        (shape((peer_count, capacity, eighth), bf16), shape((picks_per, token_rows), jnp.int32)),
+        (shape((peer_count, capacity, eighth), bf16), shape((picks_per, token_rows), jnp.int32), shape((token_rows, LANES), f32)),
         (part, routes.T, hidden_in, moe_gain.reshape(1, model_width)),
         smem=1,
         name="prepare",
@@ -241,11 +255,9 @@
 
     crossed = swapped(prompt_cache[:, 0], "role", 0)
     order = swapped(handoff, "role", 0)
-    landed = held_until(landed, crossed, order)
 
     hidden = hidden_in.astype(f32)
-    scale_in = inverse_rms(jnp.sum(hidden * hidden, axis=1, keepdims=True), model_width)
-    moe_in = (hidden * scale_in * moe_gain.astype(f32)).astype(bf16)
+    moe_in = (hidden * scale_in[:, :1] * moe_gain.astype(f32)).astype(bf16)
     logits = jnp.dot(moe_in, router, preferred_element_type=f32)
     gate_probs = jax.nn.softmax(jnp.take_along_axis(logits, routes, axis=1), axis=1)
     targets = jnp.arange(total_slots, dtype=jnp.int32)
@@ -258,14 +270,21 @@
     target_half = targets // capacity % 2
     halves = jnp.stack([jnp.where(target_half == i, both_terms, jnp.zeros((), bf16)) for i in range(2)])
 
+    requests, max_blocks = block_table.shape
+    head_dim = kv_weight.shape[2]
+    flat_weight = kv_weight.reshape(model_width, 2 * head_dim)
+    middle = total_slots // 2
+    landed = held_until(landed, crossed, order, halves, flat_weight)
     from_y = swapped(landed, "tp", 1)
     from_x = held_until(swapped(landed, "grp", 0), from_y)
+    landed_core = swapped(landed, "tp", 0)
     mine = (landed, from_x, from_y)
-    theirs = tuple(swapped(x, "tp", 0) for x in mine)
-    last_mine = swapped(from_x, "tp", 1)
-    last_theirs = swapped(last_mine, "tp", 0)
-
-    ordered = held_until(crossed.at[order[0]].get(mode="promise_in_bounds"), from_x)
+    theirs = (landed_core, swapped(from_x, "tp", 0), swapped(from_y, "tp", 0))
+    last_mine = (swapped(from_x[:middle], "tp", 1), swapped(from_y[middle:], "grp", 0))
+    last_theirs = tuple(swapped(x, "tp", 0) for x in last_mine)
+
+    order = held_until(order, landed_core)
+    ordered = crossed.at[order[0]].get(mode="promise_in_bounds")
     arrived = lax.all_to_all(ordered, "grp", split_axis=0, concat_axis=0, tiled=True)
 
     blocks = jnp.stack(
@@ -288,15 +307,13 @@
     sums = call(
         late_units,
         (shape((total_slots, eighth), bf16),) * 8,
-        (blocks, last_mine, last_theirs, *sums, gate_own, up_own, down_weight[0], ordered),
+        (blocks, *last_mine, *last_theirs, *sums, gate_own, up_own, down_weight[0], ordered),
         smem=1,
         away=1,
         name="late_units",
         flops=3 * total_slots * model_width * unit_count,
     )
 
-    requests, max_blocks = block_table.shape
-    head_dim = kv_weight.shape[2]
     draft_count = token_rows // requests
     per_kv = queries.shape[1] // head_dim
     query_rows = queries.reshape(requests, draft_count * per_kv, head_dim)
@@ -310,16 +327,20 @@
         flops=4 * requests * draft_count * per_kv * head_dim * max_blocks * decode_cache.shape[3],
     )
 
-    def both_cores(i):
-        return sums[i].astype(f32) + swapped(sums[4 + i], "tp", 0).astype(f32)
-
-    far = swapped(both_cores(3).astype(bf16), "tp", 1)
-    sum_x = swapped((both_cores(1) + far.astype(f32)).astype(bf16), "grp", 0)
-    sum_y = swapped(held_until(both_cores(2).astype(bf16), far), "tp", 1)
+    from_core = tuple(swapped(x, "tp", 0) for x in sums[4:])
+    both_ways = (sums[3].astype(f32) + from_core[3].astype(f32)).astype(bf16)
+    low, high = swapped(both_ways[:middle], "tp", 1), swapped(both_ways[middle:], "grp", 0)
+    to_x, to_y = call(
+        turn,
+        (shape((total_slots, eighth), bf16),) * 2,
+        (sums[1], from_core[1], sums[2], from_core[2], low, high),
+        name="turn",
+    )
+    sum_x, sum_y = swapped(to_x, "grp", 0), swapped(to_y, "tp", 1)
     summed = call(
         join,
         shape((total_slots, eighth), bf16),
-        (sums[0], swapped(sums[4], "tp", 0), sum_x, sum_y, *stats),
+        (sums[0], from_core[0], sum_x, sum_y, *stats),
         away=3,
         name="join",
     )
@@ -327,13 +348,12 @@
         summed.reshape(peer_count, capacity, eighth), "grp", split_axis=0, concat_axis=0, tiled=True
     ).reshape(total_slots, eighth)
     stats = tuple(x.reshape(token_rows, per_kv * head_dim) for x in stats)
-    flat_weight = kv_weight.reshape(model_width, 2 * head_dim)
     residual_out, scaled = call(
         finish,
         (shape((token_rows, quarter), f32), shape((token_rows, quarter + LANES), bf16)),
-        (part, halves, returned, hidden_in, attn_gain.reshape(1, model_width), flat_weight, *stats),
-        smem=1,
-        away=4,
+        (part, halves, returned, hidden_in, attn_gain.reshape(1, model_width), *stats),
+        smem=1,
+        away=3,
         name="finish",
     )
 

time: 220 us -> 223 us (1.014)
  starting transfers between devices: 58.1 us -> 63.9 us
  other arithmetic: 9.14 us -> 5.83 us
    ppermute x19 -> x22, starting transfers between devices: 27.2 us -> 34.4 us  [swapped(): lax.ppermute(x, axis, [(i, i ^ 1 << bit) for i in range(lax.axis_size(axi...]
    convert_element_type x4 -> x2, other arithmetic: 3.98 us -> 0.21 us  [the longest x1 0.21 us: local(): both_ways = (sums[3].astype(f32) + from_core[3].astype(f32)).astype(bf16)]
    all_to_all x1, waiting for transfers between devices: 15.2 us -> 17.7 us  [local(): lax.all_to_all(summed.reshape(peer_count, capacity, eighth), 'grp', split...]
    all_to_all x1, starting transfers between devices: 11.3 us -> 9 us  [local(): lax.all_to_all(ordered, 'grp', split_axis=0, concat_axis=0, tiled=True)]
    unnamed x64 -> x62, local copies, waits for them, and re-layouts: 13.9 us -> 11.7 us
    pallas_call x7 -> x8, Pallas kernels: 36.1 us -> 37.6 us  [call(): pl.pallas_call(kernel, out_shape=out_shape, in_specs=[pl.BlockSpec(memory...]
    ppermute x19 -> x22, waiting for transfers between devices: 72.9 us -> 72 us  [swapped(): lax.ppermute(x, axis, [(i, i ^ 1 << bit) for i in range(lax.axis_size(axi...]
  transfers between devices with their start and end apart: 22 -> 25, of which waited for: 11 -> 12; matrix products, arithmetic and copies ran while one was open for 11% -> 8% of each run, Pallas kernels for 11% -> 11%
where the time goes in v3:
time: 223 us; the launch traced here: 222 us
  waiting for transfers between devices  89.7 us (40%)
  starting transfers between devices  63.9 us (29%)
  Pallas kernels  37.6 us (17%)
  local copies, waits for them, and re-layouts  23.6 us (11%)
  other arithmetic  5.83 us (3%)
    ppermute x22, waiting for transfers between devices, swapped(): lax.ppermute(x, axis, [(i, i ^ 1 << bit) for i in range(lax.axis_size(axi...  72 us
    pallas_call x8, Pallas kernels, call(): pl.pallas_call(kernel, out_shape=out_shape, in_specs=[pl.BlockSpec(memory...  37.6 us
    ppermute x22, starting transfers between devices, swapped(): lax.ppermute(x, axis, [(i, i ^ 1 << bit) for i in range(lax.axis_size(axi...  34.4 us
    all_to_all x1, waiting for transfers between devices, local(): lax.all_to_all(summed.reshape(peer_count, capacity, eighth), 'grp', split...  17.7 us
    all_to_all x1, starting transfers between devices, local(): lax.all_to_all(packed, 'grp', split_axis=0, concat_axis=0, tiled=True)  11.9 us
    unnamed x62, local copies, waits for them, and re-layouts  11.7 us
    all_to_all x1, starting transfers between devices, local(): lax.all_to_all(ordered, 'grp', split_axis=0, concat_axis=0, tiled=True)  9 us
    all_to_all x1, starting transfers between devices, local(): lax.all_to_all(summed.reshape(peer_count, capacity, eighth), 'grp', split...  8.63 us
  transfers between devices with their start and end apart: 25, of which 12 were waited for; matrix products, arithmetic and copies ran while one was open for 8% of the time, Pallas kernels for 11%

profile of v3, /device:TPU:1, one launch (start us, length us, event | category | flops | bytes accessed | tf_op | source)
XLA Modules:
  0.0 222.1 jit_solution(4327558862014906055)
XLA Ops:
  3.3 1.6 prepare.1
  4.9 11.9 %all-to-all-start = ((bf16[32,24,512]{2,1,0:T(8,128)(2,1)}), bf16[32,24,512]{2,1,0:T(8,128)(2,1)S(1)}, u32[]{:S(2)}, u32[]{:S(2)}) async-start(bf16[32,24,512]{2,1,0:T(8,128)(2,1)} %get-tuple-element.27), calls=%async_computation | async-start | bytes 1572864 | tf_op jit(solution)/shard_map/all_to_all | solution.py:253
  19.2 2.0 gather_fusion.1
  23.0 1.6 copy.43
  24.6 38.8 %collective-permute-done.1.refs_2_.refs_0_ = s32[1,32]{1,0:T(1,128)S(1)} collective-permute-done((s32[1,32]{1,0:T(1,128)S(1)}, s32[1,32]{1,0:T(1,128)S(1)}, u32[]{:S(2)}, u32[]{:S(2)}) %collective-permute-start.1) | collective-permute-done | bytes 160 | tf_op jit(solution)/shard_map/ppermute | solution.py:15
  64.3 1.9 collective-permute-start.8
  67.4 2.9 %collective-permute-start.3 = (bf16[768,512]{1,0:T(8,128)(2,1)}, bf16[768,512]{1,0:T(8,128)(2,1)S(1)}, u32[]{:S(2)}, u32[]{:S(2)}) collective-permute-start(bf16[768,512]{1,0:T(8,128)(2,1)} %held_until.3.refs_0_), channel_id=1, source_target_pairs={{0,2},{1,3},{2,0},{3,1},{4,6},{5,7},{6,4},{7,5},{8,10},{9,11},{10,... | collective-permute-start | bytes 2359304 | tf_op jit(solution)/shard_map/ppermute | solution.py:15
  71.8 3.7 %gather_fusion = bf16[32,2,128,128]{3,2,1,0:T(8,128)(2,1)} fusion(bf16[32,2,128,128]{3,2,1,0:T(8,128)(2,1)} %collective-permute-done.refs_1_, s32[1024]{0:T(1024)S(1)} %pad_clamp_fusion), kind=kCustom, calls=%fused_computation | custom fusion | bytes 4194432 | tf_op jit(solution)/shard_map/gather | solution.py:287
  75.6 9.0 %all-to-all-start.1 = ((bf16[32,2,128,128]{3,2,1,0:T(8,128)(2,1)}), bf16[32,2,128,128]{3,2,1,0:T(8,128)(2,1)}, u32[]{:S(2)}, u32[]{:S(2)}) async-start(bf16[32,2,128,128]{3,2,1,0:T(8,128)(2,1)} %gather_fusion), calls=%async_computation.1 | async-start | bytes 4194304 | tf_op jit(solution)/shard_map/all_to_all | solution.py:288
  85.5 2.4 %collective-permute-done.3.refs_1_.refs_2_ = bf16[768,512]{1,0:T(8,128)(2,1)S(1)} collective-permute-done((bf16[768,512]{1,0:T(8,128)(2,1)}, bf16[768,512]{1,0:T(8,128)(2,1)S(1)}, u32[]{:S(2)}, u32[]{:S(2)}) %collective-permute-start.3) | collective-permute-done | bytes 786464 | tf_op jit(solution)/shard_map/ppermute | solution.py:15
  91.1 3.0 %collective-permute-start.4 = (bf16[384,512]{1,0:T(8,128)(2,1)S(1)}, bf16[384,512]{1,0:T(8,128)(2,1)}, u32[]{:S(2)}, u32[]{:S(2)}) collective-permute-start(bf16[384,512]{1,0:T(8,128)(2,1)S(1)} %slice.24), channel_id=1, source_target_pairs={{0,2},{1,3},{2,0},{3,1},{4,6},{5,7},{6,4},{7,5},{8,10},{9,11},{10,... | collective-permute-start | bytes 1179656 | tf_op jit(solution)/shard_map/ppermute | solution.py:15
  96.0 7.1 %collective-permute-done.4.mine_low = bf16[384,512]{1,0:T(8,128)(2,1)} collective-permute-done((bf16[384,512]{1,0:T(8,128)(2,1)S(1)}, bf16[384,512]{1,0:T(8,128)(2,1)}, u32[]{:S(2)}, u32[]{:S(2)}) %collective-permute-start.4) | collective-permute-done | bytes 393248 | tf_op jit(solution)/shard_map/ppermute | solution.py:15
  104.4 6.5 %collective-permute-done.5.mine_high = bf16[384,512]{1,0:T(8,128)(2,1)} collective-permute-done((bf16[384,512]{1,0:T(8,128)(2,1)S(1)}, bf16[384,512]{1,0:T(8,128)(2,1)}, u32[]{:S(2)}, u32[]{:S(2)}) %collective-permute-start.5) | collective-permute-done | bytes 393248 | tf_op jit(solution)/shard_map/ppermute | solution.py:15
  110.8 1.5 collective-permute-start.7
  112.4 5.0 %early_units.1 = (f32[768,192]{1,0:T(8,128)S(1)}, f32[768,192]{1,0:T(8,128)S(1)}) custom-call(s32[8]{0:T(128)S(1)} %stack.41.blocks_ref, bf16[768,512]{1,0:T(8,128)(2,1)S(1)} %copy-done.3, bf16[768,512]{1,0:T(8,128)(2,1)S(1)} %copy-done.7, bf16[768,512]{1,0:T(8,128)(2,1)S(1)} %copy-done.5, bf16[768,512]{1,0:T(8,128)(2,1)S(1)} %copy-done.13, ...), custom_call_target="tpu_custom_call" | custom-call | flops 1811939328 | bytes 9044000 | tf_op jit(solution)/shard_map/early_units/pallas_call | solution.py:175
  119.2 7.2 %late_units.1 = (bf16[768,512]{1,0:T(8,128)(2,1)S(1)}, bf16[768,512]{1,0:T(8,128)(2,1)S(1)}, bf16[768,512]{1,0:T(8,128)(2,1)S(1)}, bf16[768,512]{1,0:T(8,128)(2,...) custom-call(s32[8]{0:T(128)S(1)} %stack.41.blocks_ref, ...), custom_call_target="tpu_custom_call" | custom-call | flops 1811939328 | bytes 15859744 | tf_op jit(solution)/shard_map/late_units/pallas_call | solution.py:175
  127.1 1.9 collective-permute-done.14
  129.9 2.3 %collective-permute-start.16 = (bf16[384,512]{1,0:T(8,128)(2,1)S(1)}, bf16[384,512]{1,0:T(8,128)(2,1)S(1)}, u32[]{:S(2)}, u32[]{:S(2)}) collective-permute-start(bf16[384,512]{1,0:T(8,128)(2,1)S(1)} %get-tuple-element.49), channel_id=1, source_target_pairs={{0,4},{4,0},{8,12},{12,8},{16,20},{20,16},{24,28},{28,24},{32,36},... | collective-permute-start | bytes 1179656 | tf_op jit(solution)/shard_map/ppermute | solution.py:15
  132.9 8.6 %collective-permute-done.15.low_ref = bf16[384,512]{1,0:T(8,128)(2,1)S(1)} collective-permute-done((bf16[384,512]{1,0:T(8,128)(2,1)S(1)}, bf16[384,512]{1,0:T(8,128)(2,1)S(1)}, u32[]{:S(2)}, u32[]{:S(2)}) %collective-permute-start.15) | collective-permute-done | bytes 393248 | tf_op jit(solution)/shard_map/ppermute | solution.py:15
  141.5 1.5 turn.1
  142.9 2.3 %collective-permute-start.17 = (bf16[768,512]{1,0:T(8,128)(2,1)}, bf16[768,512]{1,0:T(8,128)(2,1)}, u32[]{:S(2)}, u32[]{:S(2)}) collective-permute-start(bf16[768,512]{1,0:T(8,128)(2,1)} %get-tuple-element.38), channel_id=1, source_target_pairs={{0,4},{4,0},{8,12},{12,8},{16,20},{20,16},{24,28},{28,24},{32,36},... | collective-permute-start | bytes 2359304 | tf_op jit(solution)/shard_map/ppermute | solution.py:15
  146.9 3.5 %pad_maximum_fusion.pool_ref = bf16[48,2,128,128]{3,2,1,0:T(8,128)(2,1)} fusion(bf16[32,2,128,128]{3,2,1,0:T(8,128)(2,1)} %all-to-all-done.1, bf16[16,2,128,128]{3,2,1,0:T(8,128)(2,1)S(1)} %bitcast.51), kind=kLoop, calls=%fused_computation.2 | loop fusion | flops 1572864 | bytes 6291456 | tf_op jit(solution)/shard_map/concatenate | solution.py:320
  150.4 10.3 %cached_attention.1 = (f32[32,64,128]{2,1,0:T(8,128)S(1)}, f32[32,64,128]{2,1,0:T(8,128)S(1)}, f32[32,64,128]{2,1,0:T(8,128)S(1)}) custom-call(s32[128]{0:T(128)S(1)} %reshape.211.table_ref, s32[32]{0:T(128)S(1)} %copy-done.22, bf16[32,64,128]{2,1,0:T(8,128)(2,1)S(1)} %reshape.212.query_ref, bf16[48,2,128,128]{3,2,1,0:T(8,128)(2,1)} %pad_maximum_fusion.pool_ref), custom_call_target="tpu_custom_call" | custom-call | flops 536870912 | bytes 6816384 | tf_op jit(solution)/shard_map/cached_attention/pallas_call | solution.py:175
  162.5 2.4 %collective-permute-done.18.y_ref = bf16[768,512]{1,0:T(8,128)(2,1)} collective-permute-done((bf16[768,512]{1,0:T(8,128)(2,1)}, bf16[768,512]{1,0:T(8,128)(2,1)}, u32[]{:S(2)}, u32[]{:S(2)}) %collective-permute-start.18) | collective-permute-done | bytes 786464 | tf_op jit(solution)/shard_map/ppermute | solution.py:15
  164.9 2.9 %join.1 = bf16[768,512]{1,0:T(8,128)(2,1)} custom-call(bf16[768,512]{1,0:T(8,128)(2,1)S(1)} %copy-done.17, bf16[768,512]{1,0:T(8,128)(2,1)} %collective-permute-done.11.theirs_ref, bf16[768,512]{1,0:T(8,128)(2,1)} %collective-permute-done.17.x_ref, bf16[768,512]{1,0:T(8,128)(2,1)} %collective-permute-done.18.y_ref, ...), custom_call_target="tpu_custom_call" | custom-call | bytes 7077888 | tf_op jit(solution)/shard_map/join/pallas_call | solution.py:175
  167.8 8.6 %all-to-all-start.2 = ((bf16[32,24,512]{2,1,0:T(8,128)(2,1)}), bf16[32,24,512]{2,1,0:T(8,128)(2,1)}, u32[]{:S(2)}, u32[]{:S(2)}) async-start(bf16[32,24,512]{2,1,0:T(8,128)(2,1)} %bitcast.24), calls=%async_computation.2 | async-start | bytes 1572864 | tf_op jit(solution)/shard_map/all_to_all | solution.py:347
  178.2 17.7 %all-to-all-done.2 = bf16[32,24,512]{2,1,0:T(8,128)(2,1)} async-done(((bf16[32,24,512]{2,1,0:T(8,128)(2,1)}), bf16[32,24,512]{2,1,0:T(8,128)(2,1)}, u32[]{:S(2)}, u32[]{:S(2)}) %all-to-all-start.2) | async-done | bytes 786464 | tf_op jit(solution)/shard_map/all_to_all | solution.py:347
  198.3 2.6 %finish.1 = (f32[128,1024]{1,0:T(8,128)}, bf16[128,1152]{1,0:T(8,128)(2,1)S(1)}) custom-call(s32[1]{0:T(128)} %bitcast.part_ref, bf16[2,256,768]{2,1,0:T(8,128)(2,1)S(1)} %copy-done.1, bf16[768,512]{1,0:T(8,128)(2,1)} %bitcast.25.returned_ref, bf16[128,4096]{1,0:T(8,128)(2,1)S(1)} %copy-done.11, bf16[1,4096]{1,0:T(2,128)(2,1)S(1)} %reshape.215.gain_ref, ...), custom_call_target="tpu_custom_call" | custom-call | bytes 6594564 | tf_op jit(solution)/shard_map/finish/pallas_call | solution.py:175
  201.5 5.0 %collective-permute-start.19 = (bf16[128,1152]{1,0:T(8,128)(2,1)S(1)}, bf16[128,1152]{1,0:T(8,128)(2,1)S(1)}, u32[]{:S(2)}, u32[]{:S(2)}) collective-permute-start(bf16[128,1152]{1,0:T(8,128)(2,1)S(1)} %get-tuple-element.44.own_ref), channel_id=1, source_target_pairs={{0,1},{1,0},{2,3},{3,2},{4,5},{5,4},{6,7},{7,6},{8,9},{9,8},{10,11... | collective-permute-start | bytes 884744 | tf_op jit(solution)/shard_map/ppermute | solution.py:15
  206.5 1.4 collective-permute-done.20.y_ref
  207.9 5.7 %collective-permute-start.21 = (bf16[128,1152]{1,0:T(8,128)(2,1)S(1)}, bf16[128,1152]{1,0:T(8,128)(2,1)S(1)}, u32[]{:S(2)}, u32[]{:S(2)}) collective-permute-start(bf16[128,1152]{1,0:T(8,128)(2,1)S(1)} %collective-permute-done.20.y_ref), channel_id=1, source_target_pairs={{0,1},{1,0},{2,3},{3,2},{4,5},{5,4},{6,7},{7,6},{8,9},{9,8},{10,11... | collective-permute-start | bytes 884744 | tf_op jit(solution)/shard_map/ppermute | solution.py:15
  214.9 6.6 %last_step.1 = (bf16[128,256]{1,0:T(8,128)(2,1)S(1)}, bf16[128,2048]{1,0:T(8,128)(2,1)}) custom-call(s32[1]{0:T(128)} %bitcast.part_ref, bf16[128,1152]{1,0:T(8,128)(2,1)S(1)} %get-tuple-element.44.own_ref, bf16[128,1152]{1,0:T(8,128)(2,1)S(1)} %collective-permute-done.19.core_ref, bf16[128,1152]{1,0:T(8,128)(2,1)S(1)} %collective-permute-done.20.y_ref, ...), custom_call_target="tpu_custom_call" | custom-call | bytes 7536644 | tf_op jit(solution)/shard_map/last_step/pallas_call | solution.py:175
  (126 shorter events, 31.8 us)
Async XLA Ops:
  0.6 18.1 %copy-start = (bf16[4096,16]{0,1:T(8,128)(2,1)S(1)}, bf16[4096,16]{0,1:T(8,128)(2,1)}, u32[]{:S(2)}) copy-start(bf16[4096,16]{0,1:T(8,128)(2,1)} %param.17) | copy-start | bytes 393220
  0.6 17.7 %copy-start.25 = (bf16[4096]{0:T(1024)(128)(2,1)S(1)}, bf16[4096]{0:T(1024)(128)(2,1)}, u32[]{:S(2)}) copy-start(bf16[4096]{0:T(1024)(128)(2,1)} %param.16) | copy-start | bytes 24580
  0.7 17.7 %copy-start.21 = (s32[128,2]{0,1:T(2,128)S(1)}, s32[128,2]{0,1:T(2,128)}, u32[]{:S(2)}) copy-start(s32[128,2]{0,1:T(2,128)} %param.18) | copy-start | bytes 3076
  4.9 58.5 %all-to-all-start = ((bf16[32,24,512]{2,1,0:T(8,128)(2,1)}), bf16[32,24,512]{2,1,0:T(8,128)(2,1)S(1)}, u32[]{:S(2)}, u32[]{:S(2)}) async-start(bf16[32,24,512]{2,1,0:T(8,128)(2,1)} %get-tuple-element.27), calls=%async_computation | async-start | bytes 1572864 | tf_op jit(solution)/shard_map/all_to_all | solution.py:253
  16.8 46.6 %collective-permute-start = (bf16[32,2,128,128]{3,2,1,0:T(8,128)(2,1)}, bf16[32,2,128,128]{3,2,1,0:T(8,128)(2,1)}, u32[]{:S(2)}, u32[]{:S(2)}) collective-permute-start(bf16[32,2,128,128]{3,2,1,0:T(8,128)(2,1)} %bitcast.52), channel_id=1, source_target_pairs={{0,128},{128,0},{1,129},{129,1},{2,130},{130,2},{3,131},{131,3},{4... | collective-permute-start | bytes 6291464 | tf_op jit(solution)/shard_map/ppermute | solution.py:15
  18.2 45.2 %collective-permute-start.1 = (s32[1,32]{1,0:T(1,128)S(1)}, s32[1,32]{1,0:T(1,128)S(1)}, u32[]{:S(2)}, u32[]{:S(2)}) collective-permute-start(s32[1,32]{1,0:T(1,128)S(1)} %copy-done.29), channel_id=1, source_target_pairs={{0,128},{128,0},{1,129},{129,1},{2,130},{130,2},{3,131},{131,3},{4... | collective-permute-start | bytes 392 | tf_op jit(solution)/shard_map/ppermute | solution.py:15
  64.3 6.0 %collective-permute-start.8 = (bf16[768,512]{1,0:T(8,128)(2,1)}, bf16[768,512]{1,0:T(8,128)(2,1)S(1)}, u32[]{:S(2)}, u32[]{:S(2)}) collective-permute-start(bf16[768,512]{1,0:T(8,128)(2,1)} %held_until.3.refs_0_), channel_id=1, source_target_pairs={{0,1},{1,0},{2,3},{3,2},{4,5},{5,4},{6,7},{7,6},{8,9},{9,8},{10,11... | collective-permute-start | bytes 2359304 | tf_op jit(solution)/shard_map/ppermute | solution.py:15
  66.1 19.4 %collective-permute-start.2 = (bf16[768,512]{1,0:T(8,128)(2,1)}, bf16[768,512]{1,0:T(8,128)(2,1)S(1)}, u32[]{:S(2)}, u32[]{:S(2)}) collective-permute-start(bf16[768,512]{1,0:T(8,128)(2,1)} %held_until.3.refs_0_), channel_id=1, source_target_pairs={{0,4},{4,0},{8,12},{12,8},{16,20},{20,16},{24,28},{28,24},{32,36},... | collective-permute-start | bytes 2359304 | tf_op jit(solution)/shard_map/ppermute | solution.py:15
  67.4 20.6 %collective-permute-start.3 = (bf16[768,512]{1,0:T(8,128)(2,1)}, bf16[768,512]{1,0:T(8,128)(2,1)S(1)}, u32[]{:S(2)}, u32[]{:S(2)}) collective-permute-start(bf16[768,512]{1,0:T(8,128)(2,1)} %held_until.3.refs_0_), channel_id=1, source_target_pairs={{0,2},{1,3},{2,0},{3,1},{4,6},{5,7},{6,4},{7,5},{8,10},{9,11},{10,... | collective-permute-start | bytes 2359304 | tf_op jit(solution)/shard_map/ppermute | solution.py:15
  75.6 71.3 %all-to-all-start.1 = ((bf16[32,2,128,128]{3,2,1,0:T(8,128)(2,1)}), bf16[32,2,128,128]{3,2,1,0:T(8,128)(2,1)}, u32[]{:S(2)}, u32[]{:S(2)}) async-start(bf16[32,2,128,128]{3,2,1,0:T(8,128)(2,1)} %gather_fusion), calls=%async_computation.1 | async-start | bytes 4194304 | tf_op jit(solution)/shard_map/all_to_all | solution.py:288
  84.6 27.8 %copy-start.3 = (bf16[768,512]{1,0:T(8,128)(2,1)S(1)}, bf16[768,512]{1,0:T(8,128)(2,1)}, u32[]{:S(2)}) copy-start(bf16[768,512]{1,0:T(8,128)(2,1)} %held_until.3.refs_0_) | copy-start | bytes 2359300
  84.6 27.8 %copy-start.13 = (bf16[768,512]{1,0:T(8,128)(2,1)S(1)}, bf16[768,512]{1,0:T(8,128)(2,1)}, u32[]{:S(2)}) copy-start(bf16[768,512]{1,0:T(8,128)(2,1)} %copy-done.12) | copy-start | bytes 2359300
  88.9 23.5 %copy-start.5 = (bf16[768,512]{1,0:T(8,128)(2,1)S(1)}, bf16[768,512]{1,0:T(8,128)(2,1)}, u32[]{:S(2)}) copy-start(bf16[768,512]{1,0:T(8,128)(2,1)} %copy-done.4) | copy-start | bytes 2359300
  88.9 23.5 %copy-start.7 = (bf16[768,512]{1,0:T(8,128)(2,1)S(1)}, bf16[768,512]{1,0:T(8,128)(2,1)}, u32[]{:S(2)}) copy-start(bf16[768,512]{1,0:T(8,128)(2,1)} %held_until.4.refs_1_) | copy-start | bytes 2359300
  88.9 23.4 %collective-permute-start.9 = (bf16[768,512]{1,0:T(8,128)(2,1)}, bf16[768,512]{1,0:T(8,128)(2,1)}, u32[]{:S(2)}, u32[]{:S(2)}) collective-permute-start(bf16[768,512]{1,0:T(8,128)(2,1)} %held_until.4.refs_1_), channel_id=1, source_target_pairs={{0,1},{1,0},{2,3},{3,2},{4,5},{5,4},{6,7},{7,6},{8,9},{9,8},{10,11... | collective-permute-start | bytes 2359304 | tf_op jit(solution)/shard_map/ppermute | solution.py:15
  90.0 22.4 %collective-permute-start.10 = (bf16[768,512]{1,0:T(8,128)(2,1)}, bf16[768,512]{1,0:T(8,128)(2,1)}, u32[]{:S(2)}, u32[]{:S(2)}) collective-permute-start(bf16[768,512]{1,0:T(8,128)(2,1)} %copy-done.4), channel_id=1, source_target_pairs={{0,1},{1,0},{2,3},{3,2},{4,5},{5,4},{6,7},{7,6},{8,9},{9,8},{10,11... | collective-permute-start | bytes 2359304 | tf_op jit(solution)/shard_map/ppermute | solution.py:15
  91.1 12.0 %collective-permute-start.4 = (bf16[384,512]{1,0:T(8,128)(2,1)S(1)}, bf16[384,512]{1,0:T(8,128)(2,1)}, u32[]{:S(2)}, u32[]{:S(2)}) collective-permute-start(bf16[384,512]{1,0:T(8,128)(2,1)S(1)} %slice.24), channel_id=1, source_target_pairs={{0,2},{1,3},{2,0},{3,1},{4,6},{5,7},{6,4},{7,5},{8,10},{9,11},{10,... | collective-permute-start | bytes 1179656 | tf_op jit(solution)/shard_map/ppermute | solution.py:15
  95.1 15.7 %collective-permute-start.5 = (bf16[384,512]{1,0:T(8,128)(2,1)S(1)}, bf16[384,512]{1,0:T(8,128)(2,1)}, u32[]{:S(2)}, u32[]{:S(2)}) collective-permute-start(bf16[384,512]{1,0:T(8,128)(2,1)S(1)} %slice.25), channel_id=1, source_target_pairs={{0,4},{4,0},{8,12},{12,8},{16,20},{20,16},{24,28},{28,24},{32,36},... | collective-permute-start | bytes 1179656 | tf_op jit(solution)/shard_map/ppermute | solution.py:15
  103.1 16.1 %collective-permute-start.6 = (bf16[384,512]{1,0:T(8,128)(2,1)}, bf16[384,512]{1,0:T(8,128)(2,1)}, u32[]{:S(2)}, u32[]{:S(2)}) collective-permute-start(bf16[384,512]{1,0:T(8,128)(2,1)} %collective-permute-done.4.mine_low), channel_id=1, source_target_pairs={{0,1},{1,0},{2,3},{3,2},{4,5},{5,4},{6,7},{7,6},{8,9},{9,8},{10,11... | collective-permute-start | bytes 1179656 | tf_op jit(solution)/shard_map/ppermute | solution.py:15
  110.8 8.4 %collective-permute-start.7 = (bf16[384,512]{1,0:T(8,128)(2,1)}, bf16[384,512]{1,0:T(8,128)(2,1)}, u32[]{:S(2)}, u32[]{:S(2)}) collective-permute-start(bf16[384,512]{1,0:T(8,128)(2,1)} %collective-permute-done.5.mine_high), channel_id=1, source_target_pairs={{0,1},{1,0},{2,3},{3,2},{4,5},{5,4},{6,7},{7,6},{8,9},{9,8},{10,11... | collective-permute-start | bytes 1179656 | tf_op jit(solution)/shard_map/ppermute | solution.py:15
  126.4 2.6 %collective-permute-start.14 = (bf16[768,512]{1,0:T(8,128)(2,1)}, bf16[768,512]{1,0:T(8,128)(2,1)S(1)}, u32[]{:S(2)}, u32[]{:S(2)}) collective-permute-start(bf16[768,512]{1,0:T(8,128)(2,1)} %get-tuple-element.37), channel_id=1, source_target_pairs={{0,1},{1,0},{2,3},{3,2},{4,5},{5,4},{6,7},{7,6},{8,9},{9,8},{10,11... | collective-permute-start | bytes 2359304 | tf_op jit(solution)/shard_map/ppermute | solution.py:15
  126.5 6.4 %collective-permute-start.12 = (bf16[768,512]{1,0:T(8,128)(2,1)}, bf16[768,512]{1,0:T(8,128)(2,1)S(1)}, u32[]{:S(2)}, u32[]{:S(2)}) collective-permute-start(bf16[768,512]{1,0:T(8,128)(2,1)} %get-tuple-element.33), channel_id=1, source_target_pairs={{0,1},{1,0},{2,3},{3,2},{4,5},{5,4},{6,7},{7,6},{8,9},{9,8},{10,11... | collective-permute-start | bytes 2359304 | tf_op jit(solution)/shard_map/ppermute | solution.py:15
  127.0 5.9 %collective-permute-start.13 = (bf16[768,512]{1,0:T(8,128)(2,1)}, bf16[768,512]{1,0:T(8,128)(2,1)S(1)}, u32[]{:S(2)}, u32[]{:S(2)}) collective-permute-start(bf16[768,512]{1,0:T(8,128)(2,1)} %get-tuple-element.35), channel_id=1, source_target_pairs={{0,1},{1,0},{2,3},{3,2},{4,5},{5,4},{6,7},{7,6},{8,9},{9,8},{10,11... | collective-permute-start | bytes 2359304 | tf_op jit(solution)/shard_map/ppermute | solution.py:15
  129.3 12.2 %collective-permute-start.15 = (bf16[384,512]{1,0:T(8,128)(2,1)S(1)}, bf16[384,512]{1,0:T(8,128)(2,1)S(1)}, u32[]{:S(2)}, u32[]{:S(2)}) collective-permute-start(bf16[384,512]{1,0:T(8,128)(2,1)S(1)} %get-tuple-element.50), channel_id=1, source_target_pairs={{0,2},{1,3},{2,0},{3,1},{4,6},{5,7},{6,4},{7,5},{8,10},{9,11},{10,... | collective-permute-start | bytes 1179656 | tf_op jit(solution)/shard_map/ppermute | solution.py:15
  129.9 11.6 %collective-permute-start.16 = (bf16[384,512]{1,0:T(8,128)(2,1)S(1)}, bf16[384,512]{1,0:T(8,128)(2,1)S(1)}, u32[]{:S(2)}, u32[]{:S(2)}) collective-permute-start(bf16[384,512]{1,0:T(8,128)(2,1)S(1)} %get-tuple-element.49), channel_id=1, source_target_pairs={{0,4},{4,0},{8,12},{12,8},{16,20},{20,16},{24,28},{28,24},{32,36},... | collective-permute-start | bytes 1179656 | tf_op jit(solution)/shard_map/ppermute | solution.py:15
  132.2 29.5 %collective-permute-start.11 = (bf16[768,512]{1,0:T(8,128)(2,1)}, bf16[768,512]{1,0:T(8,128)(2,1)}, u32[]{:S(2)}, u32[]{:S(2)}) collective-permute-start(bf16[768,512]{1,0:T(8,128)(2,1)} %get-tuple-element.31), channel_id=1, source_target_pairs={{0,1},{1,0},{2,3},{3,2},{4,5},{5,4},{6,7},{7,6},{8,9},{9,8},{10,11... | collective-permute-start | bytes 2359304 | tf_op jit(solution)/shard_map/ppermute | solution.py:15
  142.9 19.6 %collective-permute-start.17 = (bf16[768,512]{1,0:T(8,128)(2,1)}, bf16[768,512]{1,0:T(8,128)(2,1)}, u32[]{:S(2)}, u32[]{:S(2)}) collective-permute-start(bf16[768,512]{1,0:T(8,128)(2,1)} %get-tuple-element.38), channel_id=1, source_target_pairs={{0,4},{4,0},{8,12},{12,8},{16,20},{20,16},{24,28},{28,24},{32,36},... | collective-permute-start | bytes 2359304 | tf_op jit(solution)/shard_map/ppermute | solution.py:15
  145.3 19.6 %collective-permute-start.18 = (bf16[768,512]{1,0:T(8,128)(2,1)}, bf16[768,512]{1,0:T(8,128)(2,1)}, u32[]{:S(2)}, u32[]{:S(2)}) collective-permute-start(bf16[768,512]{1,0:T(8,128)(2,1)} %get-tuple-element.39), channel_id=1, source_target_pairs={{0,2},{1,3},{2,0},{3,1},{4,6},{5,7},{6,4},{7,5},{8,10},{9,11},{10,... | collective-permute-start | bytes 2359304 | tf_op jit(solution)/shard_map/ppermute | solution.py:15
  167.8 28.1 %all-to-all-start.2 = ((bf16[32,24,512]{2,1,0:T(8,128)(2,1)}), bf16[32,24,512]{2,1,0:T(8,128)(2,1)}, u32[]{:S(2)}, u32[]{:S(2)}) async-start(bf16[32,24,512]{2,1,0:T(8,128)(2,1)} %bitcast.24), calls=%async_computation.2 | async-start | bytes 1572864 | tf_op jit(solution)/shard_map/all_to_all | solution.py:347
  200.9 7.1 %collective-permute-start.20 = (bf16[128,1152]{1,0:T(8,128)(2,1)S(1)}, bf16[128,1152]{1,0:T(8,128)(2,1)S(1)}, u32[]{:S(2)}, u32[]{:S(2)}) collective-permute-start(bf16[128,1152]{1,0:T(8,128)(2,1)S(1)} %get-tuple-element.44.own_ref), channel_id=1, source_target_pairs={{0,2},{1,3},{2,0},{3,1},{4,6},{5,7},{6,4},{7,5},{8,10},{9,11},{10,... | collective-permute-start | bytes 884744 | tf_op jit(solution)/shard_map/ppermute | solution.py:15
  201.5 12.1 %collective-permute-start.19 = (bf16[128,1152]{1,0:T(8,128)(2,1)S(1)}, bf16[128,1152]{1,0:T(8,128)(2,1)S(1)}, u32[]{:S(2)}, u32[]{:S(2)}) collective-permute-start(bf16[128,1152]{1,0:T(8,128)(2,1)S(1)} %get-tuple-element.44.own_ref), channel_id=1, source_target_pairs={{0,1},{1,0},{2,3},{3,2},{4,5},{5,4},{6,7},{7,6},{8,9},{9,8},{10,11... | collective-permute-start | bytes 884744 | tf_op jit(solution)/shard_map/ppermute | solution.py:15
  207.9 6.9 %collective-permute-start.21 = (bf16[128,1152]{1,0:T(8,128)(2,1)S(1)}, bf16[128,1152]{1,0:T(8,128)(2,1)S(1)}, u32[]{:S(2)}, u32[]{:S(2)}) collective-permute-start(bf16[128,1152]{1,0:T(8,128)(2,1)S(1)} %collective-permute-done.20.y_ref), channel_id=1, source_target_pairs={{0,1},{1,0},{2,3},{3,2},{4,5},{5,4},{6,7},{7,6},{8,9},{9,8},{10,11... | collective-permute-start | bytes 884744 | tf_op jit(solution)/shard_map/ppermute | solution.py:15
  (23 other events, 124.1 us)

commit v4 on v3

--- a/solution.py
+++ b/solution.py
@@ -84,7 +84,8 @@
         outputs[i][...] = jnp.dot(act, columns, preferred_element_type=jnp.float32).astype(jnp.bfloat16)
 
 
-def turn(mine_x, theirs_x, mine_y, theirs_y, low_ref, high_ref, x_ref, y_ref):
+def turn(mine_x, theirs_x, mine_y, theirs_y, low_ref, high_ref, *refs):
+    x_ref, y_ref = refs[-2:]
     half = low_ref.shape[0]
     for mine, theirs, far, part, out in ((mine_x, theirs_x, low_ref, 0, x_ref), (mine_y, theirs_y, high_ref, 1, y_ref)):
         for i in range(2):
@@ -274,14 +275,14 @@
     head_dim = kv_weight.shape[2]
     flat_weight = kv_weight.reshape(model_width, 2 * head_dim)
     middle = total_slots // 2
-    landed = held_until(landed, crossed, order, halves, flat_weight)
+    landed = held_until(landed, crossed, order)
     from_y = swapped(landed, "tp", 1)
     from_x = held_until(swapped(landed, "grp", 0), from_y)
     landed_core = swapped(landed, "tp", 0)
     mine = (landed, from_x, from_y)
     theirs = (landed_core, swapped(from_x, "tp", 0), swapped(from_y, "tp", 0))
-    last_mine = (swapped(from_x[:middle], "tp", 1), swapped(from_y[middle:], "grp", 0))
-    last_theirs = tuple(swapped(x, "tp", 0) for x in last_mine)
+    by_y = 2 * total_slots // 3
+    last_mine = (swapped(from_x[:by_y], "tp", 1), swapped(from_y[by_y:], "grp", 0))
 
     order = held_until(order, landed_core)
     ordered = crossed.at[order[0]].get(mode="promise_in_bounds")
@@ -304,6 +305,8 @@
         name="early_units",
         flops=3 * total_slots * model_width * unit_count,
     )
+    last_mine = tuple(held_until(x, *sums) for x in last_mine)
+    last_theirs = tuple(swapped(x, "tp", 0) for x in last_mine)
     sums = call(
         late_units,
         (shape((total_slots, eighth), bf16),) * 8,
@@ -333,7 +336,8 @@
     to_x, to_y = call(
         turn,
         (shape((total_slots, eighth), bf16),) * 2,
-        (sums[1], from_core[1], sums[2], from_core[2], low, high),
+        (sums[1], from_core[1], sums[2], from_core[2], low, high, halves, flat_weight),
+        away=2,
         name="turn",
     )
     sum_x, sum_y = swapped(to_x, "grp", 0), swapped(to_y, "tp", 1)

time: 223 us -> 221 us (level)
  waiting for transfers between devices: 89.7 us -> 83 us
  starting transfers between devices: 63.9 us -> 67.6 us
    ppermute x22, waiting for transfers between devices: 72 us -> 65 us  [swapped(): lax.ppermute(x, axis, [(i, i ^ 1 << bit) for i in range(lax.axis_size(axi...]
    ppermute x22, starting transfers between devices: 34.4 us -> 37.5 us  [swapped(): lax.ppermute(x, axis, [(i, i ^ 1 << bit) for i in range(lax.axis_size(axi...]
    all_to_all x1, starting transfers between devices: 9 us -> 11.4 us  [local(): lax.all_to_all(ordered, 'grp', split_axis=0, concat_axis=0, tiled=True)]
    unnamed x62 -> x64, local copies, waits for them, and re-layouts: 11.7 us -> 13 us
  transfers between devices with their start and end apart: 25 -> 25, of which waited for: 12 -> 12; matrix products, arithmetic and copies ran while one was open for 8% -> 9% of each run, Pallas kernels for 11% -> 11%
where the time goes in v4:
time: 221 us; the launch traced here: 220 us
  waiting for transfers between devices  83 us (38%)
  starting transfers between devices  67.6 us (31%)
  Pallas kernels  37.4 us (17%)
  local copies, waits for them, and re-layouts  24.4 us (11%)
  other arithmetic  6.67 us (3%)
    ppermute x22, waiting for transfers between devices, swapped(): lax.ppermute(x, axis, [(i, i ^ 1 << bit) for i in range(lax.axis_size(axi...  65 us
    ppermute x22, starting transfers between devices, swapped(): lax.ppermute(x, axis, [(i, i ^ 1 << bit) for i in range(lax.axis_size(axi...  37.5 us
    pallas_call x8, Pallas kernels, call(): pl.pallas_call(kernel, out_shape=out_shape, in_specs=[pl.BlockSpec(memory...  37.4 us
    all_to_all x1, waiting for transfers between devices, local(): lax.all_to_all(summed.reshape(peer_count, capacity, eighth), 'grp', split...  18 us
    unnamed x64, local copies, waits for them, and re-layouts  13 us
    all_to_all x1, starting transfers between devices, local(): lax.all_to_all(ordered, 'grp', split_axis=0, concat_axis=0, tiled=True)  11.4 us
    all_to_all x1, starting transfers between devices, local(): lax.all_to_all(packed, 'grp', split_axis=0, concat_axis=0, tiled=True)  11 us
    all_to_all x1, starting transfers between devices, local(): lax.all_to_all(summed.reshape(peer_count, capacity, eighth), 'grp', split...  7.69 us
  transfers between devices with their start and end apart: 25, of which 12 were waited for; matrix products, arithmetic and copies ran while one was open for 9% of the time, Pallas kernels for 11%

profile of v4, /device:TPU:1, one launch (start us, length us, event | category | flops | bytes accessed | tf_op | source)
XLA Modules:
  0.0 220.5 jit_solution(4457406302366685406)
XLA Ops:
  0.7 2.2 %collective-permute-start = (bf16[32,2,128,128]{3,2,1,0:T(8,128)(2,1)}, bf16[32,2,128,128]{3,2,1,0:T(8,128)(2,1)S(1)}, u32[]{:S(2)}, u32[]{:S(2)}) collective-permute-start(bf16[32,2,128,128]{3,2,1,0:T(8,128)(2,1)} %bitcast.52), channel_id=1, source_target_pairs={{0,128},{128,0},{1,129},{129,1},{2,130},{130,2},{3,131},{131,3},{4... | collective-permute-start | bytes 6291464 | tf_op jit(solution)/shard_map/ppermute | solution.py:15
  7.1 11.0 %all-to-all-start = ((bf16[32,24,512]{2,1,0:T(8,128)(2,1)}), bf16[32,24,512]{2,1,0:T(8,128)(2,1)S(1)}, u32[]{:S(2)}, u32[]{:S(2)}) async-start(bf16[32,24,512]{2,1,0:T(8,128)(2,1)} %get-tuple-element.27), calls=%async_computation | async-start | bytes 1572864 | tf_op jit(solution)/shard_map/all_to_all | solution.py:254
  18.4 28.9 %collective-permute-done.1.refs_2_.refs_0_ = s32[1,32]{1,0:T(1,128)S(1)} collective-permute-done((s32[1,32]{1,0:T(1,128)S(1)}, s32[1,32]{1,0:T(1,128)S(1)}, u32[]{:S(2)}, u32[]{:S(2)}) %collective-permute-start.1) | collective-permute-done | bytes 160 | tf_op jit(solution)/shard_map/ppermute | solution.py:15
  48.9 3.9 %collective-permute-start.3 = (bf16[768,512]{1,0:T(8,128)(2,1)}, bf16[768,512]{1,0:T(8,128)(2,1)S(1)}, u32[]{:S(2)}, u32[]{:S(2)}) collective-permute-start(bf16[768,512]{1,0:T(8,128)(2,1)} %held_until.5.refs_0_), channel_id=1, source_target_pairs={{0,2},{1,3},{2,0},{3,1},{4,6},{5,7},{6,4},{7,5},{8,10},{9,11},{10,... | collective-permute-start | bytes 2359304 | tf_op jit(solution)/shard_map/ppermute | solution.py:15
  54.0 2.2 collective-permute-start.5
  56.2 12.9 %collective-permute-done.3.refs_1_.refs_2_ = bf16[768,512]{1,0:T(8,128)(2,1)S(1)} collective-permute-done((bf16[768,512]{1,0:T(8,128)(2,1)}, bf16[768,512]{1,0:T(8,128)(2,1)S(1)}, u32[]{:S(2)}, u32[]{:S(2)}) %collective-permute-start.3) | collective-permute-done | bytes 786464 | tf_op jit(solution)/shard_map/ppermute | solution.py:15
  71.1 2.8 %collective-permute-start.6 = (bf16[768,512]{1,0:T(8,128)(2,1)}, bf16[768,512]{1,0:T(8,128)(2,1)}, u32[]{:S(2)}, u32[]{:S(2)}) collective-permute-start(bf16[768,512]{1,0:T(8,128)(2,1)} %held_until.6.refs_1_), channel_id=1, source_target_pairs={{0,1},{1,0},{2,3},{3,2},{4,5},{5,4},{6,7},{7,6},{8,9},{9,8},{10,11... | collective-permute-start | bytes 2359304 | tf_op jit(solution)/shard_map/ppermute | solution.py:15
  75.5 3.8 %gather_fusion = bf16[32,2,128,128]{3,2,1,0:T(8,128)(2,1)} fusion(bf16[32,2,128,128]{3,2,1,0:T(8,128)(2,1)} %copy-done.23, s32[1024]{0:T(1024)S(1)} %pad_clamp_fusion), kind=kCustom, calls=%fused_computation | custom fusion | bytes 4194432 | tf_op jit(solution)/shard_map/gather | solution.py:288
  79.3 11.4 %all-to-all-start.1 = ((bf16[32,2,128,128]{3,2,1,0:T(8,128)(2,1)}), bf16[32,2,128,128]{3,2,1,0:T(8,128)(2,1)}, u32[]{:S(2)}, u32[]{:S(2)}) async-start(bf16[32,2,128,128]{3,2,1,0:T(8,128)(2,1)} %gather_fusion), calls=%async_computation.1 | async-start | bytes 4194304 | tf_op jit(solution)/shard_map/all_to_all | solution.py:289
  91.6 2.4 %collective-permute-start.4 = (bf16[512,512]{1,0:T(8,128)(2,1)}, bf16[512,512]{1,0:T(8,128)(2,1)}, u32[]{:S(2)}, u32[]{:S(2)}) collective-permute-start(bf16[512,512]{1,0:T(8,128)(2,1)} %slice.24), channel_id=1, source_target_pairs={{0,2},{1,3},{2,0},{3,1},{4,6},{5,7},{6,4},{7,5},{8,10},{9,11},{10,... | collective-permute-start | bytes 1572872 | tf_op jit(solution)/shard_map/ppermute | solution.py:15
  96.7 5.0 %early_units.1 = (f32[768,192]{1,0:T(8,128)S(1)}, f32[768,192]{1,0:T(8,128)S(1)}) custom-call(s32[8]{0:T(128)S(1)} %stack.41.blocks_ref, bf16[768,512]{1,0:T(8,128)(2,1)S(1)} %copy-done.5, bf16[768,512]{1,0:T(8,128)(2,1)S(1)} %copy-done.7, bf16[768,512]{1,0:T(8,128)(2,1)S(1)} %copy-done.9, bf16[768,512]{1,0:T(8,128)(2,1)S(1)} %copy-done.15, ...), custom_call_target="tpu_custom_call" | custom-call | flops 1811939328 | bytes 9044000 | tf_op jit(solution)/shard_map/early_units/pallas_call | solution.py:176
  103.5 2.6 %collective-permute-done.4.refs_0_ = bf16[512,512]{1,0:T(8,128)(2,1)} collective-permute-done((bf16[512,512]{1,0:T(8,128)(2,1)}, bf16[512,512]{1,0:T(8,128)(2,1)}, u32[]{:S(2)}, u32[]{:S(2)}) %collective-permute-start.4) | collective-permute-done | bytes 524320 | tf_op jit(solution)/shard_map/ppermute | solution.py:15
  106.1 1.7 collective-permute-start.9
  108.2 2.7 %collective-permute-done.8.refs_0_ = bf16[256,512]{1,0:T(8,128)(2,1)S(1)} collective-permute-done((bf16[256,512]{1,0:T(8,128)(2,1)}, bf16[256,512]{1,0:T(8,128)(2,1)S(1)}, u32[]{:S(2)}, u32[]{:S(2)}) %collective-permute-start.8) | collective-permute-done | bytes 262176 | tf_op jit(solution)/shard_map/ppermute | solution.py:15
  113.0 2.0 gather_fusion.1
  115.2 7.0 %late_units.1 = (bf16[768,512]{1,0:T(8,128)(2,1)S(1)}, bf16[768,512]{1,0:T(8,128)(2,1)S(1)}, bf16[768,512]{1,0:T(8,128)(2,1)S(1)}, bf16[768,512]{1,0:T(8,128)(2,...) custom-call(s32[8]{0:T(128)S(1)} %stack.41.blocks_ref, ...), custom_call_target="tpu_custom_call" | custom-call | flops 1811939328 | bytes 15859744 | tf_op jit(solution)/shard_map/late_units/pallas_call | solution.py:176
  125.0 2.0 collective-permute-start.15
  127.0 1.6 copy.45
  130.2 7.1 %collective-permute-done.15.low_ref = bf16[384,512]{1,0:T(8,128)(2,1)S(1)} collective-permute-done((bf16[384,512]{1,0:T(8,128)(2,1)S(1)}, bf16[384,512]{1,0:T(8,128)(2,1)S(1)}, u32[]{:S(2)}, u32[]{:S(2)}) %collective-permute-start.15) | collective-permute-done | bytes 393248 | tf_op jit(solution)/shard_map/ppermute | solution.py:15
  137.3 3.9 %collective-permute-done.16.high_ref = bf16[384,512]{1,0:T(8,128)(2,1)S(1)} collective-permute-done((bf16[384,512]{1,0:T(8,128)(2,1)S(1)}, bf16[384,512]{1,0:T(8,128)(2,1)S(1)}, u32[]{:S(2)}, u32[]{:S(2)}) %collective-permute-start.16) | collective-permute-done | bytes 393248 | tf_op jit(solution)/shard_map/ppermute | solution.py:15
  144.1 1.9 collective-permute-start.18
  146.5 3.8 %pad_maximum_fusion.pool_ref = bf16[48,2,128,128]{3,2,1,0:T(8,128)(2,1)} fusion(bf16[32,2,128,128]{3,2,1,0:T(8,128)(2,1)} %all-to-all-done.1, bf16[16,2,128,128]{3,2,1,0:T(8,128)(2,1)} %bitcast.51), kind=kLoop, calls=%fused_computation.2 | loop fusion | flops 1572864 | bytes 6291456 | tf_op jit(solution)/shard_map/concatenate | solution.py:323
  150.3 10.2 %cached_attention.1 = (f32[32,64,128]{2,1,0:T(8,128)S(1)}, f32[32,64,128]{2,1,0:T(8,128)S(1)}, f32[32,64,128]{2,1,0:T(8,128)S(1)}) custom-call(s32[128]{0:T(128)S(1)} %reshape.211.table_ref, s32[32]{0:T(128)S(1)} %copy-done.22, bf16[32,64,128]{2,1,0:T(8,128)(2,1)S(1)} %reshape.212.query_ref, bf16[48,2,128,128]{3,2,1,0:T(8,128)(2,1)} %pad_maximum_fusion.pool_ref), custom_call_target="tpu_custom_call" | custom-call | flops 536870912 | bytes 6816384 | tf_op jit(solution)/shard_map/cached_attention/pallas_call | solution.py:176
  161.5 2.6 %collective-permute-done.18.y_ref = bf16[768,512]{1,0:T(8,128)(2,1)} collective-permute-done((bf16[768,512]{1,0:T(8,128)(2,1)}, bf16[768,512]{1,0:T(8,128)(2,1)}, u32[]{:S(2)}, u32[]{:S(2)}) %collective-permute-start.18) | collective-permute-done | bytes 786464 | tf_op jit(solution)/shard_map/ppermute | solution.py:15
  164.2 2.9 %join.1 = bf16[768,512]{1,0:T(8,128)(2,1)} custom-call(bf16[768,512]{1,0:T(8,128)(2,1)S(1)} %get-tuple-element.30.mine_ref, bf16[768,512]{1,0:T(8,128)(2,1)} %collective-permute-done.11.theirs_ref, bf16[768,512]{1,0:T(8,128)(2,1)} %collective-permute-done.17.x_ref, bf16[768,512]{1,0:T(8,128)(2,1)} %collective-permute-done.18.y_ref, ...), custom_call_target="tpu_custom_call" | custom-call | bytes 7077888 | tf_op jit(solution)/shard_map/join/pallas_call | solution.py:176
  167.1 7.7 %all-to-all-start.2 = ((bf16[32,24,512]{2,1,0:T(8,128)(2,1)}), bf16[32,24,512]{2,1,0:T(8,128)(2,1)}, u32[]{:S(2)}, u32[]{:S(2)}) async-start(bf16[32,24,512]{2,1,0:T(8,128)(2,1)} %bitcast.24), calls=%async_computation.2 | async-start | bytes 1572864 | tf_op jit(solution)/shard_map/all_to_all | solution.py:351
  176.6 18.0 %all-to-all-done.2 = bf16[32,24,512]{2,1,0:T(8,128)(2,1)} async-done(((bf16[32,24,512]{2,1,0:T(8,128)(2,1)}), bf16[32,24,512]{2,1,0:T(8,128)(2,1)}, u32[]{:S(2)}, u32[]{:S(2)}) %all-to-all-start.2) | async-done | bytes 786464 | tf_op jit(solution)/shard_map/all_to_all | solution.py:351
  196.9 2.6 %finish.1 = (f32[128,1024]{1,0:T(8,128)}, bf16[128,1152]{1,0:T(8,128)(2,1)S(1)}) custom-call(s32[1]{0:T(128)} %bitcast.part_ref, bf16[2,256,768]{2,1,0:T(8,128)(2,1)S(1)} %copy-done.3, bf16[768,512]{1,0:T(8,128)(2,1)} %bitcast.25.returned_ref, bf16[128,4096]{1,0:T(8,128)(2,1)S(1)} %copy-done.13, bf16[1,4096]{1,0:T(2,128)(2,1)S(1)} %reshape.215.gain_ref, ...), custom_call_target="tpu_custom_call" | custom-call | bytes 6594564 | tf_op jit(solution)/shard_map/finish/pallas_call | solution.py:176
  199.5 2.5 %collective-permute-start.20 = (bf16[128,1152]{1,0:T(8,128)(2,1)S(1)}, bf16[128,1152]{1,0:T(8,128)(2,1)S(1)}, u32[]{:S(2)}, u32[]{:S(2)}) collective-permute-start(bf16[128,1152]{1,0:T(8,128)(2,1)S(1)} %get-tuple-element.44.own_ref), channel_id=1, source_target_pairs={{0,2},{1,3},{2,0},{3,1},{4,6},{5,7},{6,4},{7,5},{8,10},{9,11},{10,... | collective-permute-start | bytes 884744 | tf_op jit(solution)/shard_map/ppermute | solution.py:15
  202.0 4.2 %collective-permute-start.19 = (bf16[128,1152]{1,0:T(8,128)(2,1)S(1)}, bf16[128,1152]{1,0:T(8,128)(2,1)S(1)}, u32[]{:S(2)}, u32[]{:S(2)}) collective-permute-start(bf16[128,1152]{1,0:T(8,128)(2,1)S(1)} %get-tuple-element.44.own_ref), channel_id=1, source_target_pairs={{0,1},{1,0},{2,3},{3,2},{4,5},{5,4},{6,7},{7,6},{8,9},{9,8},{10,11... | collective-permute-start | bytes 884744 | tf_op jit(solution)/shard_map/ppermute | solution.py:15
  206.6 5.5 %collective-permute-start.21 = (bf16[128,1152]{1,0:T(8,128)(2,1)S(1)}, bf16[128,1152]{1,0:T(8,128)(2,1)S(1)}, u32[]{:S(2)}, u32[]{:S(2)}) collective-permute-start(bf16[128,1152]{1,0:T(8,128)(2,1)S(1)} %collective-permute-done.20.y_ref), channel_id=1, source_target_pairs={{0,1},{1,0},{2,3},{3,2},{4,5},{5,4},{6,7},{7,6},{8,9},{9,8},{10,11... | collective-permute-start | bytes 884744 | tf_op jit(solution)/shard_map/ppermute | solution.py:15
  213.3 6.6 %last_step.1 = (bf16[128,256]{1,0:T(8,128)(2,1)S(1)}, bf16[128,2048]{1,0:T(8,128)(2,1)}) custom-call(s32[1]{0:T(128)} %bitcast.part_ref, bf16[128,1152]{1,0:T(8,128)(2,1)S(1)} %get-tuple-element.44.own_ref, bf16[128,1152]{1,0:T(8,128)(2,1)S(1)} %collective-permute-done.19.core_ref, bf16[128,1152]{1,0:T(8,128)(2,1)S(1)} %collective-permute-done.20.y_ref, ...), custom_call_target="tpu_custom_call" | custom-call | bytes 7536644 | tf_op jit(solution)/shard_map/last_step/pallas_call | solution.py:176
  (130 shorter events, 34.0 us)
Async XLA Ops:
  0.6 107.1 %copy-start = (bf16[4096,16]{0,1:T(8,128)(2,1)S(1)}, bf16[4096,16]{0,1:T(8,128)(2,1)}, u32[]{:S(2)}) copy-start(bf16[4096,16]{0,1:T(8,128)(2,1)} %param.17) | copy-start | bytes 393220
  0.6 17.5 %copy-start.30 = (s32[1,32]{1,0:T(1,128)S(1)}, s32[1,32]{1,0:T(1,128)}, u32[]{:S(2)}) copy-start(s32[1,32]{1,0:T(1,128)} %param.27) | copy-start | bytes 388
  0.7 46.7 %collective-permute-start = (bf16[32,2,128,128]{3,2,1,0:T(8,128)(2,1)}, bf16[32,2,128,128]{3,2,1,0:T(8,128)(2,1)S(1)}, u32[]{:S(2)}, u32[]{:S(2)}) collective-permute-start(bf16[32,2,128,128]{3,2,1,0:T(8,128)(2,1)} %bitcast.52), channel_id=1, source_target_pairs={{0,128},{128,0},{1,129},{129,1},{2,130},{130,2},{3,131},{131,3},{4... | collective-permute-start | bytes 6291464 | tf_op jit(solution)/shard_map/ppermute | solution.py:15
  7.1 40.2 %all-to-all-start = ((bf16[32,24,512]{2,1,0:T(8,128)(2,1)}), bf16[32,24,512]{2,1,0:T(8,128)(2,1)S(1)}, u32[]{:S(2)}, u32[]{:S(2)}) async-start(bf16[32,24,512]{2,1,0:T(8,128)(2,1)} %get-tuple-element.27), calls=%async_computation | async-start | bytes 1572864 | tf_op jit(solution)/shard_map/all_to_all | solution.py:254
  18.1 29.2 %collective-permute-start.1 = (s32[1,32]{1,0:T(1,128)S(1)}, s32[1,32]{1,0:T(1,128)S(1)}, u32[]{:S(2)}, u32[]{:S(2)}) collective-permute-start(s32[1,32]{1,0:T(1,128)S(1)} %copy-done.30), channel_id=1, source_target_pairs={{0,128},{128,0},{1,129},{129,1},{2,130},{130,2},{3,131},{131,3},{4... | collective-permute-start | bytes 392 | tf_op jit(solution)/shard_map/ppermute | solution.py:15
  48.9 20.2 %collective-permute-start.3 = (bf16[768,512]{1,0:T(8,128)(2,1)}, bf16[768,512]{1,0:T(8,128)(2,1)S(1)}, u32[]{:S(2)}, u32[]{:S(2)}) collective-permute-start(bf16[768,512]{1,0:T(8,128)(2,1)} %held_until.5.refs_0_), channel_id=1, source_target_pairs={{0,2},{1,3},{2,0},{3,1},{4,6},{5,7},{6,4},{7,5},{8,10},{9,11},{10,... | collective-permute-start | bytes 2359304 | tf_op jit(solution)/shard_map/ppermute | solution.py:15
  52.8 17.4 %collective-permute-start.2 = (bf16[768,512]{1,0:T(8,128)(2,1)}, bf16[768,512]{1,0:T(8,128)(2,1)S(1)}, u32[]{:S(2)}, u32[]{:S(2)}) collective-permute-start(bf16[768,512]{1,0:T(8,128)(2,1)} %held_until.5.refs_0_), channel_id=1, source_target_pairs={{0,4},{4,0},{8,12},{12,8},{16,20},{20,16},{24,28},{28,24},{32,36},... | collective-permute-start | bytes 2359304 | tf_op jit(solution)/shard_map/ppermute | solution.py:15
  54.0 19.9 %collective-permute-start.5 = (bf16[768,512]{1,0:T(8,128)(2,1)}, bf16[768,512]{1,0:T(8,128)(2,1)S(1)}, u32[]{:S(2)}, u32[]{:S(2)}) collective-permute-start(bf16[768,512]{1,0:T(8,128)(2,1)} %held_until.5.refs_0_), channel_id=1, source_target_pairs={{0,1},{1,0},{2,3},{3,2},{4,5},{5,4},{6,7},{7,6},{8,9},{9,8},{10,11... | collective-permute-start | bytes 2359304 | tf_op jit(solution)/shard_map/ppermute | solution.py:15
  71.1 25.6 %collective-permute-start.6 = (bf16[768,512]{1,0:T(8,128)(2,1)}, bf16[768,512]{1,0:T(8,128)(2,1)}, u32[]{:S(2)}, u32[]{:S(2)}) collective-permute-start(bf16[768,512]{1,0:T(8,128)(2,1)} %held_until.6.refs_1_), channel_id=1, source_target_pairs={{0,1},{1,0},{2,3},{3,2},{4,5},{5,4},{6,7},{7,6},{8,9},{9,8},{10,11... | collective-permute-start | bytes 2359304 | tf_op jit(solution)/shard_map/ppermute | solution.py:15
  73.9 22.8 %collective-permute-start.7 = (bf16[768,512]{1,0:T(8,128)(2,1)}, bf16[768,512]{1,0:T(8,128)(2,1)}, u32[]{:S(2)}, u32[]{:S(2)}) collective-permute-start(bf16[768,512]{1,0:T(8,128)(2,1)} %copy-done.8), channel_id=1, source_target_pairs={{0,1},{1,0},{2,3},{3,2},{4,5},{5,4},{6,7},{7,6},{8,9},{9,8},{10,11... | collective-permute-start | bytes 2359304 | tf_op jit(solution)/shard_map/ppermute | solution.py:15
  79.3 14.7 %copy-start.25 = (bf16[4096]{0:T(1024)(128)(2,1)S(1)}, bf16[4096]{0:T(1024)(128)(2,1)}, u32[]{:S(2)}) copy-start(bf16[4096]{0:T(1024)(128)(2,1)} %param.16) | copy-start | bytes 24580
  79.3 15.5 %copy-start.9 = (bf16[768,512]{1,0:T(8,128)(2,1)S(1)}, bf16[768,512]{1,0:T(8,128)(2,1)}, u32[]{:S(2)}) copy-start(bf16[768,512]{1,0:T(8,128)(2,1)} %copy-done.8) | copy-start | bytes 2359300
  79.3 17.4 %copy-start.5 = (bf16[768,512]{1,0:T(8,128)(2,1)S(1)}, bf16[768,512]{1,0:T(8,128)(2,1)}, u32[]{:S(2)}) copy-start(bf16[768,512]{1,0:T(8,128)(2,1)} %held_until.5.refs_0_) | copy-start | bytes 2359300
  79.3 17.4 %copy-start.15 = (bf16[768,512]{1,0:T(8,128)(2,1)S(1)}, bf16[768,512]{1,0:T(8,128)(2,1)}, u32[]{:S(2)}) copy-start(bf16[768,512]{1,0:T(8,128)(2,1)} %copy-done.14) | copy-start | bytes 2359300
  79.3 67.2 %all-to-all-start.1 = ((bf16[32,2,128,128]{3,2,1,0:T(8,128)(2,1)}), bf16[32,2,128,128]{3,2,1,0:T(8,128)(2,1)}, u32[]{:S(2)}, u32[]{:S(2)}) async-start(bf16[32,2,128,128]{3,2,1,0:T(8,128)(2,1)} %gather_fusion), calls=%async_computation.1 | async-start | bytes 4194304 | tf_op jit(solution)/shard_map/all_to_all | solution.py:289
  91.6 14.5 %collective-permute-start.4 = (bf16[512,512]{1,0:T(8,128)(2,1)}, bf16[512,512]{1,0:T(8,128)(2,1)}, u32[]{:S(2)}, u32[]{:S(2)}) collective-permute-start(bf16[512,512]{1,0:T(8,128)(2,1)} %slice.24), channel_id=1, source_target_pairs={{0,2},{1,3},{2,0},{3,1},{4,6},{5,7},{6,4},{7,5},{8,10},{9,11},{10,... | collective-permute-start | bytes 1572872 | tf_op jit(solution)/shard_map/ppermute | solution.py:15
  95.5 15.4 %collective-permute-start.8 = (bf16[256,512]{1,0:T(8,128)(2,1)}, bf16[256,512]{1,0:T(8,128)(2,1)S(1)}, u32[]{:S(2)}, u32[]{:S(2)}) collective-permute-start(bf16[256,512]{1,0:T(8,128)(2,1)} %slice.25), channel_id=1, source_target_pairs={{0,4},{4,0},{8,12},{12,8},{16,20},{20,16},{24,28},{28,24},{32,36},... | collective-permute-start | bytes 786440 | tf_op jit(solution)/shard_map/ppermute | solution.py:15
  106.1 9.1 %collective-permute-start.9 = (bf16[512,512]{1,0:T(8,128)(2,1)}, bf16[512,512]{1,0:T(8,128)(2,1)S(1)}, u32[]{:S(2)}, u32[]{:S(2)}) collective-permute-start(bf16[512,512]{1,0:T(8,128)(2,1)} %held_until.7.mine_low), channel_id=1, source_target_pairs={{0,1},{1,0},{2,3},{3,2},{4,5},{5,4},{6,7},{7,6},{8,9},{9,8},{10,11... | collective-permute-start | bytes 1572872 | tf_op jit(solution)/shard_map/ppermute | solution.py:15
  111.6 3.6 %collective-permute-start.10 = (bf16[256,512]{1,0:T(8,128)(2,1)}, bf16[256,512]{1,0:T(8,128)(2,1)S(1)}, u32[]{:S(2)}, u32[]{:S(2)}) collective-permute-start(bf16[256,512]{1,0:T(8,128)(2,1)} %held_until.8.mine_high), channel_id=1, source_target_pairs={{0,1},{1,0},{2,3},{3,2},{4,5},{5,4},{6,7},{7,6},{8,9},{9,8},{10,11... | collective-permute-start | bytes 786440 | tf_op jit(solution)/shard_map/ppermute | solution.py:15
  122.3 2.5 %collective-permute-start.14 = (bf16[768,512]{1,0:T(8,128)(2,1)}, bf16[768,512]{1,0:T(8,128)(2,1)S(1)}, u32[]{:S(2)}, u32[]{:S(2)}) collective-permute-start(bf16[768,512]{1,0:T(8,128)(2,1)} %get-tuple-element.37), channel_id=1, source_target_pairs={{0,1},{1,0},{2,3},{3,2},{4,5},{5,4},{6,7},{7,6},{8,9},{9,8},{10,11... | collective-permute-start | bytes 2359304 | tf_op jit(solution)/shard_map/ppermute | solution.py:15
  122.5 7.7 %collective-permute-start.12 = (bf16[768,512]{1,0:T(8,128)(2,1)}, bf16[768,512]{1,0:T(8,128)(2,1)S(1)}, u32[]{:S(2)}, u32[]{:S(2)}) collective-permute-start(bf16[768,512]{1,0:T(8,128)(2,1)} %get-tuple-element.33), channel_id=1, source_target_pairs={{0,1},{1,0},{2,3},{3,2},{4,5},{5,4},{6,7},{7,6},{8,9},{9,8},{10,11... | collective-permute-start | bytes 2359304 | tf_op jit(solution)/shard_map/ppermute | solution.py:15
  123.1 7.1 %collective-permute-start.13 = (bf16[768,512]{1,0:T(8,128)(2,1)}, bf16[768,512]{1,0:T(8,128)(2,1)S(1)}, u32[]{:S(2)}, u32[]{:S(2)}) collective-permute-start(bf16[768,512]{1,0:T(8,128)(2,1)} %get-tuple-element.35), channel_id=1, source_target_pairs={{0,1},{1,0},{2,3},{3,2},{4,5},{5,4},{6,7},{7,6},{8,9},{9,8},{10,11... | collective-permute-start | bytes 2359304 | tf_op jit(solution)/shard_map/ppermute | solution.py:15
  125.0 12.3 %collective-permute-start.15 = (bf16[384,512]{1,0:T(8,128)(2,1)S(1)}, bf16[384,512]{1,0:T(8,128)(2,1)S(1)}, u32[]{:S(2)}, u32[]{:S(2)}) collective-permute-start(bf16[384,512]{1,0:T(8,128)(2,1)S(1)} %get-tuple-element.50), channel_id=1, source_target_pairs={{0,2},{1,3},{2,0},{3,1},{4,6},{5,7},{6,4},{7,5},{8,10},{9,11},{10,... | collective-permute-start | bytes 1179656 | tf_op jit(solution)/shard_map/ppermute | solution.py:15
  127.0 14.2 %collective-permute-start.16 = (bf16[384,512]{1,0:T(8,128)(2,1)S(1)}, bf16[384,512]{1,0:T(8,128)(2,1)S(1)}, u32[]{:S(2)}, u32[]{:S(2)}) collective-permute-start(bf16[384,512]{1,0:T(8,128)(2,1)S(1)} %get-tuple-element.49), channel_id=1, source_target_pairs={{0,4},{4,0},{8,12},{12,8},{16,20},{20,16},{24,28},{28,24},{32,36},... | collective-permute-start | bytes 1179656 | tf_op jit(solution)/shard_map/ppermute | solution.py:15
  129.8 31.8 %collective-permute-start.11 = (bf16[768,512]{1,0:T(8,128)(2,1)}, bf16[768,512]{1,0:T(8,128)(2,1)}, u32[]{:S(2)}, u32[]{:S(2)}) collective-permute-start(bf16[768,512]{1,0:T(8,128)(2,1)} %get-tuple-element.31), channel_id=1, source_target_pairs={{0,1},{1,0},{2,3},{3,2},{4,5},{5,4},{6,7},{7,6},{8,9},{9,8},{10,11... | collective-permute-start | bytes 2359304 | tf_op jit(solution)/shard_map/ppermute | solution.py:15
  142.7 18.8 %collective-permute-start.17 = (bf16[768,512]{1,0:T(8,128)(2,1)}, bf16[768,512]{1,0:T(8,128)(2,1)}, u32[]{:S(2)}, u32[]{:S(2)}) collective-permute-start(bf16[768,512]{1,0:T(8,128)(2,1)} %get-tuple-element.38), channel_id=1, source_target_pairs={{0,4},{4,0},{8,12},{12,8},{16,20},{20,16},{24,28},{28,24},{32,36},... | collective-permute-start | bytes 2359304 | tf_op jit(solution)/shard_map/ppermute | solution.py:15
  144.1 20.0 %collective-permute-start.18 = (bf16[768,512]{1,0:T(8,128)(2,1)}, bf16[768,512]{1,0:T(8,128)(2,1)}, u32[]{:S(2)}, u32[]{:S(2)}) collective-permute-start(bf16[768,512]{1,0:T(8,128)(2,1)} %get-tuple-element.39), channel_id=1, source_target_pairs={{0,2},{1,3},{2,0},{3,1},{4,6},{5,7},{6,4},{7,5},{8,10},{9,11},{10,... | collective-permute-start | bytes 2359304 | tf_op jit(solution)/shard_map/ppermute | solution.py:15
  167.1 27.5 %all-to-all-start.2 = ((bf16[32,24,512]{2,1,0:T(8,128)(2,1)}), bf16[32,24,512]{2,1,0:T(8,128)(2,1)}, u32[]{:S(2)}, u32[]{:S(2)}) async-start(bf16[32,24,512]{2,1,0:T(8,128)(2,1)} %bitcast.24), calls=%async_computation.2 | async-start | bytes 1572864 | tf_op jit(solution)/shard_map/all_to_all | solution.py:351
  196.9 16.3 %copy-start.17 = (bf16[128,2048]{1,0:T(8,128)(2,1)S(1)}, bf16[128,2048]{1,0:T(8,128)(2,1)}, u32[]{:S(2)}) copy-start(bf16[128,2048]{1,0:T(8,128)(2,1)} %query_ref.1) | copy-start | bytes 1572868
  199.5 7.1 %collective-permute-start.20 = (bf16[128,1152]{1,0:T(8,128)(2,1)S(1)}, bf16[128,1152]{1,0:T(8,128)(2,1)S(1)}, u32[]{:S(2)}, u32[]{:S(2)}) collective-permute-start(bf16[128,1152]{1,0:T(8,128)(2,1)S(1)} %get-tuple-element.44.own_ref), channel_id=1, source_target_pairs={{0,2},{1,3},{2,0},{3,1},{4,6},{5,7},{6,4},{7,5},{8,10},{9,11},{10,... | collective-permute-start | bytes 884744 | tf_op jit(solution)/shard_map/ppermute | solution.py:15
  202.0 10.0 %collective-permute-start.19 = (bf16[128,1152]{1,0:T(8,128)(2,1)S(1)}, bf16[128,1152]{1,0:T(8,128)(2,1)S(1)}, u32[]{:S(2)}, u32[]{:S(2)}) collective-permute-start(bf16[128,1152]{1,0:T(8,128)(2,1)S(1)} %get-tuple-element.44.own_ref), channel_id=1, source_target_pairs={{0,1},{1,0},{2,3},{3,2},{4,5},{5,4},{6,7},{7,6},{8,9},{9,8},{10,11... | collective-permute-start | bytes 884744 | tf_op jit(solution)/shard_map/ppermute | solution.py:15
  206.6 6.7 %collective-permute-start.21 = (bf16[128,1152]{1,0:T(8,128)(2,1)S(1)}, bf16[128,1152]{1,0:T(8,128)(2,1)S(1)}, u32[]{:S(2)}, u32[]{:S(2)}) collective-permute-start(bf16[128,1152]{1,0:T(8,128)(2,1)S(1)} %collective-permute-done.20.y_ref), channel_id=1, source_target_pairs={{0,1},{1,0},{2,3},{3,2},{4,5},{5,4},{6,7},{7,6},{8,9},{9,8},{10,11... | collective-permute-start | bytes 884744 | tf_op jit(solution)/shard_map/ppermute | solution.py:15
  (24 other events, 71.6 us)

commit v5 on v4

--- a/solution.py
+++ b/solution.py
@@ -86,14 +86,15 @@
 
 def turn(mine_x, theirs_x, mine_y, theirs_y, low_ref, high_ref, *refs):
     x_ref, y_ref = refs[-2:]
-    half = low_ref.shape[0]
-    for mine, theirs, far, part, out in ((mine_x, theirs_x, low_ref, 0, x_ref), (mine_y, theirs_y, high_ref, 1, y_ref)):
-        for i in range(2):
-            span = slice(i * half, (i + 1) * half)
-            total = mine[span].astype(jnp.float32) + theirs[span].astype(jnp.float32)
-            if i == part:
-                total = total + far[...].astype(jnp.float32)
-            out[span] = total.astype(jnp.bfloat16)
+    split = low_ref.shape[0]
+    low, high = slice(0, split), slice(split, x_ref.shape[0])
+    for mine, theirs, far, extra, plain, out in (
+        (mine_x, theirs_x, low_ref, low, high, x_ref),
+        (mine_y, theirs_y, high_ref, high, low, y_ref),
+    ):
+        out[plain] = (mine[plain].astype(jnp.float32) + theirs[plain].astype(jnp.float32)).astype(jnp.bfloat16)
+        total = mine[extra].astype(jnp.float32) + theirs[extra].astype(jnp.float32) + far[...].astype(jnp.float32)
+        out[extra] = total.astype(jnp.bfloat16)
 
 
 def join(mine_ref, theirs_ref, x_ref, y_ref, *refs):
@@ -274,19 +275,15 @@
     requests, max_blocks = block_table.shape
     head_dim = kv_weight.shape[2]
     flat_weight = kv_weight.reshape(model_width, 2 * head_dim)
-    middle = total_slots // 2
     landed = held_until(landed, crossed, order)
     from_y = swapped(landed, "tp", 1)
-    from_x = held_until(swapped(landed, "grp", 0), from_y)
     landed_core = swapped(landed, "tp", 0)
+    ordered = crossed.at[held_until(order, landed_core)[0]].get(mode="promise_in_bounds")
+    from_x = held_until(swapped(landed, "grp", 0), from_y, ordered)
     mine = (landed, from_x, from_y)
     theirs = (landed_core, swapped(from_x, "tp", 0), swapped(from_y, "tp", 0))
     by_y = 2 * total_slots // 3
     last_mine = (swapped(from_x[:by_y], "tp", 1), swapped(from_y[by_y:], "grp", 0))
-
-    order = held_until(order, landed_core)
-    ordered = crossed.at[order[0]].get(mode="promise_in_bounds")
-    arrived = lax.all_to_all(ordered, "grp", split_axis=0, concat_axis=0, tiled=True)
 
     blocks = jnp.stack(
         [
@@ -305,6 +302,8 @@
         name="early_units",
         flops=3 * total_slots * model_width * unit_count,
     )
+    ordered = held_until(ordered, *sums)
+    arrived = lax.all_to_all(ordered, "grp", split_axis=0, concat_axis=0, tiled=True)
     last_mine = tuple(held_until(x, *sums) for x in last_mine)
     last_theirs = tuple(swapped(x, "tp", 0) for x in last_mine)
     sums = call(
@@ -332,7 +331,7 @@
 
     from_core = tuple(swapped(x, "tp", 0) for x in sums[4:])
     both_ways = (sums[3].astype(f32) + from_core[3].astype(f32)).astype(bf16)
-    low, high = swapped(both_ways[:middle], "tp", 1), swapped(both_ways[middle:], "grp", 0)
+    low, high = swapped(both_ways[:by_y], "tp", 1), swapped(both_ways[by_y:], "grp", 0)
     to_x, to_y = call(
         turn,
         (shape((total_slots, eighth), bf16),) * 2,

time: 221 us -> 227 us (1.027)
  waiting for transfers between devices: 83 us -> 91 us
  starting transfers between devices: 67.6 us -> 63.9 us
  local copies, waits for them, and re-layouts: 24.4 us -> 26.9 us
    ppermute x22, waiting for transfers between devices: 65 us -> 73 us  [swapped(): lax.ppermute(x, axis, [(i, i ^ 1 << bit) for i in range(lax.axis_size(axi...]
    ppermute x22, starting transfers between devices: 37.5 us -> 33.9 us  [swapped(): lax.ppermute(x, axis, [(i, i ^ 1 << bit) for i in range(lax.axis_size(axi...]
    unnamed x64 -> x68, local copies, waits for them, and re-layouts: 13 us -> 16 us
  transfers between devices with their start and end apart: 25 -> 25, of which waited for: 12 -> 14; matrix products, arithmetic and copies ran while one was open for 9% -> 8% of each run, Pallas kernels for 11% -> 9%
where the time goes in v5:
time: 227 us; the launch traced here: 226 us
  waiting for transfers between devices  91 us (40%)
  starting transfers between devices  63.9 us (28%)
  Pallas kernels  37 us (16%)
  local copies, waits for them, and re-layouts  26.9 us (12%)
  other arithmetic  6.04 us (3%)
    ppermute x22, waiting for transfers between devices, swapped(): lax.ppermute(x, axis, [(i, i ^ 1 << bit) for i in range(lax.axis_size(axi...  73 us
    pallas_call x8, Pallas kernels, call(): pl.pallas_call(kernel, out_shape=out_shape, in_specs=[pl.BlockSpec(memory...  37 us
    ppermute x22, starting transfers between devices, swapped(): lax.ppermute(x, axis, [(i, i ^ 1 << bit) for i in range(lax.axis_size(axi...  33.9 us
    all_to_all x1, waiting for transfers between devices, local(): lax.all_to_all(summed.reshape(peer_count, capacity, eighth), 'grp', split...  18 us
    unnamed x68, local copies, waits for them, and re-layouts  16 us
    all_to_all x1, starting transfers between devices, local(): lax.all_to_all(packed, 'grp', split_axis=0, concat_axis=0, tiled=True)  11 us
    all_to_all x1, starting transfers between devices, local(): lax.all_to_all(ordered, 'grp', split_axis=0, concat_axis=0, tiled=True)  11 us
    all_to_all x1, starting transfers between devices, local(): lax.all_to_all(summed.reshape(peer_count, capacity, eighth), 'grp', split...  8.01 us
  transfers between devices with their start and end apart: 25, of which 14 were waited for; matrix products, arithmetic and copies ran while one was open for 8% of the time, Pallas kernels for 9%

profile of v5, /device:TPU:1, one launch (start us, length us, event | category | flops | bytes accessed | tf_op | source)
XLA Modules:
  0.0 226.3 jit_solution(12841594515679619193)
XLA Ops:
  0.7 2.2 collective-permute-start
  5.5 1.6 prepare.1
  7.1 11.0 %all-to-all-start = ((bf16[32,24,512]{2,1,0:T(8,128)(2,1)}), bf16[32,24,512]{2,1,0:T(8,128)(2,1)S(1)}, u32[]{:S(2)}, u32[]{:S(2)}) async-start(bf16[32,24,512]{2,1,0:T(8,128)(2,1)} %get-tuple-element.27), calls=%async_computation | async-start | bytes 1572864 | tf_op jit(solution)/shard_map/all_to_all | solution.py:255
  18.4 28.9 %collective-permute-done.1.refs_2_.refs_0_ = s32[1,32]{1,0:T(1,128)S(1)} collective-permute-done((s32[1,32]{1,0:T(1,128)S(1)}, s32[1,32]{1,0:T(1,128)S(1)}, u32[]{:S(2)}, u32[]{:S(2)}) %collective-permute-start.1) | collective-permute-done | bytes 160 | tf_op jit(solution)/shard_map/ppermute | solution.py:15
  48.9 2.4 %collective-permute-start.4 = (bf16[768,512]{1,0:T(8,128)(2,1)}, bf16[768,512]{1,0:T(8,128)(2,1)S(1)}, u32[]{:S(2)}, u32[]{:S(2)}) collective-permute-start(bf16[768,512]{1,0:T(8,128)(2,1)} %held_until.6.refs_0_), channel_id=1, source_target_pairs={{0,1},{1,0},{2,3},{3,2},{4,5},{5,4},{6,7},{7,6},{8,9},{9,8},{10,11... | collective-permute-start | bytes 2359304 | tf_op jit(solution)/shard_map/ppermute | solution.py:15
  52.7 2.9 %collective-permute-start.3 = (bf16[768,512]{1,0:T(8,128)(2,1)}, bf16[768,512]{1,0:T(8,128)(2,1)S(1)}, u32[]{:S(2)}, u32[]{:S(2)}) collective-permute-start(bf16[768,512]{1,0:T(8,128)(2,1)} %held_until.6.refs_0_), channel_id=1, source_target_pairs={{0,2},{1,3},{2,0},{3,1},{4,6},{5,7},{6,4},{7,5},{8,10},{9,11},{10,... | collective-permute-start | bytes 2359304 | tf_op jit(solution)/shard_map/ppermute | solution.py:15
  57.3 3.8 %gather_fusion = bf16[32,2,128,128]{3,2,1,0:T(8,128)(2,1)} fusion(bf16[32,2,128,128]{3,2,1,0:T(8,128)(2,1)} %copy-done.26, s32[1024]{0:T(1024)S(1)} %pad_clamp_fusion), kind=kCustom, calls=%fused_computation | custom fusion | bytes 4194432 | tf_op jit(solution)/shard_map/gather | solution.py:281
  61.0 9.7 %collective-permute-done.2.refs_0_ = bf16[768,512]{1,0:T(8,128)(2,1)S(1)} collective-permute-done((bf16[768,512]{1,0:T(8,128)(2,1)}, bf16[768,512]{1,0:T(8,128)(2,1)S(1)}, u32[]{:S(2)}, u32[]{:S(2)}) %collective-permute-start.2) | collective-permute-done | bytes 786464 | tf_op jit(solution)/shard_map/ppermute | solution.py:15
  70.8 2.6 %collective-permute-done.3.refs_1_.refs_2_ = bf16[768,512]{1,0:T(8,128)(2,1)S(1)} collective-permute-done((bf16[768,512]{1,0:T(8,128)(2,1)}, bf16[768,512]{1,0:T(8,128)(2,1)S(1)}, u32[]{:S(2)}, u32[]{:S(2)}) %collective-permute-start.3) | collective-permute-done | bytes 786464 | tf_op jit(solution)/shard_map/ppermute | solution.py:15
  75.4 3.1 %collective-permute-done.6.refs_4_ = bf16[768,512]{1,0:T(8,128)(2,1)S(1)} collective-permute-done((bf16[768,512]{1,0:T(8,128)(2,1)}, bf16[768,512]{1,0:T(8,128)(2,1)S(1)}, u32[]{:S(2)}, u32[]{:S(2)}) %collective-permute-start.6) | collective-permute-done | bytes 786464 | tf_op jit(solution)/shard_map/ppermute | solution.py:15
  81.0 4.7 %early_units.1 = (f32[768,192]{1,0:T(8,128)S(1)}, f32[768,192]{1,0:T(8,128)S(1)}) custom-call(s32[8]{0:T(128)S(1)} %stack.41.blocks_ref, bf16[768,512]{1,0:T(8,128)(2,1)S(1)} %copy-done.5, bf16[768,512]{1,0:T(8,128)(2,1)S(1)} %copy-done.7, bf16[768,512]{1,0:T(8,128)(2,1)S(1)} %copy-done.10, bf16[768,512]{1,0:T(8,128)(2,1)S(1)} %copy-done.16, ...), custom_call_target="tpu_custom_call" | custom-call | flops 1811939328 | bytes 9044000 | tf_op jit(solution)/shard_map/early_units/pallas_call | solution.py:177
  87.5 11.0 %all-to-all-start.1 = ((bf16[32,2,128,128]{3,2,1,0:T(8,128)(2,1)}), bf16[32,2,128,128]{3,2,1,0:T(8,128)(2,1)}, u32[]{:S(2)}, u32[]{:S(2)}) async-start(bf16[32,2,128,128]{3,2,1,0:T(8,128)(2,1)} %held_until.11.refs_0_), calls=%async_computation.1 | async-start | bytes 4194304 | tf_op jit(solution)/shard_map/all_to_all | solution.py:306
  98.6 3.0 %collective-permute-start.5 = (bf16[512,512]{1,0:T(8,128)(2,1)S(1)}, bf16[512,512]{1,0:T(8,128)(2,1)S(1)}, u32[]{:S(2)}, u32[]{:S(2)}) collective-permute-start(bf16[512,512]{1,0:T(8,128)(2,1)S(1)} %slice.24), channel_id=1, source_target_pairs={{0,2},{1,3},{2,0},{3,1},{4,6},{5,7},{6,4},{7,5},{8,10},{9,11},{10,... | collective-permute-start | bytes 1572872 | tf_op jit(solution)/shard_map/ppermute | solution.py:15
  103.8 9.3 %collective-permute-done.5.refs_0_ = bf16[512,512]{1,0:T(8,128)(2,1)S(1)} collective-permute-done((bf16[512,512]{1,0:T(8,128)(2,1)S(1)}, bf16[512,512]{1,0:T(8,128)(2,1)S(1)}, u32[]{:S(2)}, u32[]{:S(2)}) %collective-permute-start.5) | collective-permute-done | bytes 524320 | tf_op jit(solution)/shard_map/ppermute | solution.py:15
  115.4 4.0 %collective-permute-done.8.refs_0_ = bf16[256,512]{1,0:T(8,128)(2,1)S(1)} collective-permute-done((bf16[256,512]{1,0:T(8,128)(2,1)S(1)}, bf16[256,512]{1,0:T(8,128)(2,1)S(1)}, u32[]{:S(2)}, u32[]{:S(2)}) %collective-permute-start.8) | collective-permute-done | bytes 262176 | tf_op jit(solution)/shard_map/ppermute | solution.py:15
  121.4 2.0 gather_fusion.1
  123.6 6.9 %late_units.1 = (bf16[768,512]{1,0:T(8,128)(2,1)S(1)}, bf16[768,512]{1,0:T(8,128)(2,1)S(1)}, bf16[768,512]{1,0:T(8,128)(2,1)S(1)}, bf16[768,512]{1,0:T(8,128)(2,...) custom-call(s32[8]{0:T(128)S(1)} %stack.41.blocks_ref, ...), custom_call_target="tpu_custom_call" | custom-call | flops 1811939328 | bytes 15859744 | tf_op jit(solution)/shard_map/late_units/pallas_call | solution.py:177
  133.3 1.8 collective-permute-start.15
  135.1 1.6 copy.46
  138.5 8.3 %collective-permute-done.16.high_ref = bf16[256,512]{1,0:T(8,128)(2,1)S(1)} collective-permute-done((bf16[256,512]{1,0:T(8,128)(2,1)S(1)}, bf16[256,512]{1,0:T(8,128)(2,1)S(1)}, u32[]{:S(2)}, u32[]{:S(2)}) %collective-permute-start.16) | collective-permute-done | bytes 262176 | tf_op jit(solution)/shard_map/ppermute | solution.py:15
  146.7 1.6 collective-permute-done.15.low_ref
  149.9 2.2 collective-permute-start.18
  152.5 3.8 %pad_maximum_fusion.pool_ref = bf16[48,2,128,128]{3,2,1,0:T(8,128)(2,1)} fusion(bf16[32,2,128,128]{3,2,1,0:T(8,128)(2,1)} %all-to-all-done.1, bf16[16,2,128,128]{3,2,1,0:T(8,128)(2,1)} %bitcast.51), kind=kLoop, calls=%fused_computation.2 | loop fusion | flops 1572864 | bytes 6291456 | tf_op jit(solution)/shard_map/concatenate | solution.py:322
  156.3 10.2 %cached_attention.1 = (f32[32,64,128]{2,1,0:T(8,128)S(1)}, f32[32,64,128]{2,1,0:T(8,128)S(1)}, f32[32,64,128]{2,1,0:T(8,128)S(1)}) custom-call(s32[128]{0:T(128)S(1)} %reshape.211.table_ref, s32[32]{0:T(128)S(1)} %copy-done.25, bf16[32,64,128]{2,1,0:T(8,128)(2,1)S(1)} %reshape.212.query_ref, bf16[48,2,128,128]{3,2,1,0:T(8,128)(2,1)} %pad_maximum_fusion.pool_ref), custom_call_target="tpu_custom_call" | custom-call | flops 536870912 | bytes 6816384 | tf_op jit(solution)/shard_map/cached_attention/pallas_call | solution.py:177
  169.9 2.9 %join.1 = bf16[768,512]{1,0:T(8,128)(2,1)} custom-call(bf16[768,512]{1,0:T(8,128)(2,1)S(1)} %get-tuple-element.30.mine_ref, bf16[768,512]{1,0:T(8,128)(2,1)} %collective-permute-done.11.theirs_ref, bf16[768,512]{1,0:T(8,128)(2,1)} %collective-permute-done.17.x_ref, bf16[768,512]{1,0:T(8,128)(2,1)} %collective-permute-done.18.y_ref, ...), custom_call_target="tpu_custom_call" | custom-call | bytes 7077888 | tf_op jit(solution)/shard_map/join/pallas_call | solution.py:177
  172.8 8.0 %all-to-all-start.2 = ((bf16[32,24,512]{2,1,0:T(8,128)(2,1)}), bf16[32,24,512]{2,1,0:T(8,128)(2,1)}, u32[]{:S(2)}, u32[]{:S(2)}) async-start(bf16[32,24,512]{2,1,0:T(8,128)(2,1)} %bitcast.24), calls=%async_computation.2 | async-start | bytes 1572864 | tf_op jit(solution)/shard_map/all_to_all | solution.py:350
  182.6 18.0 %all-to-all-done.2 = bf16[32,24,512]{2,1,0:T(8,128)(2,1)} async-done(((bf16[32,24,512]{2,1,0:T(8,128)(2,1)}), bf16[32,24,512]{2,1,0:T(8,128)(2,1)}, u32[]{:S(2)}, u32[]{:S(2)}) %all-to-all-start.2) | async-done | bytes 786464 | tf_op jit(solution)/shard_map/all_to_all | solution.py:350
  202.9 2.6 %finish.1 = (f32[128,1024]{1,0:T(8,128)}, bf16[128,1152]{1,0:T(8,128)(2,1)S(1)}) custom-call(s32[1]{0:T(128)} %bitcast.part_ref, bf16[2,256,768]{2,1,0:T(8,128)(2,1)S(1)} %copy-done.3, bf16[768,512]{1,0:T(8,128)(2,1)} %bitcast.25.returned_ref, bf16[128,4096]{1,0:T(8,128)(2,1)S(1)} %copy-done.14, bf16[1,4096]{1,0:T(2,128)(2,1)S(1)} %reshape.215.gain_ref, ...), custom_call_target="tpu_custom_call" | custom-call | bytes 6594564 | tf_op jit(solution)/shard_map/finish/pallas_call | solution.py:177
  205.5 2.3 %collective-permute-start.20 = (bf16[128,1152]{1,0:T(8,128)(2,1)S(1)}, bf16[128,1152]{1,0:T(8,128)(2,1)S(1)}, u32[]{:S(2)}, u32[]{:S(2)}) collective-permute-start(bf16[128,1152]{1,0:T(8,128)(2,1)S(1)} %get-tuple-element.44.own_ref), channel_id=1, source_target_pairs={{0,2},{1,3},{2,0},{3,1},{4,6},{5,7},{6,4},{7,5},{8,10},{9,11},{10,... | collective-permute-start | bytes 884744 | tf_op jit(solution)/shard_map/ppermute | solution.py:15
  207.8 4.8 %collective-permute-start.19 = (bf16[128,1152]{1,0:T(8,128)(2,1)S(1)}, bf16[128,1152]{1,0:T(8,128)(2,1)S(1)}, u32[]{:S(2)}, u32[]{:S(2)}) collective-permute-start(bf16[128,1152]{1,0:T(8,128)(2,1)S(1)} %get-tuple-element.44.own_ref), channel_id=1, source_target_pairs={{0,1},{1,0},{2,3},{3,2},{4,5},{5,4},{6,7},{7,6},{8,9},{9,8},{10,11... | collective-permute-start | bytes 884744 | tf_op jit(solution)/shard_map/ppermute | solution.py:15
  212.7 5.2 %collective-permute-start.21 = (bf16[128,1152]{1,0:T(8,128)(2,1)S(1)}, bf16[128,1152]{1,0:T(8,128)(2,1)S(1)}, u32[]{:S(2)}, u32[]{:S(2)}) collective-permute-start(bf16[128,1152]{1,0:T(8,128)(2,1)S(1)} %collective-permute-done.20.y_ref), channel_id=1, source_target_pairs={{0,1},{1,0},{2,3},{3,2},{4,5},{5,4},{6,7},{7,6},{8,9},{9,8},{10,11... | collective-permute-start | bytes 884744 | tf_op jit(solution)/shard_map/ppermute | solution.py:15
  219.1 6.6 %last_step.1 = (bf16[128,256]{1,0:T(8,128)(2,1)S(1)}, bf16[128,2048]{1,0:T(8,128)(2,1)}) custom-call(s32[1]{0:T(128)} %bitcast.part_ref, bf16[128,1152]{1,0:T(8,128)(2,1)S(1)} %get-tuple-element.44.own_ref, bf16[128,1152]{1,0:T(8,128)(2,1)S(1)} %collective-permute-done.19.core_ref, bf16[128,1152]{1,0:T(8,128)(2,1)S(1)} %collective-permute-done.20.y_ref, ...), custom_call_target="tpu_custom_call" | custom-call | bytes 7536644 | tf_op jit(solution)/shard_map/last_step/pallas_call | solution.py:177
  (136 shorter events, 36.1 us)
Async XLA Ops:
  0.6 120.3 %copy-start = (bf16[4096,16]{0,1:T(8,128)(2,1)S(1)}, bf16[4096,16]{0,1:T(8,128)(2,1)}, u32[]{:S(2)}) copy-start(bf16[4096,16]{0,1:T(8,128)(2,1)} %param.17) | copy-start | bytes 393220
  0.6 17.5 %copy-start.32 = (s32[1,32]{1,0:T(1,128)S(1)}, s32[1,32]{1,0:T(1,128)}, u32[]{:S(2)}) copy-start(s32[1,32]{1,0:T(1,128)} %param.27) | copy-start | bytes 388
  0.7 46.7 %collective-permute-start = (bf16[32,2,128,128]{3,2,1,0:T(8,128)(2,1)}, bf16[32,2,128,128]{3,2,1,0:T(8,128)(2,1)S(1)}, u32[]{:S(2)}, u32[]{:S(2)}) collective-permute-start(bf16[32,2,128,128]{3,2,1,0:T(8,128)(2,1)} %bitcast.52), channel_id=1, source_target_pairs={{0,128},{128,0},{1,129},{129,1},{2,130},{130,2},{3,131},{131,3},{4... | collective-permute-start | bytes 6291464 | tf_op jit(solution)/shard_map/ppermute | solution.py:15
  7.1 40.2 %all-to-all-start = ((bf16[32,24,512]{2,1,0:T(8,128)(2,1)}), bf16[32,24,512]{2,1,0:T(8,128)(2,1)S(1)}, u32[]{:S(2)}, u32[]{:S(2)}) async-start(bf16[32,24,512]{2,1,0:T(8,128)(2,1)} %get-tuple-element.27), calls=%async_computation | async-start | bytes 1572864 | tf_op jit(solution)/shard_map/all_to_all | solution.py:255
  18.1 29.2 %collective-permute-start.1 = (s32[1,32]{1,0:T(1,128)S(1)}, s32[1,32]{1,0:T(1,128)S(1)}, u32[]{:S(2)}, u32[]{:S(2)}) collective-permute-start(s32[1,32]{1,0:T(1,128)S(1)} %copy-done.32), channel_id=1, source_target_pairs={{0,128},{128,0},{1,129},{129,1},{2,130},{130,2},{3,131},{131,3},{4... | collective-permute-start | bytes 392 | tf_op jit(solution)/shard_map/ppermute | solution.py:15
  48.9 6.7 %collective-permute-start.4 = (bf16[768,512]{1,0:T(8,128)(2,1)}, bf16[768,512]{1,0:T(8,128)(2,1)S(1)}, u32[]{:S(2)}, u32[]{:S(2)}) collective-permute-start(bf16[768,512]{1,0:T(8,128)(2,1)} %held_until.6.refs_0_), channel_id=1, source_target_pairs={{0,1},{1,0},{2,3},{3,2},{4,5},{5,4},{6,7},{7,6},{8,9},{9,8},{10,11... | collective-permute-start | bytes 2359304 | tf_op jit(solution)/shard_map/ppermute | solution.py:15
  51.4 19.4 %collective-permute-start.2 = (bf16[768,512]{1,0:T(8,128)(2,1)}, bf16[768,512]{1,0:T(8,128)(2,1)S(1)}, u32[]{:S(2)}, u32[]{:S(2)}) collective-permute-start(bf16[768,512]{1,0:T(8,128)(2,1)} %held_until.6.refs_0_), channel_id=1, source_target_pairs={{0,4},{4,0},{8,12},{12,8},{16,20},{20,16},{24,28},{28,24},{32,36},... | collective-permute-start | bytes 2359304 | tf_op jit(solution)/shard_map/ppermute | solution.py:15
  52.7 20.6 %collective-permute-start.3 = (bf16[768,512]{1,0:T(8,128)(2,1)}, bf16[768,512]{1,0:T(8,128)(2,1)S(1)}, u32[]{:S(2)}, u32[]{:S(2)}) collective-permute-start(bf16[768,512]{1,0:T(8,128)(2,1)} %held_until.6.refs_0_), channel_id=1, source_target_pairs={{0,2},{1,3},{2,0},{3,1},{4,6},{5,7},{6,4},{7,5},{8,10},{9,11},{10,... | collective-permute-start | bytes 2359304 | tf_op jit(solution)/shard_map/ppermute | solution.py:15
  61.0 17.7 %copy-start.5 = (bf16[768,512]{1,0:T(8,128)(2,1)S(1)}, bf16[768,512]{1,0:T(8,128)(2,1)}, u32[]{:S(2)}) copy-start(bf16[768,512]{1,0:T(8,128)(2,1)} %held_until.6.refs_0_) | copy-start | bytes 2359300
  61.0 17.7 %copy-start.16 = (bf16[768,512]{1,0:T(8,128)(2,1)S(1)}, bf16[768,512]{1,0:T(8,128)(2,1)}, u32[]{:S(2)}) copy-start(bf16[768,512]{1,0:T(8,128)(2,1)} %copy-done.15) | copy-start | bytes 2359300
  74.3 4.3 %collective-permute-start.6 = (bf16[768,512]{1,0:T(8,128)(2,1)}, bf16[768,512]{1,0:T(8,128)(2,1)S(1)}, u32[]{:S(2)}, u32[]{:S(2)}) collective-permute-start(bf16[768,512]{1,0:T(8,128)(2,1)} %held_until.8.refs_1_), channel_id=1, source_target_pairs={{0,1},{1,0},{2,3},{3,2},{4,5},{5,4},{6,7},{7,6},{8,9},{9,8},{10,11... | collective-permute-start | bytes 2359304 | tf_op jit(solution)/shard_map/ppermute | solution.py:15
  75.3 3.4 %collective-permute-start.7 = (bf16[768,512]{1,0:T(8,128)(2,1)}, bf16[768,512]{1,0:T(8,128)(2,1)}, u32[]{:S(2)}, u32[]{:S(2)}) collective-permute-start(bf16[768,512]{1,0:T(8,128)(2,1)} %copy-done.9), channel_id=1, source_target_pairs={{0,1},{1,0},{2,3},{3,2},{4,5},{5,4},{6,7},{7,6},{8,9},{9,8},{10,11... | collective-permute-start | bytes 2359304 | tf_op jit(solution)/shard_map/ppermute | solution.py:15
  87.5 65.0 %all-to-all-start.1 = ((bf16[32,2,128,128]{3,2,1,0:T(8,128)(2,1)}), bf16[32,2,128,128]{3,2,1,0:T(8,128)(2,1)}, u32[]{:S(2)}, u32[]{:S(2)}) async-start(bf16[32,2,128,128]{3,2,1,0:T(8,128)(2,1)} %held_until.11.refs_0_), calls=%async_computation.1 | async-start | bytes 4194304 | tf_op jit(solution)/shard_map/all_to_all | solution.py:306
  98.6 16.8 %copy-start.24 = (s32[128,2]{0,1:T(2,128)S(1)}, s32[128,2]{0,1:T(2,128)}, u32[]{:S(2)}) copy-start(s32[128,2]{0,1:T(2,128)} %param.18) | copy-start | bytes 3076
  98.6 14.5 %collective-permute-start.5 = (bf16[512,512]{1,0:T(8,128)(2,1)S(1)}, bf16[512,512]{1,0:T(8,128)(2,1)S(1)}, u32[]{:S(2)}, u32[]{:S(2)}) collective-permute-start(bf16[512,512]{1,0:T(8,128)(2,1)S(1)} %slice.24), channel_id=1, source_target_pairs={{0,2},{1,3},{2,0},{3,1},{4,6},{5,7},{6,4},{7,5},{8,10},{9,11},{10,... | collective-permute-start | bytes 1572872 | tf_op jit(solution)/shard_map/ppermute | solution.py:15
  102.6 18.1 %copy-start.28 = (bf16[4096]{0:T(1024)(128)(2,1)S(1)}, bf16[4096]{0:T(1024)(128)(2,1)}, u32[]{:S(2)}) copy-start(bf16[4096]{0:T(1024)(128)(2,1)} %param.16) | copy-start | bytes 24580
  102.6 18.3 %copy-start.13 = (bf16[128,4096]{1,0:T(8,128)(2,1)S(1)}, bf16[128,4096]{1,0:T(8,128)(2,1)}, u32[]{:S(2)}) copy-start(bf16[128,4096]{1,0:T(8,128)(2,1)} %hidden_ref.3) | copy-start | bytes 3145732
  102.6 16.8 %collective-permute-start.8 = (bf16[256,512]{1,0:T(8,128)(2,1)S(1)}, bf16[256,512]{1,0:T(8,128)(2,1)S(1)}, u32[]{:S(2)}, u32[]{:S(2)}) collective-permute-start(bf16[256,512]{1,0:T(8,128)(2,1)S(1)} %slice.25), channel_id=1, source_target_pairs={{0,4},{4,0},{8,12},{12,8},{16,20},{20,16},{24,28},{28,24},{32,36},... | collective-permute-start | bytes 786440 | tf_op jit(solution)/shard_map/ppermute | solution.py:15
  113.9 9.6 %collective-permute-start.9 = (bf16[512,512]{1,0:T(8,128)(2,1)}, bf16[512,512]{1,0:T(8,128)(2,1)S(1)}, u32[]{:S(2)}, u32[]{:S(2)}) collective-permute-start(bf16[512,512]{1,0:T(8,128)(2,1)} %held_until.9.mine_low), channel_id=1, source_target_pairs={{0,1},{1,0},{2,3},{3,2},{4,5},{5,4},{6,7},{7,6},{8,9},{9,8},{10,11... | collective-permute-start | bytes 1572872 | tf_op jit(solution)/shard_map/ppermute | solution.py:15
  120.1 3.5 %collective-permute-start.10 = (bf16[256,512]{1,0:T(8,128)(2,1)}, bf16[256,512]{1,0:T(8,128)(2,1)S(1)}, u32[]{:S(2)}, u32[]{:S(2)}) collective-permute-start(bf16[256,512]{1,0:T(8,128)(2,1)} %held_until.10.mine_high), channel_id=1, source_target_pairs={{0,1},{1,0},{2,3},{3,2},{4,5},{5,4},{6,7},{7,6},{8,9},{9,8},{10,11... | collective-permute-start | bytes 786440 | tf_op jit(solution)/shard_map/ppermute | solution.py:15
  130.5 2.5 %collective-permute-start.14 = (bf16[768,512]{1,0:T(8,128)(2,1)}, bf16[768,512]{1,0:T(8,128)(2,1)S(1)}, u32[]{:S(2)}, u32[]{:S(2)}) collective-permute-start(bf16[768,512]{1,0:T(8,128)(2,1)} %get-tuple-element.37), channel_id=1, source_target_pairs={{0,1},{1,0},{2,3},{3,2},{4,5},{5,4},{6,7},{7,6},{8,9},{9,8},{10,11... | collective-permute-start | bytes 2359304 | tf_op jit(solution)/shard_map/ppermute | solution.py:15
  130.9 7.6 %collective-permute-start.12 = (bf16[768,512]{1,0:T(8,128)(2,1)}, bf16[768,512]{1,0:T(8,128)(2,1)S(1)}, u32[]{:S(2)}, u32[]{:S(2)}) collective-permute-start(bf16[768,512]{1,0:T(8,128)(2,1)} %get-tuple-element.33), channel_id=1, source_target_pairs={{0,1},{1,0},{2,3},{3,2},{4,5},{5,4},{6,7},{7,6},{8,9},{9,8},{10,11... | collective-permute-start | bytes 2359304 | tf_op jit(solution)/shard_map/ppermute | solution.py:15
  131.4 7.1 %collective-permute-start.13 = (bf16[768,512]{1,0:T(8,128)(2,1)}, bf16[768,512]{1,0:T(8,128)(2,1)S(1)}, u32[]{:S(2)}, u32[]{:S(2)}) collective-permute-start(bf16[768,512]{1,0:T(8,128)(2,1)} %get-tuple-element.35), channel_id=1, source_target_pairs={{0,1},{1,0},{2,3},{3,2},{4,5},{5,4},{6,7},{7,6},{8,9},{9,8},{10,11... | collective-permute-start | bytes 2359304 | tf_op jit(solution)/shard_map/ppermute | solution.py:15
  133.3 15.1 %collective-permute-start.15 = (bf16[512,512]{1,0:T(8,128)(2,1)S(1)}, bf16[512,512]{1,0:T(8,128)(2,1)S(1)}, u32[]{:S(2)}, u32[]{:S(2)}) collective-permute-start(bf16[512,512]{1,0:T(8,128)(2,1)S(1)} %slice.26), channel_id=1, source_target_pairs={{0,2},{1,3},{2,0},{3,1},{4,6},{5,7},{6,4},{7,5},{8,10},{9,11},{10,... | collective-permute-start | bytes 1572872 | tf_op jit(solution)/shard_map/ppermute | solution.py:15
  136.8 9.9 %collective-permute-start.16 = (bf16[256,512]{1,0:T(8,128)(2,1)S(1)}, bf16[256,512]{1,0:T(8,128)(2,1)S(1)}, u32[]{:S(2)}, u32[]{:S(2)}) collective-permute-start(bf16[256,512]{1,0:T(8,128)(2,1)S(1)} %slice.27), channel_id=1, source_target_pairs={{0,4},{4,0},{8,12},{12,8},{16,20},{20,16},{24,28},{28,24},{32,36},... | collective-permute-start | bytes 786440 | tf_op jit(solution)/shard_map/ppermute | solution.py:15
  138.0 29.5 %collective-permute-start.11 = (bf16[768,512]{1,0:T(8,128)(2,1)}, bf16[768,512]{1,0:T(8,128)(2,1)}, u32[]{:S(2)}, u32[]{:S(2)}) collective-permute-start(bf16[768,512]{1,0:T(8,128)(2,1)} %get-tuple-element.31), channel_id=1, source_target_pairs={{0,1},{1,0},{2,3},{3,2},{4,5},{5,4},{6,7},{7,6},{8,9},{9,8},{10,11... | collective-permute-start | bytes 2359304 | tf_op jit(solution)/shard_map/ppermute | solution.py:15
  149.9 18.5 %collective-permute-start.17 = (bf16[768,512]{1,0:T(8,128)(2,1)}, bf16[768,512]{1,0:T(8,128)(2,1)}, u32[]{:S(2)}, u32[]{:S(2)}) collective-permute-start(bf16[768,512]{1,0:T(8,128)(2,1)} %get-tuple-element.38), channel_id=1, source_target_pairs={{0,4},{4,0},{8,12},{12,8},{16,20},{20,16},{24,28},{28,24},{32,36},... | collective-permute-start | bytes 2359304 | tf_op jit(solution)/shard_map/ppermute | solution.py:15
  149.9 20.0 %collective-permute-start.18 = (bf16[768,512]{1,0:T(8,128)(2,1)}, bf16[768,512]{1,0:T(8,128)(2,1)}, u32[]{:S(2)}, u32[]{:S(2)}) collective-permute-start(bf16[768,512]{1,0:T(8,128)(2,1)} %get-tuple-element.39), channel_id=1, source_target_pairs={{0,2},{1,3},{2,0},{3,1},{4,6},{5,7},{6,4},{7,5},{8,10},{9,11},{10,... | collective-permute-start | bytes 2359304 | tf_op jit(solution)/shard_map/ppermute | solution.py:15
  172.8 27.7 %all-to-all-start.2 = ((bf16[32,24,512]{2,1,0:T(8,128)(2,1)}), bf16[32,24,512]{2,1,0:T(8,128)(2,1)}, u32[]{:S(2)}, u32[]{:S(2)}) async-start(bf16[32,24,512]{2,1,0:T(8,128)(2,1)} %bitcast.24), calls=%async_computation.2 | async-start | bytes 1572864 | tf_op jit(solution)/shard_map/all_to_all | solution.py:350
  205.5 7.2 %collective-permute-start.20 = (bf16[128,1152]{1,0:T(8,128)(2,1)S(1)}, bf16[128,1152]{1,0:T(8,128)(2,1)S(1)}, u32[]{:S(2)}, u32[]{:S(2)}) collective-permute-start(bf16[128,1152]{1,0:T(8,128)(2,1)S(1)} %get-tuple-element.44.own_ref), channel_id=1, source_target_pairs={{0,2},{1,3},{2,0},{3,1},{4,6},{5,7},{6,4},{7,5},{8,10},{9,11},{10,... | collective-permute-start | bytes 884744 | tf_op jit(solution)/shard_map/ppermute | solution.py:15
  207.8 10.0 %collective-permute-start.19 = (bf16[128,1152]{1,0:T(8,128)(2,1)S(1)}, bf16[128,1152]{1,0:T(8,128)(2,1)S(1)}, u32[]{:S(2)}, u32[]{:S(2)}) collective-permute-start(bf16[128,1152]{1,0:T(8,128)(2,1)S(1)} %get-tuple-element.44.own_ref), channel_id=1, source_target_pairs={{0,1},{1,0},{2,3},{3,2},{4,5},{5,4},{6,7},{7,6},{8,9},{9,8},{10,11... | collective-permute-start | bytes 884744 | tf_op jit(solution)/shard_map/ppermute | solution.py:15
  212.7 6.4 %collective-permute-start.21 = (bf16[128,1152]{1,0:T(8,128)(2,1)S(1)}, bf16[128,1152]{1,0:T(8,128)(2,1)S(1)}, u32[]{:S(2)}, u32[]{:S(2)}) collective-permute-start(bf16[128,1152]{1,0:T(8,128)(2,1)S(1)} %collective-permute-done.20.y_ref), channel_id=1, source_target_pairs={{0,1},{1,0},{2,3},{3,2},{4,5},{5,4},{6,7},{7,6},{8,9},{9,8},{10,11... | collective-permute-start | bytes 884744 | tf_op jit(solution)/shard_map/ppermute | solution.py:15
  (26 other events, 74.3 us)

commit v6 on v5

--- a/solution.py
+++ b/solution.py
@@ -70,14 +70,13 @@
         out[...] = total
 
 
-def late_units(blocks_ref, mine_low, mine_high, theirs_low, theirs_high, gate_sum, up_sum, gate_ref, up_ref, down_ref, *refs):
+def late_units(blocks_ref, mine_ref, theirs_ref, gate_sum, up_sum, gate_ref, up_ref, down_ref, *refs):
     outputs = refs[-8:]
-    eighth = mine_low.shape[1]
+    eighth = mine_ref.shape[1]
     gate, up = gate_sum[...], up_sum[...]
-    for i, low, high in ((3, mine_low, mine_high), (7, theirs_low, theirs_high)):
-        piece = jnp.concatenate([low[...], high[...]], axis=0)
-        gate = gate + wide(piece, gate_ref[:, window(blocks_ref, i, eighth)])
-        up = up + wide(piece, up_ref[:, window(blocks_ref, i, eighth)])
+    for i, piece in ((3, mine_ref), (7, theirs_ref)):
+        gate = gate + wide(piece[...], gate_ref[:, window(blocks_ref, i, eighth)])
+        up = up + wide(piece[...], up_ref[:, window(blocks_ref, i, eighth)])
     act = (gate / (1.0 + jnp.exp(-gate)) * up).astype(jnp.bfloat16)
     for i in (3, 7, 2, 6, 1, 5, 0, 4):
         columns = down_ref[:, window(blocks_ref, i, eighth)]
@@ -276,14 +275,16 @@
     head_dim = kv_weight.shape[2]
     flat_weight = kv_weight.reshape(model_width, 2 * head_dim)
     landed = held_until(landed, crossed, order)
+    by_y = 2 * total_slots // 3
     from_y = swapped(landed, "tp", 1)
-    landed_core = swapped(landed, "tp", 0)
-    ordered = crossed.at[held_until(order, landed_core)[0]].get(mode="promise_in_bounds")
-    from_x = held_until(swapped(landed, "grp", 0), from_y, ordered)
+    from_x = held_until(swapped(landed, "grp", 0), from_y)
     mine = (landed, from_x, from_y)
-    theirs = (landed_core, swapped(from_x, "tp", 0), swapped(from_y, "tp", 0))
-    by_y = 2 * total_slots // 3
-    last_mine = (swapped(from_x[:by_y], "tp", 1), swapped(from_y[by_y:], "grp", 0))
+    theirs = tuple(swapped(x, "tp", 0) for x in mine)
+    last_mine = swapped(from_x, "tp", 1)
+    last_theirs = swapped(last_mine, "tp", 0)
+
+    ordered = held_until(crossed.at[order[0]].get(mode="promise_in_bounds"), from_x)
+    arrived = lax.all_to_all(ordered, "grp", split_axis=0, concat_axis=0, tiled=True)
 
     blocks = jnp.stack(
         [
@@ -302,18 +303,29 @@
         name="early_units",
         flops=3 * total_slots * model_width * unit_count,
     )
-    ordered = held_until(ordered, *sums)
-    arrived = lax.all_to_all(ordered, "grp", split_axis=0, concat_axis=0, tiled=True)
-    last_mine = tuple(held_until(x, *sums) for x in last_mine)
-    last_theirs = tuple(swapped(x, "tp", 0) for x in last_mine)
     sums = call(
         late_units,
         (shape((total_slots, eighth), bf16),) * 8,
-        (blocks, *last_mine, *last_theirs, *sums, gate_own, up_own, down_weight[0], ordered),
+        (blocks, last_mine, last_theirs, *sums, gate_own, up_own, down_weight[0], ordered),
         smem=1,
         away=1,
         name="late_units",
         flops=3 * total_slots * model_width * unit_count,
+    )
+
+    requests, max_blocks = block_table.shape
+    head_dim = kv_weight.shape[2]
+    draft_count = token_rows // requests
+    per_kv = queries.shape[1] // head_dim
+    query_rows = queries.reshape(requests, draft_count * per_kv, head_dim)
+    pool = jnp.concatenate([decode_cache[:, 0], arrived], axis=0)
+    stats = call(
+        functools.partial(cached_attention, max_blocks=max_blocks),
+        (shape((requests, draft_count * per_kv, head_dim), f32),) * 3,
+        (block_table.reshape(-1), lengths, query_rows, pool),
+        smem=2,
+        name="cached_attention",
+        flops=4 * requests * draft_count * per_kv * head_dim * max_blocks * decode_cache.shape[3],
     )
 
     draft_count = token_rows // requests

time: 227 us -> 216 us (0.952)
  waiting for transfers between devices: 91 us -> 77.3 us
  starting transfers between devices: 63.9 us -> 67.5 us
    ppermute x22 -> x20, waiting for transfers between devices: 73 us -> 59.4 us  [swapped(): lax.ppermute(x, axis, [(i, i ^ 1 << bit) for i in range(lax.axis_size(axi...]
    unnamed x68 -> x62, local copies, waits for them, and re-layouts: 16 us -> 11.9 us
    ppermute x22 -> x20, starting transfers between devices: 33.9 us -> 35.1 us  [swapped(): lax.ppermute(x, axis, [(i, i ^ 1 << bit) for i in range(lax.axis_size(axi...]
  transfers between devices with their start and end apart: 25 -> 23, of which waited for: 14 -> 10; matrix products, arithmetic and copies ran while one was open for 8% -> 10% of each run, Pallas kernels for 9% -> 12%
where the time goes in v6:
time: 216 us; the launch traced here: 215 us
  waiting for transfers between devices  77.3 us (36%)
  starting transfers between devices  67.5 us (31%)
  Pallas kernels  37.2 us (17%)
  local copies, waits for them, and re-layouts  24.8 us (11%)
  other arithmetic  6.37 us (3%)
    ppermute x20, waiting for transfers between devices, swapped(): lax.ppermute(x, axis, [(i, i ^ 1 << bit) for i in range(lax.axis_size(axi...  59.4 us
    pallas_call x8, Pallas kernels, call(): pl.pallas_call(kernel, out_shape=out_shape, in_specs=[pl.BlockSpec(memory...  37.2 us
    ppermute x20, starting transfers between devices, swapped(): lax.ppermute(x, axis, [(i, i ^ 1 << bit) for i in range(lax.axis_size(axi...  35.1 us
    all_to_all x1, waiting for transfers between devices, local(): lax.all_to_all(summed.reshape(peer_count, capacity, eighth), 'grp', split...  17.8 us
    unnamed x62, local copies, waits for them, and re-layouts  11.9 us
    all_to_all x1, starting transfers between devices, local(): lax.all_to_all(ordered, 'grp', split_axis=0, concat_axis=0, tiled=True)  11.4 us
    all_to_all x1, starting transfers between devices, local(): lax.all_to_all(packed, 'grp', split_axis=0, concat_axis=0, tiled=True)  11 us
    all_to_all x1, starting transfers between devices, local(): lax.all_to_all(summed.reshape(peer_count, capacity, eighth), 'grp', split...  9.95 us
  transfers between devices with their start and end apart: 23, of which 10 were waited for; matrix products, arithmetic and copies ran while one was open for 10% of the time, Pallas kernels for 12%

profile of v6, /device:TPU:1, one launch (start us, length us, event | category | flops | bytes accessed | tf_op | source)
XLA Modules:
  0.0 215.3 jit_solution(466180725841510168)
XLA Ops:
  0.7 2.2 %collective-permute-start = (bf16[32,2,128,128]{3,2,1,0:T(8,128)(2,1)}, bf16[32,2,128,128]{3,2,1,0:T(8,128)(2,1)S(1)}, u32[]{:S(2)}, u32[]{:S(2)}) collective-permute-start(bf16[32,2,128,128]{3,2,1,0:T(8,128)(2,1)} %bitcast.52), channel_id=1, source_target_pairs={{0,128},{128,0},{1,129},{129,1},{2,130},{130,2},{3,131},{131,3},{4... | collective-permute-start | bytes 6291464 | tf_op jit(solution)/shard_map/ppermute | solution.py:15
  5.5 1.6 prepare.1
  7.7 11.0 %all-to-all-start = ((bf16[32,24,512]{2,1,0:T(8,128)(2,1)}), bf16[32,24,512]{2,1,0:T(8,128)(2,1)S(1)}, u32[]{:S(2)}, u32[]{:S(2)}) async-start(bf16[32,24,512]{2,1,0:T(8,128)(2,1)} %get-tuple-element.27), calls=%async_computation | async-start | bytes 1572864 | tf_op jit(solution)/shard_map/all_to_all | solution.py:254
  19.0 28.3 %collective-permute-done.1.refs_2_ = s32[1,32]{1,0:T(1,128)S(1)} collective-permute-done((s32[1,32]{1,0:T(1,128)S(1)}, s32[1,32]{1,0:T(1,128)S(1)}, u32[]{:S(2)}, u32[]{:S(2)}) %collective-permute-start.1) | collective-permute-done | bytes 160 | tf_op jit(solution)/shard_map/ppermute | solution.py:15
  48.9 3.9 %collective-permute-start.3 = (bf16[768,512]{1,0:T(8,128)(2,1)}, bf16[768,512]{1,0:T(8,128)(2,1)S(1)}, u32[]{:S(2)}, u32[]{:S(2)}) collective-permute-start(bf16[768,512]{1,0:T(8,128)(2,1)} %held_until.3.refs_0_), channel_id=1, source_target_pairs={{0,2},{1,3},{2,0},{3,1},{4,6},{5,7},{6,4},{7,5},{8,10},{9,11},{10,... | collective-permute-start | bytes 2359304 | tf_op jit(solution)/shard_map/ppermute | solution.py:15
  54.7 14.4 %collective-permute-done.3.refs_1_.refs_2_ = bf16[768,512]{1,0:T(8,128)(2,1)S(1)} collective-permute-done((bf16[768,512]{1,0:T(8,128)(2,1)}, bf16[768,512]{1,0:T(8,128)(2,1)S(1)}, u32[]{:S(2)}, u32[]{:S(2)}) %collective-permute-start.3) | collective-permute-done | bytes 786464 | tf_op jit(solution)/shard_map/ppermute | solution.py:15
  71.1 2.7 %collective-permute-start.4 = (bf16[768,512]{1,0:T(8,128)(2,1)}, bf16[768,512]{1,0:T(8,128)(2,1)}, u32[]{:S(2)}, u32[]{:S(2)}) collective-permute-start(bf16[768,512]{1,0:T(8,128)(2,1)} %held_until.4.refs_1_), channel_id=1, source_target_pairs={{0,2},{1,3},{2,0},{3,1},{4,6},{5,7},{6,4},{7,5},{8,10},{9,11},{10,... | collective-permute-start | bytes 2359304 | tf_op jit(solution)/shard_map/ppermute | solution.py:15
  73.7 3.8 %gather_fusion = bf16[32,2,128,128]{3,2,1,0:T(8,128)(2,1)} fusion(bf16[32,2,128,128]{3,2,1,0:T(8,128)(2,1)} %copy-done.22, s32[1024]{0:T(1024)S(1)} %pad_clamp_fusion), kind=kCustom, calls=%fused_computation | custom fusion | bytes 4194432 | tf_op jit(solution)/shard_map/gather | solution.py:286
  77.6 11.4 %all-to-all-start.1 = ((bf16[32,2,128,128]{3,2,1,0:T(8,128)(2,1)}), bf16[32,2,128,128]{3,2,1,0:T(8,128)(2,1)}, u32[]{:S(2)}, u32[]{:S(2)}) async-start(bf16[32,2,128,128]{3,2,1,0:T(8,128)(2,1)} %held_until.5.refs_0_), calls=%async_computation.1 | async-start | bytes 4194304 | tf_op jit(solution)/shard_map/all_to_all | solution.py:287
  89.0 3.2 %collective-permute-start.6 = (bf16[768,512]{1,0:T(8,128)(2,1)S(1)}, bf16[768,512]{1,0:T(8,128)(2,1)}, u32[]{:S(2)}, u32[]{:S(2)}) collective-permute-start(bf16[768,512]{1,0:T(8,128)(2,1)S(1)} %copy-done.5), channel_id=1, source_target_pairs={{0,1},{1,0},{2,3},{3,2},{4,5},{5,4},{6,7},{7,6},{8,9},{9,8},{10,11... | collective-permute-start | bytes 2359304 | tf_op jit(solution)/shard_map/ppermute | solution.py:15
  94.4 1.5 reshape.228
  98.0 2.1 gather_fusion.1
  100.5 5.2 %early_units.1 = (f32[768,192]{1,0:T(8,128)S(1)}, f32[768,192]{1,0:T(8,128)S(1)}) custom-call(s32[8]{0:T(128)S(1)} %stack.41.blocks_ref, bf16[768,512]{1,0:T(8,128)(2,1)S(1)} %copy-done.5, bf16[768,512]{1,0:T(8,128)(2,1)S(1)} %copy-done.3, bf16[768,512]{1,0:T(8,128)(2,1)S(1)} %copy-done.11, bf16[768,512]{1,0:T(8,128)(2,1)} %collective-permute-done.6.refs_3_, ...), custom_call_target="tpu_custom_call" | custom-call | flops 1811939328 | bytes 9044000 | tf_op jit(solution)/shard_map/early_units/pallas_call | solution.py:176
  107.5 6.9 %late_units.1 = (bf16[768,512]{1,0:T(8,128)(2,1)S(1)}, bf16[768,512]{1,0:T(8,128)(2,1)S(1)}, bf16[768,512]{1,0:T(8,128)(2,1)S(1)}, bf16[768,512]{1,0:T(8,128)(2,...) custom-call(s32[8]{0:T(128)S(1)} %stack.41.blocks_ref, ...), custom_call_target="tpu_custom_call" | custom-call | flops 1811939328 | bytes 15859744 | tf_op jit(solution)/shard_map/late_units/pallas_call | solution.py:176
  115.5 1.4 collective-permute-done.12
  117.2 2.6 %collective-permute-start.13 = (bf16[512,512]{1,0:T(8,128)(2,1)S(1)}, bf16[512,512]{1,0:T(8,128)(2,1)S(1)}, u32[]{:S(2)}, u32[]{:S(2)}) collective-permute-start(bf16[512,512]{1,0:T(8,128)(2,1)S(1)} %slice.16), channel_id=1, source_target_pairs={{0,2},{1,3},{2,0},{3,1},{4,6},{5,7},{6,4},{7,5},{8,10},{9,11},{10,... | collective-permute-start | bytes 1572872 | tf_op jit(solution)/shard_map/ppermute | solution.py:15
  119.9 1.6 copy.43
  124.6 8.0 %collective-permute-done.14.high_ref = bf16[256,512]{1,0:T(8,128)(2,1)S(1)} collective-permute-done((bf16[256,512]{1,0:T(8,128)(2,1)S(1)}, bf16[256,512]{1,0:T(8,128)(2,1)S(1)}, u32[]{:S(2)}, u32[]{:S(2)}) %collective-permute-start.14) | collective-permute-done | bytes 262176 | tf_op jit(solution)/shard_map/ppermute | solution.py:15
  133.8 3.3 %collective-permute-start.15 = (bf16[768,512]{1,0:T(8,128)(2,1)}, bf16[768,512]{1,0:T(8,128)(2,1)}, u32[]{:S(2)}, u32[]{:S(2)}) collective-permute-start(bf16[768,512]{1,0:T(8,128)(2,1)} %get-tuple-element.38), channel_id=1, source_target_pairs={{0,4},{4,0},{8,12},{12,8},{16,20},{20,16},{24,28},{28,24},{32,36},... | collective-permute-start | bytes 2359304 | tf_op jit(solution)/shard_map/ppermute | solution.py:15
  138.5 3.5 %pad_maximum_fusion.pool_ref = bf16[48,2,128,128]{3,2,1,0:T(8,128)(2,1)} fusion(bf16[32,2,128,128]{3,2,1,0:T(8,128)(2,1)} %all-to-all-done.1, bf16[16,2,128,128]{3,2,1,0:T(8,128)(2,1)S(1)} %bitcast.51), kind=kLoop, calls=%fused_computation.2 | loop fusion | flops 1572864 | bytes 6291456 | tf_op jit(solution)/shard_map/concatenate | solution.py:334
  142.0 10.3 %cached_attention.1 = (f32[32,64,128]{2,1,0:T(8,128)S(1)}, f32[32,64,128]{2,1,0:T(8,128)S(1)}, f32[32,64,128]{2,1,0:T(8,128)S(1)}) custom-call(s32[128]{0:T(128)S(1)} %reshape.211.table_ref, s32[32]{0:T(128)S(1)} %copy-done.21, bf16[32,64,128]{2,1,0:T(8,128)(2,1)S(1)} %reshape.212.query_ref, bf16[48,2,128,128]{3,2,1,0:T(8,128)(2,1)} %pad_maximum_fusion.pool_ref), custom_call_target="tpu_custom_call" | custom-call | flops 536870912 | bytes 6816384 | tf_op jit(solution)/shard_map/cached_attention/pallas_call | solution.py:176
  153.3 1.3 collective-permute-done.15.x_ref
  154.6 2.1 collective-permute-done.16.y_ref
  156.7 2.9 %join.1 = bf16[768,512]{1,0:T(8,128)(2,1)} custom-call(bf16[768,512]{1,0:T(8,128)(2,1)S(1)} %copy-done.15, bf16[768,512]{1,0:T(8,128)(2,1)} %collective-permute-done.9.theirs_ref, bf16[768,512]{1,0:T(8,128)(2,1)} %collective-permute-done.15.x_ref, bf16[768,512]{1,0:T(8,128)(2,1)} %collective-permute-done.16.y_ref, ...), custom_call_target="tpu_custom_call" | custom-call | bytes 7077888 | tf_op jit(solution)/shard_map/join/pallas_call | solution.py:176
  159.6 9.9 %all-to-all-start.2 = ((bf16[32,24,512]{2,1,0:T(8,128)(2,1)}), bf16[32,24,512]{2,1,0:T(8,128)(2,1)}, u32[]{:S(2)}, u32[]{:S(2)}) async-start(bf16[32,24,512]{2,1,0:T(8,128)(2,1)} %bitcast.24), calls=%async_computation.2 | async-start | bytes 1572864 | tf_op jit(solution)/shard_map/all_to_all | solution.py:362
  170.0 1.4 reshape.218.refs_2_.mixed_ref
  171.4 17.8 %all-to-all-done.2 = bf16[32,24,512]{2,1,0:T(8,128)(2,1)} async-done(((bf16[32,24,512]{2,1,0:T(8,128)(2,1)}), bf16[32,24,512]{2,1,0:T(8,128)(2,1)}, u32[]{:S(2)}, u32[]{:S(2)}) %all-to-all-start.2) | async-done | bytes 786464 | tf_op jit(solution)/shard_map/all_to_all | solution.py:362
  191.5 2.6 %finish.1 = (f32[128,1024]{1,0:T(8,128)}, bf16[128,1152]{1,0:T(8,128)(2,1)S(1)}) custom-call(s32[1]{0:T(128)} %bitcast.part_ref, bf16[2,256,768]{2,1,0:T(8,128)(2,1)S(1)} %copy-done.1, bf16[768,512]{1,0:T(8,128)(2,1)} %bitcast.25.returned_ref, bf16[128,4096]{1,0:T(8,128)(2,1)S(1)} %copy-done.9, bf16[1,4096]{1,0:T(2,128)(2,1)S(1)} %reshape.215.gain_ref, ...), custom_call_target="tpu_custom_call" | custom-call | bytes 6594564 | tf_op jit(solution)/shard_map/finish/pallas_call | solution.py:176
  194.8 4.9 %collective-permute-start.17 = (bf16[128,1152]{1,0:T(8,128)(2,1)S(1)}, bf16[128,1152]{1,0:T(8,128)(2,1)S(1)}, u32[]{:S(2)}, u32[]{:S(2)}) collective-permute-start(bf16[128,1152]{1,0:T(8,128)(2,1)S(1)} %get-tuple-element.44.own_ref), channel_id=1, source_target_pairs={{0,1},{1,0},{2,3},{3,2},{4,5},{5,4},{6,7},{7,6},{8,9},{9,8},{10,11... | collective-permute-start | bytes 884744 | tf_op jit(solution)/shard_map/ppermute | solution.py:15
  199.7 1.5 collective-permute-done.18.y_ref
  201.2 5.7 %collective-permute-start.19 = (bf16[128,1152]{1,0:T(8,128)(2,1)S(1)}, bf16[128,1152]{1,0:T(8,128)(2,1)S(1)}, u32[]{:S(2)}, u32[]{:S(2)}) collective-permute-start(bf16[128,1152]{1,0:T(8,128)(2,1)S(1)} %collective-permute-done.18.y_ref), channel_id=1, source_target_pairs={{0,1},{1,0},{2,3},{3,2},{4,5},{5,4},{6,7},{7,6},{8,9},{9,8},{10,11... | collective-permute-start | bytes 884744 | tf_op jit(solution)/shard_map/ppermute | solution.py:15
  208.1 6.6 %last_step.1 = (bf16[128,256]{1,0:T(8,128)(2,1)S(1)}, bf16[128,2048]{1,0:T(8,128)(2,1)}) custom-call(s32[1]{0:T(128)} %bitcast.part_ref, bf16[128,1152]{1,0:T(8,128)(2,1)S(1)} %get-tuple-element.44.own_ref, bf16[128,1152]{1,0:T(8,128)(2,1)S(1)} %collective-permute-done.17.core_ref, bf16[128,1152]{1,0:T(8,128)(2,1)S(1)} %collective-permute-done.18.y_ref, ...), custom_call_target="tpu_custom_call" | custom-call | bytes 7536644 | tf_op jit(solution)/shard_map/last_step/pallas_call | solution.py:176
  (121 shorter events, 28.6 us)
Async XLA Ops:
  0.6 96.2 %copy-start = (bf16[4096,16]{0,1:T(8,128)(2,1)S(1)}, bf16[4096,16]{0,1:T(8,128)(2,1)}, u32[]{:S(2)}) copy-start(bf16[4096,16]{0,1:T(8,128)(2,1)} %param.17) | copy-start | bytes 393220
  0.6 18.1 %copy-start.29 = (s32[1,32]{1,0:T(1,128)S(1)}, s32[1,32]{1,0:T(1,128)}, u32[]{:S(2)}) copy-start(s32[1,32]{1,0:T(1,128)} %param.27) | copy-start | bytes 388
  0.7 46.7 %collective-permute-start = (bf16[32,2,128,128]{3,2,1,0:T(8,128)(2,1)}, bf16[32,2,128,128]{3,2,1,0:T(8,128)(2,1)S(1)}, u32[]{:S(2)}, u32[]{:S(2)}) collective-permute-start(bf16[32,2,128,128]{3,2,1,0:T(8,128)(2,1)} %bitcast.52), channel_id=1, source_target_pairs={{0,128},{128,0},{1,129},{129,1},{2,130},{130,2},{3,131},{131,3},{4... | collective-permute-start | bytes 6291464 | tf_op jit(solution)/shard_map/ppermute | solution.py:15
  7.7 39.6 %all-to-all-start = ((bf16[32,24,512]{2,1,0:T(8,128)(2,1)}), bf16[32,24,512]{2,1,0:T(8,128)(2,1)S(1)}, u32[]{:S(2)}, u32[]{:S(2)}) async-start(bf16[32,24,512]{2,1,0:T(8,128)(2,1)} %get-tuple-element.27), calls=%async_computation | async-start | bytes 1572864 | tf_op jit(solution)/shard_map/all_to_all | solution.py:254
  18.7 28.6 %collective-permute-start.1 = (s32[1,32]{1,0:T(1,128)S(1)}, s32[1,32]{1,0:T(1,128)S(1)}, u32[]{:S(2)}, u32[]{:S(2)}) collective-permute-start(s32[1,32]{1,0:T(1,128)S(1)} %copy-done.29), channel_id=1, source_target_pairs={{0,128},{128,0},{1,129},{129,1},{2,130},{130,2},{3,131},{131,3},{4... | collective-permute-start | bytes 392 | tf_op jit(solution)/shard_map/ppermute | solution.py:15
  48.9 20.2 %collective-permute-start.3 = (bf16[768,512]{1,0:T(8,128)(2,1)}, bf16[768,512]{1,0:T(8,128)(2,1)S(1)}, u32[]{:S(2)}, u32[]{:S(2)}) collective-permute-start(bf16[768,512]{1,0:T(8,128)(2,1)} %held_until.3.refs_0_), channel_id=1, source_target_pairs={{0,2},{1,3},{2,0},{3,1},{4,6},{5,7},{6,4},{7,5},{8,10},{9,11},{10,... | collective-permute-start | bytes 2359304 | tf_op jit(solution)/shard_map/ppermute | solution.py:15
  52.8 17.4 %collective-permute-start.2 = (bf16[768,512]{1,0:T(8,128)(2,1)}, bf16[768,512]{1,0:T(8,128)(2,1)S(1)}, u32[]{:S(2)}, u32[]{:S(2)}) collective-permute-start(bf16[768,512]{1,0:T(8,128)(2,1)} %held_until.3.refs_0_), channel_id=1, source_target_pairs={{0,4},{4,0},{8,12},{12,8},{16,20},{20,16},{24,28},{28,24},{32,36},... | collective-permute-start | bytes 2359304 | tf_op jit(solution)/shard_map/ppermute | solution.py:15
  71.1 21.6 %collective-permute-start.4 = (bf16[768,512]{1,0:T(8,128)(2,1)}, bf16[768,512]{1,0:T(8,128)(2,1)}, u32[]{:S(2)}, u32[]{:S(2)}) collective-permute-start(bf16[768,512]{1,0:T(8,128)(2,1)} %held_until.4.refs_1_), channel_id=1, source_target_pairs={{0,2},{1,3},{2,0},{3,1},{4,6},{5,7},{6,4},{7,5},{8,10},{9,11},{10,... | collective-permute-start | bytes 2359304 | tf_op jit(solution)/shard_map/ppermute | solution.py:15
  77.5 14.7 %copy-start.3 = (bf16[768,512]{1,0:T(8,128)(2,1)S(1)}, bf16[768,512]{1,0:T(8,128)(2,1)}, u32[]{:S(2)}) copy-start(bf16[768,512]{1,0:T(8,128)(2,1)} %held_until.4.refs_1_) | copy-start | bytes 2359300
  77.5 14.8 %copy-start.11 = (bf16[768,512]{1,0:T(8,128)(2,1)S(1)}, bf16[768,512]{1,0:T(8,128)(2,1)}, u32[]{:S(2)}) copy-start(bf16[768,512]{1,0:T(8,128)(2,1)} %copy-done.10) | copy-start | bytes 2359300
  77.5 15.5 %copy-start.25 = (bf16[4096]{0:T(1024)(128)(2,1)S(1)}, bf16[4096]{0:T(1024)(128)(2,1)}, u32[]{:S(2)}) copy-start(bf16[4096]{0:T(1024)(128)(2,1)} %param.16) | copy-start | bytes 24580
  77.5 16.1 %copy-start.20 = (s32[128,2]{0,1:T(2,128)S(1)}, s32[128,2]{0,1:T(2,128)}, u32[]{:S(2)}) copy-start(s32[128,2]{0,1:T(2,128)} %param.18) | copy-start | bytes 3076
  77.6 19.3 %copy-start.8 = (bf16[128,4096]{1,0:T(8,128)(2,1)S(1)}, bf16[128,4096]{1,0:T(8,128)(2,1)}, u32[]{:S(2)}) copy-start(bf16[128,4096]{1,0:T(8,128)(2,1)} %hidden_ref.3) | copy-start | bytes 3145732
  77.6 60.9 %all-to-all-start.1 = ((bf16[32,2,128,128]{3,2,1,0:T(8,128)(2,1)}), bf16[32,2,128,128]{3,2,1,0:T(8,128)(2,1)}, u32[]{:S(2)}, u32[]{:S(2)}) async-start(bf16[32,2,128,128]{3,2,1,0:T(8,128)(2,1)} %held_until.5.refs_0_), calls=%async_computation.1 | async-start | bytes 4194304 | tf_op jit(solution)/shard_map/all_to_all | solution.py:287
  89.0 11.4 %collective-permute-start.6 = (bf16[768,512]{1,0:T(8,128)(2,1)S(1)}, bf16[768,512]{1,0:T(8,128)(2,1)}, u32[]{:S(2)}, u32[]{:S(2)}) collective-permute-start(bf16[768,512]{1,0:T(8,128)(2,1)S(1)} %copy-done.5), channel_id=1, source_target_pairs={{0,1},{1,0},{2,3},{3,2},{4,5},{5,4},{6,7},{7,6},{8,9},{9,8},{10,11... | collective-permute-start | bytes 2359304 | tf_op jit(solution)/shard_map/ppermute | solution.py:15
  92.2 8.3 %collective-permute-start.7 = (bf16[768,512]{1,0:T(8,128)(2,1)S(1)}, bf16[768,512]{1,0:T(8,128)(2,1)}, u32[]{:S(2)}, u32[]{:S(2)}) collective-permute-start(bf16[768,512]{1,0:T(8,128)(2,1)S(1)} %copy-done.3), channel_id=1, source_target_pairs={{0,1},{1,0},{2,3},{3,2},{4,5},{5,4},{6,7},{7,6},{8,9},{9,8},{10,11... | collective-permute-start | bytes 2359304 | tf_op jit(solution)/shard_map/ppermute | solution.py:15
  92.3 8.2 %collective-permute-start.8 = (bf16[768,512]{1,0:T(8,128)(2,1)S(1)}, bf16[768,512]{1,0:T(8,128)(2,1)}, u32[]{:S(2)}, u32[]{:S(2)}) collective-permute-start(bf16[768,512]{1,0:T(8,128)(2,1)S(1)} %copy-done.11), channel_id=1, source_target_pairs={{0,1},{1,0},{2,3},{3,2},{4,5},{5,4},{6,7},{7,6},{8,9},{9,8},{10,11... | collective-permute-start | bytes 2359304 | tf_op jit(solution)/shard_map/ppermute | solution.py:15
  92.7 14.8 %collective-permute-start.5 = (bf16[768,512]{1,0:T(8,128)(2,1)}, bf16[768,512]{1,0:T(8,128)(2,1)}, u32[]{:S(2)}, u32[]{:S(2)}) collective-permute-start(bf16[768,512]{1,0:T(8,128)(2,1)} %collective-permute-done.4.mine_ref), channel_id=1, source_target_pairs={{0,1},{1,0},{2,3},{3,2},{4,5},{5,4},{6,7},{7,6},{8,9},{9,8},{10,11... | collective-permute-start | bytes 2359304 | tf_op jit(solution)/shard_map/ppermute | solution.py:15
  114.5 2.5 %collective-permute-start.12 = (bf16[768,512]{1,0:T(8,128)(2,1)}, bf16[768,512]{1,0:T(8,128)(2,1)S(1)}, u32[]{:S(2)}, u32[]{:S(2)}) collective-permute-start(bf16[768,512]{1,0:T(8,128)(2,1)} %get-tuple-element.37), channel_id=1, source_target_pairs={{0,1},{1,0},{2,3},{3,2},{4,5},{5,4},{6,7},{7,6},{8,9},{9,8},{10,11... | collective-permute-start | bytes 2359304 | tf_op jit(solution)/shard_map/ppermute | solution.py:15
  114.9 9.7 %collective-permute-start.10 = (bf16[768,512]{1,0:T(8,128)(2,1)S(1)}, bf16[768,512]{1,0:T(8,128)(2,1)S(1)}, u32[]{:S(2)}, u32[]{:S(2)}) collective-permute-start(bf16[768,512]{1,0:T(8,128)(2,1)S(1)} %get-tuple-element.33), channel_id=1, source_target_pairs={{0,1},{1,0},{2,3},{3,2},{4,5},{5,4},{6,7},{7,6},{8,9},{9,8},{10,11... | collective-permute-start | bytes 2359304 | tf_op jit(solution)/shard_map/ppermute | solution.py:15
  115.3 9.3 %collective-permute-start.11 = (bf16[768,512]{1,0:T(8,128)(2,1)S(1)}, bf16[768,512]{1,0:T(8,128)(2,1)S(1)}, u32[]{:S(2)}, u32[]{:S(2)}) collective-permute-start(bf16[768,512]{1,0:T(8,128)(2,1)S(1)} %get-tuple-element.35), channel_id=1, source_target_pairs={{0,1},{1,0},{2,3},{3,2},{4,5},{5,4},{6,7},{7,6},{8,9},{9,8},{10,11... | collective-permute-start | bytes 2359304 | tf_op jit(solution)/shard_map/ppermute | solution.py:15
  117.2 15.4 %collective-permute-start.13 = (bf16[512,512]{1,0:T(8,128)(2,1)S(1)}, bf16[512,512]{1,0:T(8,128)(2,1)S(1)}, u32[]{:S(2)}, u32[]{:S(2)}) collective-permute-start(bf16[512,512]{1,0:T(8,128)(2,1)S(1)} %slice.16), channel_id=1, source_target_pairs={{0,2},{1,3},{2,0},{3,1},{4,6},{5,7},{6,4},{7,5},{8,10},{9,11},{10,... | collective-permute-start | bytes 1572872 | tf_op jit(solution)/shard_map/ppermute | solution.py:15
  121.5 11.1 %collective-permute-start.14 = (bf16[256,512]{1,0:T(8,128)(2,1)S(1)}, bf16[256,512]{1,0:T(8,128)(2,1)S(1)}, u32[]{:S(2)}, u32[]{:S(2)}) collective-permute-start(bf16[256,512]{1,0:T(8,128)(2,1)S(1)} %slice.17), channel_id=1, source_target_pairs={{0,4},{4,0},{8,12},{12,8},{16,20},{20,16},{24,28},{28,24},{32,36},... | collective-permute-start | bytes 786440 | tf_op jit(solution)/shard_map/ppermute | solution.py:15
  123.9 29.3 %collective-permute-start.9 = (bf16[768,512]{1,0:T(8,128)(2,1)}, bf16[768,512]{1,0:T(8,128)(2,1)}, u32[]{:S(2)}, u32[]{:S(2)}) collective-permute-start(bf16[768,512]{1,0:T(8,128)(2,1)} %get-tuple-element.31), channel_id=1, source_target_pairs={{0,1},{1,0},{2,3},{3,2},{4,5},{5,4},{6,7},{7,6},{8,9},{9,8},{10,11... | collective-permute-start | bytes 2359304 | tf_op jit(solution)/shard_map/ppermute | solution.py:15
  133.8 20.8 %collective-permute-start.15 = (bf16[768,512]{1,0:T(8,128)(2,1)}, bf16[768,512]{1,0:T(8,128)(2,1)}, u32[]{:S(2)}, u32[]{:S(2)}) collective-permute-start(bf16[768,512]{1,0:T(8,128)(2,1)} %get-tuple-element.38), channel_id=1, source_target_pairs={{0,4},{4,0},{8,12},{12,8},{16,20},{20,16},{24,28},{28,24},{32,36},... | collective-permute-start | bytes 2359304 | tf_op jit(solution)/shard_map/ppermute | solution.py:15
  137.1 19.6 %collective-permute-start.16 = (bf16[768,512]{1,0:T(8,128)(2,1)S(1)}, bf16[768,512]{1,0:T(8,128)(2,1)}, u32[]{:S(2)}, u32[]{:S(2)}) collective-permute-start(bf16[768,512]{1,0:T(8,128)(2,1)S(1)} %get-tuple-element.39), channel_id=1, source_target_pairs={{0,2},{1,3},{2,0},{3,1},{4,6},{5,7},{6,4},{7,5},{8,10},{9,11},{10,... | collective-permute-start | bytes 2359304 | tf_op jit(solution)/shard_map/ppermute | solution.py:15
  142.0 14.7 %copy-start.15 = (bf16[768,512]{1,0:T(8,128)(2,1)S(1)}, bf16[768,512]{1,0:T(8,128)(2,1)}, u32[]{:S(2)}) copy-start(bf16[768,512]{1,0:T(8,128)(2,1)} %copy-done.14) | copy-start | bytes 2359300
  159.6 29.5 %all-to-all-start.2 = ((bf16[32,24,512]{2,1,0:T(8,128)(2,1)}), bf16[32,24,512]{2,1,0:T(8,128)(2,1)}, u32[]{:S(2)}, u32[]{:S(2)}) async-start(bf16[32,24,512]{2,1,0:T(8,128)(2,1)} %bitcast.24), calls=%async_computation.2 | async-start | bytes 1572864 | tf_op jit(solution)/shard_map/all_to_all | solution.py:362
  191.5 16.6 %copy-start.13 = (bf16[128,2048]{1,0:T(8,128)(2,1)S(1)}, bf16[128,2048]{1,0:T(8,128)(2,1)}, u32[]{:S(2)}) copy-start(bf16[128,2048]{1,0:T(8,128)(2,1)} %query_ref.1) | copy-start | bytes 1572868
  194.1 7.1 %collective-permute-start.18 = (bf16[128,1152]{1,0:T(8,128)(2,1)S(1)}, bf16[128,1152]{1,0:T(8,128)(2,1)S(1)}, u32[]{:S(2)}, u32[]{:S(2)}) collective-permute-start(bf16[128,1152]{1,0:T(8,128)(2,1)S(1)} %get-tuple-element.44.own_ref), channel_id=1, source_target_pairs={{0,2},{1,3},{2,0},{3,1},{4,6},{5,7},{6,4},{7,5},{8,10},{9,11},{10,... | collective-permute-start | bytes 884744 | tf_op jit(solution)/shard_map/ppermute | solution.py:15
  194.8 12.0 %collective-permute-start.17 = (bf16[128,1152]{1,0:T(8,128)(2,1)S(1)}, bf16[128,1152]{1,0:T(8,128)(2,1)S(1)}, u32[]{:S(2)}, u32[]{:S(2)}) collective-permute-start(bf16[128,1152]{1,0:T(8,128)(2,1)S(1)} %get-tuple-element.44.own_ref), channel_id=1, source_target_pairs={{0,1},{1,0},{2,3},{3,2},{4,5},{5,4},{6,7},{7,6},{8,9},{9,8},{10,11... | collective-permute-start | bytes 884744 | tf_op jit(solution)/shard_map/ppermute | solution.py:15
  201.2 6.9 %collective-permute-start.19 = (bf16[128,1152]{1,0:T(8,128)(2,1)S(1)}, bf16[128,1152]{1,0:T(8,128)(2,1)S(1)}, u32[]{:S(2)}, u32[]{:S(2)}) collective-permute-start(bf16[128,1152]{1,0:T(8,128)(2,1)S(1)} %collective-permute-done.18.y_ref), channel_id=1, source_target_pairs={{0,1},{1,0},{2,3},{3,2},{4,5},{5,4},{6,7},{7,6},{8,9},{9,8},{10,11... | collective-permute-start | bytes 884744 | tf_op jit(solution)/shard_map/ppermute | solution.py:15
  (21 other events, 65.6 us)
